TPU v7x, 32 devices: a whole 2x2x4 slice. The times are simulated.
32 devices in a mesh: dp: 16 (over z, y, core), tensor: 2 (over x).
Axes of the slice: x: 2, y: 2, z: 4, core: 2. Of those that a mesh axis runs over, the one named last changes fastest.
Arguments:
- tokens: bfloat16 [16384, 1024], P('dp'), may hold values from -6 to 6
- lengths: int32 [16, 23], P('dp'), may hold values from 0 to 197, as said below
- norm1_gain: float32 [1024], replicated, may hold values from 0.5 to 1.5
- norm1_bias: float32 [1024], replicated, may hold values from -1.5 to 1.5
- qkv_weight: bfloat16 [3, 1024, 1024], P(None, None, 'tensor'), may hold values from -0.1875 to 0.1875
- qv_bias: float32 [2, 16, 64], P(None, 'tensor'), may hold values from -2.5 to 2.5
- proj_weight: bfloat16 [1024, 1024], P('tensor'), may hold values from -0.75 to 0.75
- proj_bias: float32 [1024], replicated, may hold values from -2.5 to 2.5
- scale_attn: float32 [1024], replicated, may hold values from 0.5 to 2
- norm2_gain: float32 [1024], replicated, may hold values from 0.5 to 1.5
- norm2_bias: float32 [1024], replicated, may hold values from -1.5 to 1.5
- fc1_weight: bfloat16 [1024, 4096], P(None, 'tensor'), may hold values from -0.1875 to 0.1875
- fc1_bias: float32 [4096], P('tensor'), may hold values from -2.5 to 2.5
- fc2_weight: bfloat16 [4096, 1024], P('tensor'), may hold values from -0.125 to 0.125
- fc2_bias: float32 [1024], replicated, may hold values from -2.5 to 2.5
- scale_mlp: float32 [1024], replicated, may hold values from 0.5 to 2
- cotangent: bfloat16 [16384, 1024], P('dp'), may hold values from -6 to 6
Outputs:
- output: bfloat16 [16384, 1024], P('dp')
- grad_tokens: bfloat16 [16384, 1024], P('dp')
- norm1_gain_grad: float32 [1024], P(('dp', 'tensor'))
- norm1_bias_grad: float32 [1024], P(('dp', 'tensor'))
- qkv_weight_grad: float32 [3, 1024, 1024], P(None, 'dp', 'tensor')
- qv_bias_grad: float32 [2, 16, 64], P(None, 'tensor', 'dp')
- proj_weight_grad: float32 [1024, 1024], P('tensor', 'dp')
- proj_bias_grad: float32 [1024], P(('dp', 'tensor'))
- scale_attn_grad: float32 [1024], P(('dp', 'tensor'))
- norm2_gain_grad: float32 [1024], P(('dp', 'tensor'))
- norm2_bias_grad: float32 [1024], P(('dp', 'tensor'))
- fc1_weight_grad: float32 [1024, 4096], P('dp', 'tensor')
- fc1_bias_grad: float32 [64, 64], P('tensor', 'dp')
- fc2_weight_grad: float32 [4096, 1024], P('tensor', 'dp')
- fc2_bias_grad: float32 [1024], P(('dp', 'tensor'))
- scale_mlp_grad: float32 [1024], P(('dp', 'tensor'))
Inputs may be any that keep to these rules, and one draw needn't show every extreme that they name: Each packed row's lengths are one or more 197, then zero or more 37, then zeros; a row's lengths add up to at most 1024.
All inputs are finite; a program needn't handle non-finite values.
Results may differ from a plain program's by a relative error of at most 0.02.
Values may be sent and summed in bfloat16 or wider, within the bound.
No kernel may reach another device: no remote copies, remote signals or barrier semaphores. Data moves between devices by JAX's collectives and lax.ppermute only.
A program may use at most 256 MiB of HBM per device.

v0:
```python
from functools import partial

import jax
import jax.numpy as jnp
from jax import lax
from jax.sharding import PartitionSpec as P

EPS = 1e-06
NEGATIVE = -1e30


def segment_row(lengths_row, row_width):
    finish = jnp.cumsum(lengths_row)
    places = jnp.arange(row_width, dtype=jnp.int32)
    labels = jnp.sum((finish[None, :] <= places[:, None]).astype(jnp.int32), axis=1)
    return jnp.where(places < finish[-1], labels, -1)


def norm_parts(values):
    average = jnp.mean(values, axis=-1, keepdims=True)
    centered = values - average
    inverse = lax.rsqrt(jnp.mean(centered * centered, axis=-1, keepdims=True) + EPS)
    return (centered * inverse, inverse)


def norm_back(grad_norm, scaled, inverse, gain):
    grad_hat = grad_norm * gain
    first_mean = jnp.mean(grad_hat, axis=-1, keepdims=True)
    second_mean = jnp.mean(grad_hat * scaled, axis=-1, keepdims=True)
    return inverse * (grad_hat - first_mean - scaled * second_mean)


def masked_scores(query_part, key_rows, label_part, labels):
    score_scale = query_part.shape[-1] ** (-0.5)
    scores = (
        jnp.einsum("qhc,khc->hqk", query_part, key_rows, preferred_element_type=jnp.float32)
        * score_scale
    )
    allowed = (label_part[:, None] == labels[None, :]) & (labels[None, :] >= 0)
    return jnp.where(allowed[None], scores, NEGATIVE)


def attend_forward(queries, key_rows, values, labels, block_rows):
    block_count = queries.shape[0] // block_rows

    def one_block(block_index):
        first_row = block_index * block_rows
        query_part = lax.dynamic_slice_in_dim(queries, first_row, block_rows, 0)
        label_part = lax.dynamic_slice_in_dim(labels, first_row, block_rows, 0)
        scores = masked_scores(query_part, key_rows, label_part, labels)
        row_top = jnp.max(scores, axis=-1, keepdims=True)
        weights = jnp.exp(scores - row_top)
        row_total = jnp.sum(weights, axis=-1, keepdims=True)
        probability_low = (weights / row_total).astype(jnp.bfloat16)
        mixed = jnp.einsum(
            "hqk,khc->qhc", probability_low, values, preferred_element_type=jnp.float32
        )
        return (mixed.astype(jnp.bfloat16), row_top, row_total)

    mixed, row_top, row_total = lax.map(one_block, jnp.arange(block_count, dtype=jnp.int32))
    return (mixed.reshape(queries.shape), row_top, row_total)


def attend_backward(queries, key_rows, values, labels, grad_mixed, row_top, row_total, block_rows):
    block_count = queries.shape[0] // block_rows
    score_scale = queries.shape[-1] ** (-0.5)

    def one_block(carry_sums, block_index):
        grad_keys, grad_values = carry_sums
        first_row = block_index * block_rows
        query_part = lax.dynamic_slice_in_dim(queries, first_row, block_rows, 0)
        label_part = lax.dynamic_slice_in_dim(labels, first_row, block_rows, 0)
        grad_part = lax.dynamic_slice_in_dim(grad_mixed, first_row, block_rows, 0)
        scores = masked_scores(query_part, key_rows, label_part, labels)
        probability = jnp.exp(scores - row_top[block_index]) / row_total[block_index]
        grad_probability = jnp.einsum(
            "qhc,khc->hqk", grad_part, values, preferred_element_type=jnp.float32
        )
        row_delta = jnp.sum(probability * grad_probability, axis=-1, keepdims=True)
        grad_scores = (probability * (grad_probability - row_delta)).astype(jnp.bfloat16)
        grad_query = (
            jnp.einsum("hqk,khc->qhc", grad_scores, key_rows, preferred_element_type=jnp.float32)
            * score_scale
        )
        grad_keys = (
            grad_keys
            + jnp.einsum(
                "hqk,qhc->khc", grad_scores, query_part, preferred_element_type=jnp.float32
            )
            * score_scale
        )
        grad_values = grad_values + jnp.einsum(
            "hqk,qhc->khc",
            probability.astype(jnp.bfloat16),
            grad_part,
            preferred_element_type=jnp.float32,
        )
        return ((grad_keys, grad_values), grad_query)

    zeros = jnp.zeros(key_rows.shape, jnp.float32)
    (grad_keys, grad_values), grad_query = lax.scan(
        one_block, (zeros, zeros), jnp.arange(block_count, dtype=jnp.int32)
    )
    return (grad_query.reshape(queries.shape), grad_keys, grad_values)


def body(
    tokens,
    lengths,
    norm1_gain,
    norm1_bias,
    qkv_weight,
    qv_bias,
    proj_weight,
    proj_bias,
    scale_attn,
    norm2_gain,
    norm2_bias,
    fc1_weight,
    fc1_bias,
    fc2_weight,
    fc2_bias,
    scale_mlp,
    cotangent,
):
    row_count = lengths.shape[0]
    token_count, model_width = tokens.shape
    pack_rows = token_count // row_count
    block_rows = min(512, pack_rows)
    local_width = qkv_weight.shape[2]
    local_heads = qv_bias.shape[1]
    head_size = qv_bias.shape[2]
    share_rows = token_count // lax.axis_size("tensor")
    share_start = lax.axis_index("tensor") * share_rows

    def own_rows(array):
        return lax.dynamic_slice_in_dim(array, share_start, share_rows, 0)

    def shaped(array):
        return array.reshape(row_count, pack_rows, local_heads, head_size)

    labels = jax.vmap(lambda lengths_row: segment_row(lengths_row, pack_rows))(lengths)
    valid = (labels.reshape(-1) >= 0).astype(jnp.float32)[:, None]
    inputs = tokens.astype(jnp.float32)
    scaled1, inverse1 = norm_parts(inputs)
    normed1 = (scaled1 * norm1_gain + norm1_bias).astype(jnp.bfloat16)
    projected = jnp.einsum("td,sdc->stc", normed1, qkv_weight, preferred_element_type=jnp.float32)
    queries = (projected[0] + qv_bias[0].reshape(-1)).astype(jnp.bfloat16)
    key_rows = projected[1].astype(jnp.bfloat16)
    values = (projected[2] + qv_bias[1].reshape(-1)).astype(jnp.bfloat16)

    def forward_row(row_items):
        return attend_forward(row_items[0], row_items[1], row_items[2], row_items[3], block_rows)

    mixed, row_top, row_total = lax.map(
        forward_row, (shaped(queries), shaped(key_rows), shaped(values), labels)
    )
    mixed = mixed.reshape(token_count, local_width)
    attn_terms = jnp.dot(mixed, proj_weight, preferred_element_type=jnp.float32)
    attn_out = lax.psum(attn_terms.astype(jnp.bfloat16), "tensor").astype(jnp.float32) + proj_bias
    middle = inputs + scale_attn * attn_out
    scaled2, inverse2 = norm_parts(middle)
    normed2 = (scaled2 * norm2_gain + norm2_bias).astype(jnp.bfloat16)
    hidden = jnp.dot(normed2, fc1_weight, preferred_element_type=jnp.float32) + fc1_bias
    activated, gelu_back = jax.vjp(partial(jax.nn.gelu, approximate=False), hidden)
    activated_low = activated.astype(jnp.bfloat16)
    mlp_terms = jnp.dot(activated_low, fc2_weight, preferred_element_type=jnp.float32)
    mlp_out = lax.psum(mlp_terms.astype(jnp.bfloat16), "tensor").astype(jnp.float32) + fc2_bias
    output = ((middle + scale_mlp * mlp_out) * valid).astype(jnp.bfloat16)
    grad_result = cotangent.astype(jnp.float32) * valid
    grad_mlp_low = (scale_mlp * grad_result).astype(jnp.bfloat16)
    grad_fc2 = jnp.einsum(
        "tf,td->fd", activated_low, grad_mlp_low, preferred_element_type=jnp.float32
    )
    grad_act = jnp.einsum("td,fd->tf", grad_mlp_low, fc2_weight, preferred_element_type=jnp.float32)
    grad_hidden = gelu_back(grad_act)[0]
    grad_hidden_low = grad_hidden.astype(jnp.bfloat16)
    grad_fc1 = jnp.einsum("td,tf->df", normed2, grad_hidden_low, preferred_element_type=jnp.float32)
    grad_fc1_bias = jnp.sum(grad_hidden, axis=0).reshape(-1, head_size)
    norm2_terms = jnp.einsum(
        "tf,df->td", grad_hidden_low, fc1_weight, preferred_element_type=jnp.float32
    )
    grad_norm2 = lax.psum(norm2_terms.astype(jnp.bfloat16), "tensor").astype(jnp.float32)
    grad_middle = grad_result + norm_back(grad_norm2, scaled2, inverse2, norm2_gain)
    norm2_share = own_rows(grad_norm2)
    middle_share = own_rows(grad_middle)
    grad_attn_low = (scale_attn * grad_middle).astype(jnp.bfloat16)
    grad_proj = jnp.einsum("tc,td->cd", mixed, grad_attn_low, preferred_element_type=jnp.float32)
    grad_mixed = jnp.einsum(
        "td,cd->tc", grad_attn_low, proj_weight, preferred_element_type=jnp.float32
    ).astype(jnp.bfloat16)

    def backward_row(row_items):
        return attend_backward(
            row_items[0],
            row_items[1],
            row_items[2],
            row_items[3],
            row_items[4],
            row_items[5],
            row_items[6],
            block_rows,
        )

    grad_query, grad_keys, grad_values = lax.map(
        backward_row,
        (
            shaped(queries),
            shaped(key_rows),
            shaped(values),
            labels,
            shaped(grad_mixed),
            row_top,
            row_total,
        ),
    )
    grad_query = grad_query.reshape(token_count, local_width)
    grad_keys = grad_keys.reshape(token_count, local_width)
    grad_values = grad_values.reshape(token_count, local_width)
    grad_bias = jnp.stack([jnp.sum(grad_query, axis=0), jnp.sum(grad_values, axis=0)]).reshape(
        2, local_heads, head_size
    )
    grad_stack = jnp.stack([grad_query, grad_keys, grad_values]).astype(jnp.bfloat16)
    grad_qkv = jnp.einsum("td,stc->sdc", normed1, grad_stack, preferred_element_type=jnp.float32)
    norm1_terms = jnp.einsum(
        "stc,sdc->td", grad_stack, qkv_weight, preferred_element_type=jnp.float32
    )
    grad_norm1 = lax.psum(norm1_terms.astype(jnp.bfloat16), "tensor").astype(jnp.float32)
    grad_input = grad_middle + norm_back(grad_norm1, scaled1, inverse1, norm1_gain)
    norm1_share = own_rows(grad_norm1)
    grad_tokens = grad_input.astype(jnp.bfloat16)
    result_share = own_rows(grad_result)
    vectors = jnp.stack(
        [
            jnp.sum(norm1_share * own_rows(scaled1), axis=0),
            jnp.sum(norm1_share, axis=0),
            jnp.sum(middle_share * own_rows(attn_out), axis=0),
            jnp.sum(scale_attn * middle_share, axis=0),
            jnp.sum(norm2_share * own_rows(scaled2), axis=0),
            jnp.sum(norm2_share, axis=0),
            jnp.sum(result_share * own_rows(mlp_out), axis=0),
            jnp.sum(scale_mlp * result_share, axis=0),
        ]
    )
    sent_qkv, sent_bias, sent_proj, sent_fc1, sent_fc1_bias, sent_fc2 = (
        lax.psum_scatter(
            grad_qkv.astype(jnp.bfloat16), "dp", scatter_dimension=1, tiled=True
        ).astype(jnp.float32),
        lax.psum_scatter(
            grad_bias.astype(jnp.bfloat16), "dp", scatter_dimension=2, tiled=True
        ).astype(jnp.float32),
        lax.psum_scatter(
            grad_proj.astype(jnp.bfloat16), "dp", scatter_dimension=1, tiled=True
        ).astype(jnp.float32),
        lax.psum_scatter(
            grad_fc1.astype(jnp.bfloat16), "dp", scatter_dimension=0, tiled=True
        ).astype(jnp.float32),
        lax.psum_scatter(
            grad_fc1_bias.astype(jnp.bfloat16), "dp", scatter_dimension=1, tiled=True
        ).astype(jnp.float32),
        lax.psum_scatter(
            grad_fc2.astype(jnp.bfloat16), "dp", scatter_dimension=1, tiled=True
        ).astype(jnp.float32),
    )
    sent_vectors = lax.psum_scatter(vectors, ("dp", "tensor"), scatter_dimension=1, tiled=True)
    return (
        output,
        grad_tokens,
        sent_vectors[0],
        sent_vectors[1],
        sent_qkv,
        sent_bias,
        sent_proj,
        sent_vectors[3],
        sent_vectors[2],
        sent_vectors[4],
        sent_vectors[5],
        sent_fc1,
        sent_fc1_bias,
        sent_fc2,
        sent_vectors[7],
        sent_vectors[6],
    )


def solution(mesh):
    in_specs = (
        P("dp", None),
        P("dp", None),
        P(),
        P(),
        P(None, None, "tensor"),
        P(None, "tensor", None),
        P("tensor", None),
        P(),
        P(),
        P(),
        P(),
        P(None, "tensor"),
        P("tensor"),
        P("tensor", None),
        P(),
        P(),
        P("dp", None),
    )
    out_specs = (
        P("dp", None),
        P("dp", None),
        P(("dp", "tensor")),
        P(("dp", "tensor")),
        P(None, "dp", "tensor"),
        P(None, "tensor", "dp"),
        P("tensor", "dp"),
        P(("dp", "tensor")),
        P(("dp", "tensor")),
        P(("dp", "tensor")),
        P(("dp", "tensor")),
        P("dp", "tensor"),
        P("tensor", "dp"),
        P("tensor", "dp"),
        P(("dp", "tensor")),
        P(("dp", "tensor")),
    )
    return jax.shard_map(body, mesh=mesh, in_specs=in_specs, out_specs=out_specs, check_vma=False)
```

profile of v0, /device:TPU:0, one launch (start us, length us, event | category | flops | bytes accessed | tf_op | source)
XLA Modules:
  0.0 978.1 jit_solution(5486811224867312413)
XLA Ops:
  7.3 2.1 convert_reduce_fusion
  9.4 2.3 fusion.34
  11.8 3.9 convolution_bitcast_fusion
  16.8 2.3 fusion.55
  21.4 3.8 add_convert_fusion.3
  25.2 34.7 %while.51 = (s32[]{:T(128)}, bf16[2,512,8,64]{1,3,2,0:T(8,128)(2,1)}, f32[2,8,512,1]{2,1,3,0:T(8,128)S(1)}, f32[2,8,512,1]{2,1,3,0:T(8,128)S(1)}, s32[2]{0:T(128...) while((s32[]{:T(128)}, ...), condition=%wide.region_7.8_spmd, body=%wide.region_4.7_spmd.sunk | while | flops 1125377024 | bytes 68321568 | solution.py:60
  27.2 4.9 fusion.99
  32.0 4.2 fusion.100
  36.3 5.4 fusion.101
  44.4 4.9 fusion.99
  49.3 4.2 fusion.100
  53.6 5.4 fusion.101
  59.9 2.4 copy.60
  63.5 2.6 convolution_convert_fusion.3
  66.2 65.7 %all-reduce.10.cloned.1.call-done = bf16[1024,1024]{1,0:T(8,128)(2,1)} async-done(((bf16[1024,1024]{1,0:T(8,128)(2,1)}), bf16[1024,1024]{1,0:T(8,128)(2,1)}) %all-reduce.10.cloned.1.call-update) | async-done | bytes 2097168 | tf_op jit(solution)/shard_map/psum | solution.py:160
  132.0 3.3 fusion.42
  138.9 25.4 %multiply_convert_fusion.1 = (bf16[1024,2048]{1,0:T(8,128)(2,1)}, f32[1024,2048]{1,0:T(8,128)}, f32[1024,2048]{1,0:T(8,128)}) fusion(f32[2048]{0:T(1024)S(1)} %copy-done.53, bf16[1024,2048]{1,0:T(8,128)(2,1)S(1)} %copy-done.49, f32[1024,1024]{1,0:T(8,128)S(1)} %subtract_multiply_fusion, f32[1024]{0:T(1024)S(1)} %copy-done.56, f32[1024]{0:T(1024)S(1)} %copy-done.44), kind=kOutput, calls=%fused_computation.44 | convolution fusion | flops 4436525056 | bytes 29376512 | tf_op jit(solution)/shard_map/dot_general | solution.py:164
  164.3 13.0 %fusion.59 = (bf16[2048]{0:T(1024)(128)(2,1)}, bf16[1024,2048]{1,0:T(8,128)(2,1)}) fusion(f32[1024,2048]{1,0:T(8,128)} %get-tuple-element.354, bf16[2048,1024]{1,0:T(8,128)(2,1)S(1)} %copy-done.50, f32[1024]{0:T(1024)S(1)} %copy-done.42, f32[1024]{0:T(1024)S(1)} %copy-done.38, bf16[1024,1024]{1,0:T(8,128)(2,1)S(1)} %copy-done.26, ...), kind=kOutput, calls=%fused_computation.136 | convolution fusion | flops 4332713984 | bytes 27283456 | tf_op jit(solution)/shard_map/td,fd->tf/dot_general | solution.py:175
  177.4 8.0 fusion.39
  185.5 9.3 convolution_convert_fusion.2
  194.7 53.7 %all-reduce.12.cloned.1.call-done = bf16[1024,1024]{1,0:T(8,128)(2,1)} async-done(((bf16[1024,1024]{1,0:T(8,128)(2,1)}), bf16[1024,1024]{1,0:T(8,128)(2,1)}) %all-reduce.12.cloned.1.call-update) | async-done | bytes 2097168 | tf_op jit(solution)/shard_map/psum | solution.py:183
  248.5 3.8 multiply_reduce_fusion.5
  253.2 4.2 convert_multiply_fusion
  257.4 2.4 convolution_convert_fusion.5
  259.8 107.9 %while.52 = (s32[]{:T(128)}, f32[1024,8,64]{0,2,1:T(8,128)}, f32[1024,8,64]{0,2,1:T(8,128)}, f32[2,512,8,64]{1,3,2,0:T(8,128)}, s32[2]{0:T(128)S(1)}, /*index=5*...) while((s32[]{:T(128)}, f32[1024,8,64]{0,2,1:T(8,128)}, ...), condition=%wide.region_17.18_spmd.clone, body=%wide.region_15.17_spmd.clone.sunk | while | flops 2730226688 | bytes 204620336 | solution.py:101
  263.5 9.6 fusion.111
  273.1 14.9 %multiply_reduce_fusion.13 = (f32[8,512]{1,0:T(8,128)S(1)}, f32[8,512,1024]{2,1,0:T(8,128)}) fusion(f32[8,512,1024]{2,1,0:T(8,128)} %fusion.111, f32[8,512]{1,0:T(8,128)S(1)} %get-tuple-element.535, f32[8,512]{1,0:T(8,128)S(1)} %get-tuple-element.536, bf16[1024,8,64]{0,2,1:T(8,128)(2,1)S(1)} %copy-done.4, bf16[1024,8,64]{0,2,1:T(8,128)(2,1)S(1)} %copy-done.14, ...), kind=kOutput, calls=%fused_computation.19.clone.1 | convolution fusion | flops 562032640 | bytes 35700740 | tf_op jit(solution)/shard_map/while/body/eval_jaxpr/while/body/eval_jaxpr/qhc,khc->hqk/dot_general | solution.py:36
  288.0 11.5 %multiply_convert_fusion.12 = bf16[8,512,1024]{2,1,0:T(8,128)(2,1)S(1)} fusion(f32[8,512,1024]{2,1,0:T(8,128)} %get-tuple-element.537, f32[8,512,1024]{2,1,0:T(8,128)} %fusion.111, f32[8,512]{1,0:T(8,128)S(1)} %get-tuple-element.538), kind=kLoop, calls=%fused_computation.18.clone.1 | loop fusion | flops 12582912 | bytes 41959424 | tf_op jit(solution)/shard_map/while/body/eval_jaxpr/while/body/eval_jaxpr/convert_element_type | solution.py:80
  299.6 7.8 bitcast_add_fusion.5
  307.4 1.8 bitcast_add_fusion.4
  309.8 2.7 fusion.112
  312.4 1.3 copy-done.25
  317.5 9.6 fusion.111
  327.1 14.9 %multiply_reduce_fusion.13 = (f32[8,512]{1,0:T(8,128)S(1)}, f32[8,512,1024]{2,1,0:T(8,128)}) fusion(f32[8,512,1024]{2,1,0:T(8,128)} %fusion.111, f32[8,512]{1,0:T(8,128)S(1)} %get-tuple-element.535, f32[8,512]{1,0:T(8,128)S(1)} %get-tuple-element.536, bf16[1024,8,64]{0,2,1:T(8,128)(2,1)S(1)} %copy-done.4, bf16[1024,8,64]{0,2,1:T(8,128)(2,1)S(1)} %copy-done.14, ...), kind=kOutput, calls=%fused_computation.19.clone.1 | convolution fusion | flops 562032640 | bytes 35700740 | tf_op jit(solution)/shard_map/while/body/eval_jaxpr/while/body/eval_jaxpr/qhc,khc->hqk/dot_general | solution.py:36
  342.0 11.5 %multiply_convert_fusion.12 = bf16[8,512,1024]{2,1,0:T(8,128)(2,1)S(1)} fusion(f32[8,512,1024]{2,1,0:T(8,128)} %get-tuple-element.537, f32[8,512,1024]{2,1,0:T(8,128)} %fusion.111, f32[8,512]{1,0:T(8,128)S(1)} %get-tuple-element.538), kind=kLoop, calls=%fused_computation.18.clone.1 | loop fusion | flops 12582912 | bytes 41959424 | tf_op jit(solution)/shard_map/while/body/eval_jaxpr/while/body/eval_jaxpr/convert_element_type | solution.py:80
  353.5 7.8 bitcast_add_fusion.5
  361.4 1.8 bitcast_add_fusion.4
  363.7 2.7 fusion.112
  367.7 3.6 fusion.56
  372.4 2.5 copy.63
  374.9 3.5 fusion.57
  378.3 2.3 copy.64
  380.6 3.5 copy.72
  384.1 4.0 reshape.311
  388.1 6.5 bitcast_convert_fusion
  395.3 8.1 convert_bitcast_fusion
  403.4 7.7 copy.66
  411.2 4.8 convolution_convert_fusion.4
  416.3 10.0 %convolution_convert_fusion.1 = bf16[1024,2048]{1,0:T(8,128)(2,1)} fusion(bf16[1024,2048]{1,0:T(8,128)(2,1)} %get-tuple-element.390, f32[1024,1024]{1,0:T(8,128)} %copy-done.11, f32[1024]{0:T(1024)S(1)} %copy-done.57, f32[1024]{0:T(1024)S(1)} %copy-done.45), kind=kOutput, calls=%fused_computation.80 | convolution fusion | flops 4300210176 | bytes 12591104 | tf_op jit(solution)/shard_map/td,tf->df/dot_general | solution.py:178
  427.1 9.5 convolution_convert_fusion
  439.3 61.7 %all-reduce.3 = (bf16[2,8,64]{1,2,0:T(8,128)(2,1)S(1)}, bf16[32,64]{1,0:T(8,128)(2,1)S(1)}) all-reduce(bf16[2,8,64]{1,2,0:T(8,128)(2,1)S(1)} %copy.67, bf16[32,64]{1,0:T(8,128)(2,1)S(1)} %convert_element_type.177), channel_id=4, replica_groups=mesh['dp'=16,'tensor'=2] {'dp'}, use_global_device_ids=true, to_apply=%region_33.34.clone | all-reduce | flops 3072 | bytes 12288
  501.7 2.2 convert_element_type.162
  505.6 2.2 convert_element_type.166
  508.4 1.8 multiply_reduce_fusion.4
  512.6 4.5 convert_add_fusion.1
  517.5 1.9 copy-done.22
  520.9 97.6 %all-reduce.14.cloned.1.call-done = bf16[3,1024,512]{2,0,1:T(4,128)(2,1)} async-done(((bf16[3,1024,512]{2,0,1:T(4,128)(2,1)}), bf16[3,1024,512]{2,0,1:T(4,128)(2,1)}) %all-reduce.14.cloned.1.call-update) | async-done | bytes 3145744
  620.4 58.0 %reduce-scatter.9.cloned.1.call-done = bf16[512,64]{0,1:T(8,128)(2,1)} async-done(((bf16[512,1024]{0,1:T(8,128)(2,1)}), bf16[512,64]{0,1:T(8,128)(2,1)}) %reduce-scatter.9.cloned.1.call-update) | async-done | bytes 65552 | tf_op jit(solution)/shard_map/reduce_scatter | solution.py:252
  678.4 1.5 convert_element_type.173
  679.9 74.1 %reduce-scatter.11.cloned.1.call-done = bf16[64,2048]{1,0:T(8,128)(2,1)} async-done(((bf16[1024,2048]{1,0:T(8,128)(2,1)}), bf16[64,2048]{1,0:T(8,128)(2,1)}) %reduce-scatter.11.cloned.1.call-update) | async-done | bytes 262160 | tf_op jit(solution)/shard_map/reduce_scatter | solution.py:255
  754.0 1.8 convert_element_type.175
  755.7 73.8 %reduce-scatter.13.cloned.1.call-done = bf16[2048,64]{0,1:T(8,128)(2,1)} async-done(((bf16[2048,1024]{0,1:T(8,128)(2,1)}), bf16[2048,64]{0,1:T(8,128)(2,1)}) %reduce-scatter.13.cloned.1.call-update) | async-done | bytes 262160 | tf_op jit(solution)/shard_map/reduce_scatter | solution.py:261
  829.5 1.8 convert_element_type.180
  831.3 133.7 %reduce-scatter.15.cloned.1.call-done = f32[32,8]{1,0:T(8,128)} async-done(((f32[1024,8]{1,0:T(8,128)}), f32[32,8]{1,0:T(8,128)}) %reduce-scatter.15.cloned.1.call-update) | async-done | bytes 1040
  (229 shorter events, 37.1 us)
Async XLA Ops:
  7.2 4.5 copy-start
  7.2 4.5 copy-start.40
  7.2 4.5 copy-start.54
  7.2 124.7 %all-reduce.10.cloned.1.call-start = ((), (), s32[]{:S(2)}) async-start(), calls=%async_computation.4 | async-start | bytes 4194304 | tf_op jit(solution)/shard_map/psum | solution.py:160
  7.3 4.5 copy-start.5
  9.4 6.3 copy-start.32
  11.8 3.9 copy-start.36
  16.8 2.3 copy-start.58
  16.8 3.3 copy-start.46
  32.0 4.3 copy-start.8
  32.0 4.3 copy-start.28
  49.3 4.3 copy-start.8
  49.3 4.3 copy-start.28
  59.9 3.6 copy-start.51
  63.5 68.4 %copy-start.30 = (f32[1024]{0:T(1024)S(1)}, f32[1024]{0:T(1024)}, u32[]{:S(2)}) copy-start(f32[1024]{0:T(1024)} %param.29) | copy-start | bytes 12292
  63.5 68.4 %copy-start.34 = (f32[1024]{0:T(1024)S(1)}, f32[1024]{0:T(1024)}, u32[]{:S(2)}) copy-start(f32[1024]{0:T(1024)} %param.28) | copy-start | bytes 12292
  66.2 182.3 %all-reduce.12.cloned.1.call-start = ((), (), s32[]{:S(2)}) async-start(), calls=%async_computation.5 | async-start | bytes 4194304 | tf_op jit(solution)/shard_map/psum | solution.py:183
  132.0 3.3 copy-start.6
  132.0 3.5 copy-start.15
  136.7 2.2 copy-start.49
  136.7 2.2 copy-start.53
  136.7 2.2 copy-start.56
  138.9 25.4 %copy-start.11 = (f32[1024,1024]{1,0:T(8,128)}, f32[1024,1024]{1,0:T(8,128)S(1)}, u32[]{:S(2)}) copy-start(f32[1024,1024]{1,0:T(8,128)S(1)} %subtract_multiply_fusion) | copy-start | bytes 12582916
  138.9 25.4 %copy-start.26 = (bf16[1024,1024]{1,0:T(8,128)(2,1)S(1)}, bf16[1024,1024]{1,0:T(8,128)(2,1)}, u32[]{:S(2)}) copy-start(bf16[1024,1024]{1,0:T(8,128)(2,1)} %param.37) | copy-start | bytes 6291460
  138.9 25.4 %copy-start.38 = (f32[1024]{0:T(1024)S(1)}, f32[1024]{0:T(1024)}, u32[]{:S(2)}) copy-start(f32[1024]{0:T(1024)} %get-tuple-element.355) | copy-start | bytes 12292
  138.9 25.4 %copy-start.42 = (f32[1024]{0:T(1024)S(1)}, f32[1024]{0:T(1024)}, u32[]{:S(2)}) copy-start(f32[1024]{0:T(1024)} %param.36) | copy-start | bytes 12292
  138.9 25.4 %copy-start.50 = (bf16[2048,1024]{1,0:T(8,128)(2,1)S(1)}, bf16[2048,1024]{1,0:T(8,128)(2,1)}, u32[]{:S(2)}) copy-start(bf16[2048,1024]{1,0:T(8,128)(2,1)} %param.34) | copy-start | bytes 12582916
  185.4 320.2 %all-reduce.16.cloned.1.call-start = ((), (), s32[]{:S(2)}) async-start(), calls=%async_computation.11 | async-start | bytes 8388608 | tf_op jit(solution)/shard_map/psum | solution.py:168
  248.5 4.0 copy-start.12
  248.5 4.7 copy-start.21
  253.2 4.2 copy-start.52
  257.4 2.4 copy-start.18
  263.5 9.7 copy-start.4
  263.5 9.6 copy-start.14
  288.0 11.5 %copy-start.9 = (f32[1024,8,64]{0,2,1:T(8,128)S(1)}, f32[1024,8,64]{0,2,1:T(8,128)}, u32[]{:S(2)}) copy-start(f32[1024,8,64]{0,2,1:T(8,128)} %get-tuple-element.597) | copy-start | bytes 6291460 | tf_op jit(solution)/shard_map/while/body/eval_jaxpr/while
  288.0 11.5 %copy-start.17 = (bf16[1024,8,64]{0,2,1:T(8,128)(2,1)S(1)}, bf16[1024,8,64]{0,2,1:T(8,128)(2,1)}, u32[]{:S(2)}) copy-start(bf16[1024,8,64]{0,2,1:T(8,128)(2,1)} %get-tuple-element.622) | copy-start | bytes 3145732 | tf_op jit(solution)/shard_map/while/body/eval_jaxpr/while
  299.6 7.8 copy-start.1
  307.4 2.3 copy-start.24
  309.8 2.7 copy-start.2
  317.4 9.7 copy-start.4
  317.5 9.6 copy-start.14
  342.0 11.5 %copy-start.9 = (f32[1024,8,64]{0,2,1:T(8,128)S(1)}, f32[1024,8,64]{0,2,1:T(8,128)}, u32[]{:S(2)}) copy-start(f32[1024,8,64]{0,2,1:T(8,128)} %get-tuple-element.597) | copy-start | bytes 6291460 | tf_op jit(solution)/shard_map/while/body/eval_jaxpr/while
  342.0 11.5 %copy-start.17 = (bf16[1024,8,64]{0,2,1:T(8,128)(2,1)S(1)}, bf16[1024,8,64]{0,2,1:T(8,128)(2,1)}, u32[]{:S(2)}) copy-start(bf16[1024,8,64]{0,2,1:T(8,128)(2,1)} %get-tuple-element.622) | copy-start | bytes 3145732 | tf_op jit(solution)/shard_map/while/body/eval_jaxpr/while
  353.5 7.8 copy-start.1
  361.4 2.3 copy-start.24
  363.7 2.7 copy-start.2
  367.7 3.6 copy-start.3
  394.6 223.9 %all-reduce.14.cloned.1.call-start = ((), (), s32[]{:S(2)}) async-start(), calls=%async_computation.10 | async-start | bytes 8388608
  403.4 7.8 copy-start.31
  411.1 5.2 copy-start.45
  411.1 5.2 copy-start.57
  411.2 267.2 %reduce-scatter.9.cloned.1.call-start = ((), (), s32[]{:S(2)}) async-start(), calls=%async_computation.6 | async-start | bytes 1114112 | tf_op jit(solution)/shard_map/reduce_scatter | solution.py:252
  416.0 337.9 %reduce-scatter.11.cloned.1.call-start = ((), (), s32[]{:S(2)}) async-start(), calls=%async_computation.7 | async-start | bytes 4456448 | tf_op jit(solution)/shard_map/reduce_scatter | solution.py:255
  426.4 403.1 %reduce-scatter.13.cloned.1.call-start = ((), (), s32[]{:S(2)}) async-start(), calls=%async_computation.8 | async-start | bytes 4456448 | tf_op jit(solution)/shard_map/reduce_scatter | solution.py:261
  436.6 2.5 copy-start.48
  436.6 528.4 %reduce-scatter.15.cloned.1.call-start = ((), (), s32[]{:S(2)}) async-start(), calls=%async_computation.9 | async-start | bytes 540672
  501.7 2.8 copy-start.13
  505.6 2.2 copy-start.7
  505.6 2.9 copy-start.20
  508.4 2.3 copy-start.19
  510.3 2.3 copy-start.23
  510.3 2.3 copy-start.35
  510.3 2.3 copy-start.47
  517.1 2.3 copy-start.22
  (16 other events, 16.9 us)
Sparse Core Ops, SparseCore 0:
  66.3 65.5 all-reduce.9
  185.5 62.9 all-reduce.11
  394.7 108.2 all-reduce.15
  507.0 111.4 all-reduce.13
  622.0 56.3 reduce-scatter.8
  682.6 71.3 reduce-scatter.10
  757.8 71.6 reduce-scatter.12
  831.9 133.0 reduce-scatter.14
where the time goes:
time: 984 us; the launch traced here: 978 us
  waiting for transfers between devices  557 us (57%)
  matrix products  198 us (20%)
  other arithmetic  83.7 us (9%)
  blocking collectives  61.7 us (6%)
  local copies, waits for them, and re-layouts  54.2 us (6%)
  between operations  16.5 us (2%)
    unnamed x10, waiting for transfers between devices  231 us
    reduce_scatter x1, waiting for transfers between devices, body(): lax.psum_scatter(grad_fc1.astype(jnp.bfloat16), 'dp', scatter_dimension=0...  74.1 us
    reduce_scatter x1, waiting for transfers between devices, body(): lax.psum_scatter(grad_fc2.astype(jnp.bfloat16), 'dp', scatter_dimension=1...  73.8 us
    psum x1, waiting for transfers between devices, body(): lax.psum(attn_terms.astype(jnp.bfloat16), 'tensor').astype(jnp.float32)  65.7 us
    unnamed x1, blocking collectives  61.7 us
    reduce_scatter x1, waiting for transfers between devices, body(): lax.psum_scatter(grad_proj.astype(jnp.bfloat16), 'dp', scatter_dimension=...  58 us
    psum x1, waiting for transfers between devices, body(): lax.psum(norm2_terms.astype(jnp.bfloat16), 'tensor').astype(jnp.float32)  53.7 us
    dot_general x4, matrix products, masked_scores(): jnp.einsum('qhc,khc->hqk', query_part, key_rows, preferred_element_type=j...  39.5 us
  transfers between devices with their start and end apart: 8, of which 7 were waited for; matrix products, arithmetic and copies ran while one was open for 7% of the time, Pallas kernels for 0%

commit v1 on v0

v1 whole, which is shorter than its diff:
```python
from functools import partial

import jax
import jax.numpy as jnp
from jax import lax
from jax.experimental import pallas as pl
from jax.experimental.pallas import tpu as pltpu
from jax.sharding import PartitionSpec as P

EPS = 1e-06
NEGATIVE = -1e30
GLOBAL_LEN = 197
LOCAL_LEN = 37
GROUP = GLOBAL_LEN // LOCAL_LEN
WINDOW = 224
BF16 = jnp.bfloat16
F32 = jnp.float32
MIB = 1 << 20


def dot_nn(a, b):
    return lax.dot_general(a, b, (((1,), (0,)), ((), ())), preferred_element_type=F32)


def dot_nt(a, b):
    return lax.dot_general(a, b, (((1,), (1,)), ((), ())), preferred_element_type=F32)


def dot_tn(a, b):
    return lax.dot_general(a, b, (((0,), (0,)), ((), ())), preferred_element_type=F32)


def norm_parts(values):
    average = jnp.mean(values, axis=-1, keepdims=True)
    centered = values - average
    inverse = lax.rsqrt(jnp.mean(centered * centered, axis=-1, keepdims=True) + EPS)
    return centered * inverse, inverse


def norm_back(grad_norm, scaled, inverse, gain):
    grad_hat = grad_norm * gain
    first_mean = jnp.mean(grad_hat, axis=-1, keepdims=True)
    second_mean = jnp.mean(grad_hat * scaled, axis=-1, keepdims=True)
    return inverse * (grad_hat - first_mean - scaled * second_mean)


def col_sum(values):
    return jnp.sum(values, axis=0, keepdims=True)


def call(kernel, name, grid, in_specs, out_specs, out_shape, args, flops, scratch=(), vmem=48, alias=None):
    moved = sum(a.size * a.dtype.itemsize for a in args) + sum(
        o.size * jnp.dtype(o.dtype).itemsize for o in jax.tree.leaves(out_shape)
    )
    return pl.pallas_call(
        kernel,
        grid=grid,
        in_specs=in_specs,
        out_specs=out_specs,
        out_shape=out_shape,
        scratch_shapes=scratch,
        input_output_aliases=alias or {},
        compiler_params=pltpu.CompilerParams(vmem_limit_bytes=vmem * MIB),
        cost_estimate=pl.CostEstimate(flops=int(flops), bytes_accessed=int(moved), transcendentals=0),
        name=name,
    )(*args)


def shape(dims, dtype):
    return jax.ShapeDtypeStruct(dims, dtype)


def whole(array):
    zeros = (0,) * array.ndim
    return pl.BlockSpec(array.shape, lambda *_: zeros)


SMEM = pl.BlockSpec(memory_space=pltpu.SMEM)


def row_total(lengths_ref):
    total = jnp.int32(0)
    for slot in range(lengths_ref.shape[1]):
        total = total + lengths_ref[0, slot]
    return total


def valid_rows(lengths_ref, first, rows):
    places = lax.broadcasted_iota(jnp.int32, (rows, 1), 0) + first
    return (places < row_total(lengths_ref)).astype(F32)


def project(tokens, gain, bias, weight, qv_bias, scale):
    count, width = tokens.shape
    local = weight.shape[2]
    rows = 256

    def kernel(x_ref, gain_ref, bias_ref, w_ref, qv_ref, q_ref, k_ref, v_ref, n_ref):
        scaled, _ = norm_parts(x_ref[...].astype(F32))
        normed = (scaled * gain_ref[...] + bias_ref[...]).astype(BF16)
        n_ref[...] = normed
        queries = (dot_nn(normed, w_ref[0]) + qv_ref[0:1]).astype(BF16)
        q_ref[...] = queries * BF16(scale)
        k_ref[...] = dot_nn(normed, w_ref[1]).astype(BF16)
        v_ref[...] = (dot_nn(normed, w_ref[2]) + qv_ref[1:2]).astype(BF16)

    by_row = pl.BlockSpec((rows, width), lambda i: (i, 0))
    by_row_local = pl.BlockSpec((rows, local), lambda i: (i, 0))
    part = shape((count, local), BF16)
    return call(
        kernel,
        "project",
        (count // rows,),
        [by_row, whole(gain), whole(bias), whole(weight), whole(qv_bias)],
        [by_row_local, by_row_local, by_row_local, by_row],
        [part, part, part, shape((count, width), BF16)],
        (tokens, gain, bias, weight, qv_bias),
        2 * count * width * 3 * local,
    )


def item_counts(lengths_ref):
    globals_ = jnp.int32(0)
    locals_ = jnp.int32(0)
    for slot in range(lengths_ref.shape[1]):
        value = lengths_ref[0, slot]
        globals_ = globals_ + jnp.where(value == GLOBAL_LEN, 1, 0)
        locals_ = locals_ + jnp.where(value == LOCAL_LEN, 1, 0)
    return globals_, locals_


def item_place(item, globals_, locals_, count):
    is_global = item < globals_
    group = item - globals_
    start = jnp.where(
        is_global, item * GLOBAL_LEN, globals_ * GLOBAL_LEN + group * (GROUP * LOCAL_LEN)
    )
    length = jnp.where(
        is_global, GLOBAL_LEN, jnp.minimum(locals_ - group * GROUP, GROUP) * LOCAL_LEN
    )
    crop = jnp.where(is_global, GLOBAL_LEN, LOCAL_LEN)
    first = jnp.minimum((start // 16) * 16, count - WINDOW)
    return pl.multiple_of(first, 16), start - first, length, crop


def crop_of(places, offset, length, crop, outside):
    inside = (places >= offset) & (places < offset + length)
    index = places - offset
    label = jnp.zeros_like(places)
    for step in range(1, GROUP):
        label = label + jnp.where(index >= step * crop, 1, 0)
    return jnp.where(inside, label, outside)


def item_total(globals_, locals_):
    return globals_ + (locals_ + GROUP - 1) // GROUP


def attend_forward(queries, keys, values, lengths):
    count, local = queries.shape
    head = 64
    pair = 2 * head

    def kernel(q_ref, k_ref, v_ref, lengths_ref, out_ref):
        globals_, locals_ = item_counts(lengths_ref)
        average = col_sum(v_ref[...].astype(F32)) * (1.0 / count)
        out_ref[...] = jnp.broadcast_to(average, (count, local)).astype(BF16)
        low_half = lax.broadcasted_iota(jnp.int32, (1, pair), 1) < head

        def step(item, carry):
            first, offset, length, crop = item_place(item, globals_, locals_, count)
            window = pl.ds(first, WINDOW)
            by_query = lax.broadcasted_iota(jnp.int32, (WINDOW, 1), 0)
            by_key = lax.broadcasted_iota(jnp.int32, (1, WINDOW), 1)
            query_crop = crop_of(by_query, offset, length, crop, -2)
            key_crop = crop_of(by_key, offset, length, crop, -1)
            mask = jnp.where(query_crop == key_crop, 0.0, NEGATIVE)
            inside = query_crop >= 0
            for index in range(local // pair):
                columns = slice(index * pair, (index + 1) * pair)
                q2 = q_ref[window, columns]
                k2 = k_ref[window, columns]
                v2 = v_ref[window, columns]
                out = None
                for keep in (low_half, jnp.logical_not(low_half)):
                    kept_k = jnp.where(keep, k2, BF16(0))
                    kept_v = jnp.where(keep, v2, BF16(0))
                    scores = dot_nt(q2, kept_k) + mask
                    weights = jnp.exp(scores - jnp.max(scores, axis=1, keepdims=True))
                    total = jnp.sum(weights, axis=1, keepdims=True)
                    low = (weights * (1.0 / total)).astype(BF16)
                    term = dot_nn(low, kept_v)
                    out = term if out is None else out + term
                out_ref[window, columns] = jnp.where(
                    inside, out, out_ref[window, columns].astype(F32)
                ).astype(BF16)
            return carry

        lax.fori_loop(0, item_total(globals_, locals_), step, 0)

    vm = pl.BlockSpec(memory_space=pltpu.VMEM)
    return call(
        kernel,
        "attend_forward",
        (),
        [vm, vm, vm, SMEM],
        vm,
        shape((count, local), BF16),
        (queries, keys, values, lengths),
        4 * count * local * WINDOW,
    )


def attend_backward(queries, keys, values, grad_mixed, lengths, scale):
    count, local = queries.shape
    head = 64
    pair = 2 * head

    def kernel(q_ref, k_ref, v_ref, g_ref, lengths_ref, out_ref, bias_ref, acc_ref):
        globals_, locals_ = item_counts(lengths_ref)
        acc_ref[...] = jnp.zeros_like(acc_ref)
        low_half = lax.broadcasted_iota(jnp.int32, (1, pair), 1) < head

        def step(item, carry):
            first, offset, length, crop = item_place(item, globals_, locals_, count)
            window = pl.ds(first, WINDOW)
            by_key = lax.broadcasted_iota(jnp.int32, (WINDOW, 1), 0)
            by_query = lax.broadcasted_iota(jnp.int32, (1, WINDOW), 1)
            query_crop = crop_of(by_query, offset, length, crop, -2)
            key_crop = crop_of(by_key, offset, length, crop, -1)
            mask = jnp.where(query_crop == key_crop, 0.0, NEGATIVE)
            inside = key_crop >= 0
            for index in range(local // pair):
                columns = slice(index * pair, (index + 1) * pair)
                q2 = q_ref[window, columns]
                k2 = k_ref[window, columns]
                v2 = v_ref[window, columns]
                g2 = jnp.where(inside, g_ref[window, columns], BF16(0))
                grad_q = grad_k = grad_v = None
                for keep in (low_half, jnp.logical_not(low_half)):
                    kept_k = jnp.where(keep, k2, BF16(0))
                    kept_v = jnp.where(keep, v2, BF16(0))
                    kept_q = jnp.where(keep, q2, BF16(0))
                    kept_g = jnp.where(keep, g2, BF16(0))
                    scores = dot_nt(kept_k, q2) + mask
                    weights = jnp.exp(scores - jnp.max(scores, axis=0, keepdims=True))
                    total = jnp.sum(weights, axis=0, keepdims=True)
                    probability = weights * (1.0 / total)
                    grad_probability = dot_nt(kept_v, g2)
                    delta = jnp.sum(probability * grad_probability, axis=0, keepdims=True)
                    grad_scores = (probability * (grad_probability - delta)).astype(BF16)
                    term_v = dot_nn(probability.astype(BF16), kept_g)
                    term_k = dot_nn(grad_scores, kept_q)
                    term_q = dot_tn(grad_scores, kept_k)
                    grad_v = term_v if grad_v is None else grad_v + term_v
                    grad_k = term_k if grad_k is None else grad_k + term_k
                    grad_q = term_q if grad_q is None else grad_q + term_q
                acc_ref[0, window, columns] += grad_q * scale
                acc_ref[1, window, columns] += grad_k
                acc_ref[2, window, columns] += grad_v
            return carry

        lax.fori_loop(0, item_total(globals_, locals_), step, 0)
        for part in range(3):
            out_ref[:, part * local : (part + 1) * local] = acc_ref[part].astype(BF16)
        bias_ref[0:1] = col_sum(acc_ref[0])
        bias_ref[1:2] = col_sum(acc_ref[2])

    vm = pl.BlockSpec(memory_space=pltpu.VMEM)
    return call(
        kernel,
        "attend_backward",
        (),
        [vm, vm, vm, vm, SMEM],
        [vm, vm],
        [shape((count, 3 * local), BF16), shape((2, local), F32)],
        (queries, keys, values, grad_mixed, lengths),
        10 * count * local * WINDOW,
        scratch=[pltpu.VMEM((3, count, local), F32)],
    )


def gelu_parts(value):
    size = jnp.abs(value)
    bell = jnp.exp(value * value * -0.5)
    t = 1.0 / (1.0 + size * (0.3275911 * 0.7071067811865476))
    poly = t * (
        0.254829592
        + t * (-0.284496736 + t * (1.421413741 + t * (-1.453152027 + t * 1.061405429)))
    )
    tail = 0.5 * poly * bell
    share = jnp.where(value >= 0, 1.0 - tail, tail)
    return value * share, share + value * (bell * 0.3989422804014327)


def feed_forward(chunk, rows, mixed, projs, tokens, cotangent, lengths, vectors, fc1, fc1_bias, fc2, kept):
    proj_bias, scale_attn, gain, bias, scale_mlp = vectors
    count, width = tokens.shape
    units = fc1.shape[1]
    step_units = min(512, units)
    steps = units // step_units
    parts = len(mixed)
    n_kept = 0 if kept is None else len(kept)

    def kernel(*refs):
        mixed_refs, refs = refs[:parts], refs[parts:]
        proj_refs, refs = refs[:parts], refs[parts:]
        x_ref, c_ref, lengths_ref, refs = refs[0], refs[1], refs[2], refs[3:]
        pb_ref, sa_ref, gain_ref, bias_ref, sm_ref, refs = *refs[:5], refs[5:]
        fc1_ref, fb_ref, fc2_ref, refs = refs[0], refs[1], refs[2], refs[3:]
        refs = refs[n_kept:]
        mid_ref, n2_ref, gm_ref, act_ref, gh_ref, fbg_ref, terms_ref, vec_ref, acc_ref = refs
        j = pl.program_id(0)

        @pl.when(j == 0)
        def _():
            attn = pb_ref[...]
            for m_ref, p_ref in zip(mixed_refs, proj_refs):
                attn = attn + dot_nn(m_ref[...], p_ref[...]).astype(BF16).astype(F32)
            middle = x_ref[...].astype(F32) + sa_ref[...] * attn
            mid_ref[...] = middle
            scaled, _ = norm_parts(middle)
            n2_ref[...] = (scaled * gain_ref[...] + bias_ref[...]).astype(BF16)
            grad = c_ref[...].astype(F32) * valid_rows(lengths_ref, chunk * rows, rows)
            gm_ref[...] = (grad * sm_ref[...]).astype(BF16)

        hidden = dot_nn(n2_ref[...], fc1_ref[...]) + fb_ref[...]
        activated, slope = gelu_parts(hidden)
        act_ref[...] = activated.astype(BF16)
        grad_hidden = dot_nt(gm_ref[...], fc2_ref[...]) * slope
        fbg_ref[...] = col_sum(grad_hidden)
        low = grad_hidden.astype(BF16)
        gh_ref[...] = low
        term = dot_nt(low, fc1_ref[...])

        @pl.when(j == 0)
        def _():
            acc_ref[...] = term

        @pl.when(j > 0)
        def _():
            acc_ref[...] += term

        @pl.when(j == steps - 1)
        def _():
            low_terms = acc_ref[...].astype(BF16)
            terms_ref[...] = low_terms
            wide = low_terms.astype(F32)
            scaled, _ = norm_parts(mid_ref[...])
            vec_ref[0:1] = col_sum(wide * scaled)
            vec_ref[1:2] = col_sum(wide)

    def of_chunk(w):
        return pl.BlockSpec((rows, w), lambda j: (chunk, 0))

    once = pl.BlockSpec((rows, mixed[0].shape[1]), lambda j: (0, 0))
    mixed_specs = [of_chunk(m.shape[1]) if m.shape[0] == count else once for m in mixed]
    row = pl.BlockSpec((1, width), lambda j: (0, 0))
    unit_block = pl.BlockSpec((rows, step_units), lambda j: (chunk, j))
    any_spec = pl.BlockSpec(memory_space=pl.ANY)
    args = (
        *mixed,
        *projs,
        tokens,
        cotangent,
        lengths,
        proj_bias,
        scale_attn,
        gain,
        bias,
        scale_mlp,
        fc1,
        fc1_bias,
        fc2,
    )
    alias = None
    if kept is not None:
        alias = {len(args) + i: i for i in range(n_kept)}
        args = args + tuple(kept)
    return call(
        kernel,
        "feed_forward",
        (steps,),
        mixed_specs
        + [whole(p) for p in projs]
        + [of_chunk(width), of_chunk(width), SMEM]
        + [row] * 5
        + [
            pl.BlockSpec((width, step_units), lambda j: (0, j)),
            pl.BlockSpec((1, step_units), lambda j: (0, j)),
            pl.BlockSpec((step_units, width), lambda j: (j, 0)),
        ]
        + [any_spec] * n_kept,
        [
            of_chunk(width),
            of_chunk(width),
            of_chunk(width),
            unit_block,
            unit_block,
            pl.BlockSpec((1, step_units), lambda j: (0, j)),
            pl.BlockSpec((rows, width), lambda j: (0, 0)),
            pl.BlockSpec((2, width), lambda j: (0, 0)),
        ],
        [
            shape((count, width), F32),
            shape((count, width), BF16),
            shape((count, width), BF16),
            shape((count, units), BF16),
            shape((count, units), BF16),
            shape((1, units), F32),
            shape((rows, width), BF16),
            shape((2, width), F32),
        ],
        args,
        2 * rows * width * (3 * units + parts * mixed[0].shape[1]),
        scratch=[pltpu.VMEM((rows, width), F32)],
        vmem=56,
        alias=alias,
    )


def second_projection(chunk, rows, activated, fc2, cotangent, lengths, scale_mlp):
    count, units = activated.shape
    width = fc2.shape[1]
    block = 256
    steps = rows // block

    def kernel(a_ref, w_ref, c_ref, lengths_ref, sm_ref, out_ref, vec_ref):
        i = pl.program_id(0)
        terms = dot_nn(a_ref[...], w_ref[...]).astype(BF16)
        out_ref[...] = terms
        grad = c_ref[...].astype(F32) * valid_rows(lengths_ref, chunk * rows + i * block, block)
        first = col_sum(grad * terms.astype(F32))
        second = col_sum(grad)

        @pl.when(i == 0)
        def _():
            vec_ref[0:1] = first
            vec_ref[1:2] = second

        @pl.when(i > 0)
        def _():
            vec_ref[0:1] += first
            vec_ref[1:2] += second

    return call(
        kernel,
        "second_projection",
        (steps,),
        [
            pl.BlockSpec((block, units), lambda i: (chunk * steps + i, 0)),
            whole(fc2),
            pl.BlockSpec((block, width), lambda i: (chunk * steps + i, 0)),
            SMEM,
            whole(scale_mlp),
        ],
        [
            pl.BlockSpec((block, width), lambda i: (i, 0)),
            pl.BlockSpec((2, width), lambda i: (0, 0)),
        ],
        [shape((rows, width), BF16), shape((2, width), F32)],
        (activated, fc2, cotangent, lengths, scale_mlp),
        2 * rows * width * units,
    )


def weight_grads(lefts, rights, step_columns, name):
    count, width = lefts[0].shape
    widths = [r.shape[1] for r in rights]
    step_columns = min([step_columns] + widths)
    starts, total = [], 0
    for w in widths:
        starts.append(total)
        total += w // step_columns
    pairs = len(lefts)

    def kernel(*refs):
        left_refs, right_refs = refs[:pairs], refs[pairs : 2 * pairs]
        out_ref = refs[2 * pairs]
        j = pl.program_id(0)
        for p in range(pairs):
            end = starts[p] + widths[p] // step_columns

            @pl.when((j >= starts[p]) & (j < end))
            def _(p=p):
                out_ref[...] = dot_tn(left_refs[p][...], right_refs[p][...]).astype(BF16)

    def right_spec(p):
        last = widths[p] // step_columns - 1
        return pl.BlockSpec(
            (count, step_columns), lambda j: (0, jnp.clip(j - starts[p], 0, last))
        )

    return call(
        kernel,
        name,
        (total,),
        [whole(l) for l in lefts] + [right_spec(p) for p in range(pairs)],
        pl.BlockSpec((width, step_columns), lambda j: (0, j)),
        shape((width, total * step_columns), BF16),
        (*lefts, *rights),
        2 * count * width * total * step_columns,
    )


def middle_back(terms, middle, tokens, cotangent, lengths, scale_attn, gain, proj):
    count, width = middle.shape
    local = proj.shape[0]
    block = 256
    parts = len(terms[0])
    chunks = len(terms)
    per = count // chunks // block
    flat = [t for group in terms for t in group]

    def kernel(*refs):
        term_refs, refs = refs[: len(flat)], refs[len(flat) :]
        mid_ref, x_ref, c_ref, lengths_ref, sa_ref, gain_ref, p_ref, refs = *refs[:7], refs[7:]
        gmid_ref, low_ref, gmix_ref, vec_ref = refs
        i = pl.program_id(0)
        for chunk in range(chunks):

            @pl.when(i // per == chunk)
            def _(chunk=chunk):
                grad_norm = None
                for part in range(parts):
                    term = term_refs[chunk * parts + part][...].astype(F32)
                    grad_norm = term if grad_norm is None else grad_norm + term
                gmid_ref[...] = grad_norm

        middle = mid_ref[...]
        scaled, inverse = norm_parts(middle)
        grad = c_ref[...].astype(F32) * valid_rows(lengths_ref, i * block, block)
        grad = grad + norm_back(gmid_ref[...], scaled, inverse, gain_ref[...])
        gmid_ref[...] = grad
        low = (sa_ref[...] * grad).astype(BF16)
        low_ref[...] = low
        gmix_ref[...] = dot_nt(low, p_ref[...]).astype(BF16)
        first = col_sum(grad * (middle - x_ref[...].astype(F32)))
        second = col_sum(grad)

        @pl.when(i == 0)
        def _():
            vec_ref[0:1] = first
            vec_ref[1:2] = second

        @pl.when(i > 0)
        def _():
            vec_ref[0:1] += first
            vec_ref[1:2] += second

    def term_spec(chunk):
        return pl.BlockSpec((block, width), lambda i: (jnp.clip(i - chunk * per, 0, per - 1), 0))

    by_row = pl.BlockSpec((block, width), lambda i: (i, 0))
    return call(
        kernel,
        "middle_back",
        (count // block,),
        [term_spec(c) for c in range(chunks) for _ in range(parts)]
        + [by_row, by_row, by_row, SMEM, whole(scale_attn), whole(gain), whole(proj)],
        [
            by_row,
            by_row,
            pl.BlockSpec((block, local), lambda i: (i, 0)),
            pl.BlockSpec((2, width), lambda i: (0, 0)),
        ],
        [
            shape((count, width), F32),
            shape((count, width), BF16),
            shape((count, local), BF16),
            shape((2, width), F32),
        ],
        (*flat, middle, tokens, cotangent, lengths, scale_attn, gain, proj),
        2 * count * width * local,
    )


def first_norm_terms(chunk, rows, grads, weight, tokens):
    count, width = tokens.shape
    local = weight.shape[2]
    block = 256
    steps = rows // block

    def kernel(g_ref, w_ref, x_ref, out_ref, vec_ref):
        i = pl.program_id(0)
        total = None
        for part in range(3):
            term = dot_nt(g_ref[:, part * local : (part + 1) * local], w_ref[part])
            total = term if total is None else total + term
        low = total.astype(BF16)
        out_ref[...] = low
        wide = low.astype(F32)
        scaled, _ = norm_parts(x_ref[...].astype(F32))
        first = col_sum(wide * scaled)
        second = col_sum(wide)

        @pl.when(i == 0)
        def _():
            vec_ref[0:1] = first
            vec_ref[1:2] = second

        @pl.when(i > 0)
        def _():
            vec_ref[0:1] += first
            vec_ref[1:2] += second

    return call(
        kernel,
        "first_norm_terms",
        (steps,),
        [
            pl.BlockSpec((block, 3 * local), lambda i: (chunk * steps + i, 0)),
            whole(weight),
            pl.BlockSpec((block, width), lambda i: (chunk * steps + i, 0)),
        ],
        [
            pl.BlockSpec((block, width), lambda i: (i, 0)),
            pl.BlockSpec((2, width), lambda i: (0, 0)),
        ],
        [shape((rows, width), BF16), shape((2, width), F32)],
        (grads, weight, tokens),
        2 * rows * width * 3 * local,
    )


def token_grads(chunk, rows, terms, grad_middle, tokens, gain, kept):
    count, width = tokens.shape
    block = 256
    steps = rows // block
    parts = len(terms)
    extra = 0 if kept is None else 1

    def kernel(*refs):
        term_refs, refs = refs[:parts], refs[parts:]
        gmid_ref, x_ref, gain_ref = refs[:3]
        out_ref = refs[3 + extra]
        grad_norm = None
        for ref in term_refs:
            term = ref[...].astype(F32)
            grad_norm = term if grad_norm is None else grad_norm + term
        scaled, inverse = norm_parts(x_ref[...].astype(F32))
        grad = gmid_ref[...] + norm_back(grad_norm, scaled, inverse, gain_ref[...])
        out_ref[...] = grad.astype(BF16)

    own = pl.BlockSpec((block, width), lambda i: (i, 0))
    by_row = pl.BlockSpec((block, width), lambda i: (chunk * steps + i, 0))
    args = (*terms, grad_middle, tokens, gain)
    alias = None
    if kept is not None:
        alias = {len(args): 0}
        args = args + (kept,)
    return call(
        kernel,
        "token_grads",
        (steps,),
        [own] * parts
        + [by_row, by_row, whole(gain)]
        + [pl.BlockSpec(memory_space=pl.ANY)] * extra,
        by_row,
        shape((count, width), BF16),
        args,
        0,
        alias=alias,
    )


def layer_output(chunk, rows, terms, middle, lengths, bias, scale, kept):
    count, width = middle.shape
    block = 256
    steps = rows // block
    parts = len(terms)
    extra = 0 if kept is None else 1

    def kernel(*refs):
        term_refs, refs = refs[:parts], refs[parts:]
        mid_ref, lengths_ref, bias_ref, scale_ref = refs[:4]
        out_ref = refs[4 + extra]
        i = pl.program_id(0)
        mlp = bias_ref[...]
        for ref in term_refs:
            mlp = mlp + ref[...].astype(F32)
        valid = valid_rows(lengths_ref, chunk * rows + i * block, block)
        out_ref[...] = (valid * (mid_ref[...] + scale_ref[...] * mlp)).astype(BF16)

    own = pl.BlockSpec((block, width), lambda i: (i, 0))
    by_row = pl.BlockSpec((block, width), lambda i: (chunk * steps + i, 0))
    args = (*terms, middle, lengths, bias, scale)
    alias = None
    if kept is not None:
        alias = {len(args): 0}
        args = args + (kept,)
    return call(
        kernel,
        "layer_output",
        (steps,),
        [own] * parts
        + [by_row, SMEM, whole(bias), whole(scale)]
        + [pl.BlockSpec(memory_space=pl.ANY)] * extra,
        by_row,
        shape((count, width), BF16),
        args,
        0,
        alias=alias,
    )


def from_peers(array):
    size = lax.axis_size("tensor")
    return [
        lax.ppermute(array, "tensor", [(i, (i + step) % size) for i in range(size)])
        for step in range(1, size)
    ]


def scatter_sum(array):
    size = lax.axis_size("dp")
    index = lax.axis_index("dp")
    stride = 1
    wide = None
    while stride < size:
        left = size // stride
        radix = 2 if stride == 1 and left % 2 == 0 else next(r for r in (2, 4, 3, left) if left % r == 0)
        if stride > 1 and left % 4 == 0 and left != 8:
            radix = 4
        rows = array.shape[0] // left
        view = array.reshape(left // radix, radix, rows, array.shape[1])
        place = (index // stride) % radix
        total = lax.dynamic_index_in_dim(view, place, 1, keepdims=False).astype(F32)
        for step in range(1, radix):
            to = lax.rem(place + step, radix)
            moves = []
            for i in range(size):
                at = (i // stride) % radix
                moves.append((i, i + ((at + step) % radix - at) * stride))
            sent = lax.dynamic_index_in_dim(view, to, 1, keepdims=False)
            total = total + lax.ppermute(sent, "dp", moves).astype(F32)
        stride *= radix
        wide = total.reshape(-1, array.shape[1])
        array = wide.astype(BF16)
    return wide


def body(
    tokens,
    lengths,
    norm1_gain,
    norm1_bias,
    qkv_weight,
    qv_bias,
    proj_weight,
    proj_bias,
    scale_attn,
    norm2_gain,
    norm2_bias,
    fc1_weight,
    fc1_bias,
    fc2_weight,
    fc2_bias,
    scale_mlp,
    cotangent,
):
    count, width = tokens.shape
    heads, head_size = qv_bias.shape[1:]
    local = heads * head_size
    units = fc1_weight.shape[1]
    tensor = lax.axis_size("tensor")
    dp = lax.axis_size("dp")
    chunks = 2
    rows = count // chunks
    scale = head_size**-0.5

    def flat(vector):
        return vector.reshape(1, -1)

    gain1, shift1, gain2, shift2 = map(flat, (norm1_gain, norm1_bias, norm2_gain, norm2_bias))
    bias_p, scale_a, bias_2, scale_m = map(flat, (proj_bias, scale_attn, fc2_bias, scale_mlp))

    projs = [proj_weight] + from_peers(proj_weight)
    queries, keys, values, normed1 = project(
        tokens, gain1, shift1, qkv_weight, qv_bias.reshape(2, local), scale
    )
    mixed = attend_forward(queries, keys, values, lengths)

    kept = None
    norm2_groups = []
    fc1_bias_sum = 0.0
    norm2_sums = 0.0
    for chunk in range(chunks):
        sent = lax.slice_in_dim(mixed, chunk * rows, (chunk + 1) * rows, axis=0)
        out = feed_forward(
            chunk,
            rows,
            [mixed] + from_peers(sent),
            projs,
            tokens,
            cotangent,
            lengths,
            (bias_p, scale_a, gain2, shift2, scale_m),
            fc1_weight,
            flat(fc1_bias),
            fc2_weight,
            kept,
        )
        kept = out[:5]
        fc1_bias_sum = fc1_bias_sum + out[5]
        norm2_sums = norm2_sums + out[7]
        norm2_groups.append([out[6]] + from_peers(out[6]))
    middle, normed2, grad_mlp, activated, grad_hidden = kept

    mlp_groups = []
    result_sums = 0.0
    for chunk in range(chunks):
        terms, sums = second_projection(
            chunk, rows, activated, fc2_weight, cotangent, lengths, scale_m
        )
        result_sums = result_sums + sums
        mlp_groups.append([terms] + from_peers(terms))

    fc_grads = weight_grads([normed2, grad_mlp], [grad_hidden, activated], 512, "fc_grads")
    fc_shares = lax.psum_scatter(fc_grads, "dp", scatter_dimension=0, tiled=True).astype(F32)

    grad_middle, grad_attn, grad_mixed, middle_sums = middle_back(
        norm2_groups, middle, tokens, cotangent, lengths, scale_a, gain2, proj_weight
    )
    grads, bias_sums = attend_backward(queries, keys, values, grad_mixed, lengths, scale)

    norm1_groups = []
    norm1_sums = 0.0
    for chunk in range(chunks):
        terms, sums = first_norm_terms(chunk, rows, grads, qkv_weight, tokens)
        norm1_sums = norm1_sums + sums
        norm1_groups.append([terms] + from_peers(terms))

    attn_grads = weight_grads([normed1, grad_attn], [grads, mixed], 512, "attn_grads")
    attn_shares = scatter_sum(attn_grads)

    output = None
    grad_tokens = None
    for chunk in range(chunks):
        output = layer_output(
            chunk, rows, mlp_groups[chunk], middle, lengths, bias_2, scale_m, output
        )
    for chunk in range(chunks):
        grad_tokens = token_grads(
            chunk, rows, norm1_groups[chunk], grad_middle, tokens, gain1, grad_tokens
        )

    once = 1.0 / tensor
    vectors = jnp.concatenate(
        [
            norm1_sums,
            middle_sums[0:1] / scale_a * once,
            middle_sums[1:2] * scale_a * once,
            norm2_sums,
            result_sums[0:1] + result_sums[1:2] * bias_2 * once,
            result_sums[1:2] * scale_m * once,
        ]
    )
    small = jnp.concatenate(
        [
            vectors.reshape(8, dp, -1).transpose(1, 0, 2).reshape(dp, -1),
            bias_sums.reshape(2 * heads, dp, -1).transpose(1, 0, 2).reshape(dp, -1),
            fc1_bias_sum.reshape(-1, dp, head_size // dp).transpose(1, 0, 2).reshape(dp, -1),
        ],
        axis=1,
    )
    small_share = scatter_sum(small)[0]
    first_end = 8 * width // dp
    second_end = first_end + 2 * local // dp
    vector_share = small_share[:first_end].reshape(8, width // dp)
    for other in from_peers(vector_share):
        vector_share = vector_share + other
    vector_share = lax.dynamic_slice_in_dim(
        vector_share, lax.axis_index("tensor") * (width // dp // tensor), width // dp // tensor, 1
    )
    bias_share = small_share[first_end:second_end].reshape(2, heads, -1)
    fc1_bias_share = small_share[second_end:].reshape(-1, head_size // dp)

    return (
        output,
        grad_tokens,
        vector_share[0],
        vector_share[1],
        jnp.stack([attn_shares[:, i * local : (i + 1) * local] for i in range(3)]),
        bias_share,
        attn_shares[:, 3 * local :].T,
        vector_share[3],
        vector_share[2],
        vector_share[4],
        vector_share[5],
        fc_shares[:, :units],
        fc1_bias_share,
        fc_shares[:, units:].T,
        vector_share[7],
        vector_share[6],
    )


def solution(mesh):
    in_specs = (
        P("dp", None),
        P("dp", None),
        P(),
        P(),
        P(None, None, "tensor"),
        P(None, "tensor", None),
        P("tensor", None),
        P(),
        P(),
        P(),
        P(),
        P(None, "tensor"),
        P("tensor"),
        P("tensor", None),
        P(),
        P(),
        P("dp", None),
    )
    out_specs = (
        P("dp", None),
        P("dp", None),
        P(("dp", "tensor")),
        P(("dp", "tensor")),
        P(None, "dp", "tensor"),
        P(None, "tensor", "dp"),
        P("tensor", "dp"),
        P(("dp", "tensor")),
        P(("dp", "tensor")),
        P(("dp", "tensor")),
        P(("dp", "tensor")),
        P("dp", "tensor"),
        P("tensor", "dp"),
        P("tensor", "dp"),
        P(("dp", "tensor")),
        P(("dp", "tensor")),
    )
    return jax.shard_map(body, mesh=mesh, in_specs=in_specs, out_specs=out_specs, check_vma=False)
```

time: 984 us -> 339 us (0.34)
  the two profiles are of different devices: /device:TPU:0 before, /device:TPU:8 now
where the time goes in v1:
time: 339 us; the launch traced here: 338 us
  waiting for transfers between devices  138 us (41%)
  Pallas kernels  130 us (38%)
  starting transfers between devices  27.5 us (8%)
  local copies, waits for them, and re-layouts  20.4 us (6%)
  between operations  14.6 us (4%)
  other arithmetic  7.25 us (2%)
    pallas_call x16, Pallas kernels, call(): pl.pallas_call(kernel, grid=grid, in_specs=in_specs, out_specs=out_specs,...  130 us
    ppermute x10, waiting for transfers between devices, from_peers(): lax.ppermute(array, 'tensor', [(i, (i + step) % size) for i in range(size)])  101 us
    ppermute x10, waiting for transfers between devices, scatter_sum(): total = total + lax.ppermute(sent, 'dp', moves).astype(F32)  36.6 us
    ppermute x10, starting transfers between devices, scatter_sum(): total = total + lax.ppermute(sent, 'dp', moves).astype(F32)  15.6 us
    ppermute x10, starting transfers between devices, from_peers(): lax.ppermute(array, 'tensor', [(i, (i + step) % size) for i in range(size)])  11.9 us
    unnamed x67, local copies, waits for them, and re-layouts  10.5 us
  transfers between devices with their start and end apart: 21, of which 8 were waited for; matrix products, arithmetic and copies ran while one was open for 5% of the time, Pallas kernels for 29%

profile of v1, /device:TPU:8, one launch (start us, length us, event | category | flops | bytes accessed | tf_op | source)
XLA Modules:
  0.0 337.9 jit_solution(12550860472593437438)
XLA Ops:
  7.2 1.6 collective-permute-start.1
  8.8 0.8 reshape.191.qv_ref
  9.6 0.7 copy-done.17
  10.2 0.7 copy-done.20
  10.9 7.2 %project.1 = (bf16[1024,512]{1,0:T(8,128)(2,1)S(1)}, bf16[1024,512]{1,0:T(8,128)(2,1)S(1)}, bf16[1024,512]{1,0:T(8,128)(2,1)S(1)}, bf16[1024,1024]{1,0:T(8,128)(2,1)S(1)}) custom-call(bf16[1024,1024]{1,0:T(8,128)(2,1)} %refs_3_.7, f32[1,1024]{1,0:T(1,128)S(1)} %bitcast.87, f32[1,1024]{1,0:T(1,128)S(1)} %bitcast.90, bf16[3,1024,512]{2,1,0:T(8,128)(2,1)} %w_ref.9, ...), custom_call_target="tpu_custom_call" | custom-call | flops 3221225472 | bytes 10498048 | tf_op jit(solution)/shard_map/project/pallas_call | solution.py:55
  18.1 5.1 %attend_forward.1.refs_0_.refs_3_ = bf16[1024,512]{1,0:T(8,128)(2,1)S(1)} custom-call(bf16[1024,512]{1,0:T(8,128)(2,1)S(1)} %get-tuple-element.50.q_ref, bf16[1024,512]{1,0:T(8,128)(2,1)S(1)} %get-tuple-element.51.k_ref, bf16[1024,512]{1,0:T(8,128)(2,1)S(1)} %get-tuple-element.52.v_ref, s32[1,23]{1,0:T(1,128)S(1)} %copy-done.14), custom_call_target="tpu_custom_call" | custom-call | flops 469762048 | bytes 4194396 | tf_op jit(solution)/shard_map/attend_forward/pallas_call | solution.py:55
  23.4 0.6 collective-permute-start.2
  24.0 1.5 collective-permute-start
  25.5 19.3 %collective-permute-done.2.refs_1_ = bf16[512,512]{1,0:T(8,128)(2,1)S(1)} collective-permute-done((bf16[512,512]{1,0:T(8,128)(2,1)S(1)}, bf16[512,512]{1,0:T(8,128)(2,1)S(1)}, u32[]{:S(2)}, u32[]{:S(2)}) %collective-permute-start.2) | collective-permute-done | bytes 524320 | tf_op jit(solution)/shard_map/ppermute | solution.py:710
  44.8 0.8 copy-done.31
  45.6 0.4 copy-done.25
  46.0 19.9 %feed_forward.2 = (f32[1024,1024]{1,0:T(8,128)}, bf16[1024,1024]{1,0:T(8,128)(2,1)}, bf16[1024,1024]{1,0:T(8,128)(2,1)}, bf16[1024,2048]{1,0:T(8,128)(2,1)}, bf1...) custom-call(bf16[1024,512]{1,0:T(8,128)(2,1)} %copy-done.3, ...), custom_call_target="tpu_custom_call" | custom-call | flops 7516192768 | bytes 34123868 | tf_op jit(solution)/shard_map/feed_forward/pallas_call | solution.py:55
  65.9 0.8 copy-done.26
  66.7 19.6 %feed_forward.3 = (f32[1024,1024]{1,0:T(8,128)}, bf16[1024,1024]{1,0:T(8,128)(2,1)}, bf16[1024,1024]{1,0:T(8,128)(2,1)}, bf16[1024,2048]{1,0:T(8,128)(2,1)}, bf1...) custom-call(bf16[1024,512]{1,0:T(8,128)(2,1)} %copy-done.3, ...), custom_call_target="tpu_custom_call", output_to_operand_aliasing={{0}: (15, {}), {1}: (16, {}), {2}: (17, {}), {3}: (18, {}),... | custom-call | flops 7516192768 | bytes 50901084 | tf_op jit(solution)/shard_map/feed_forward/pallas_call | solution.py:55
  86.3 1.6 copy-done.5
  87.9 1.6 copy-done.6
  89.5 14.0 %fc_grads.1 = bf16[1024,4096]{1,0:T(8,128)(2,1)} custom-call(bf16[1024,1024]{1,0:T(8,128)(2,1)S(1)} %copy-done.5, bf16[1024,1024]{1,0:T(8,128)(2,1)S(1)} %copy-done.6, bf16[1024,2048]{1,0:T(8,128)(2,1)} %get-tuple-element.83.refs_2_, bf16[1024,2048]{1,0:T(8,128)(2,1)} %get-tuple-element.58.a_ref.refs_3_), custom_call_target="tpu_custom_call" | custom-call | flops 8589934592 | bytes 20971520 | tf_op jit(solution)/shard_map/fc_grads/pallas_call | solution.py:55
  103.6 1.5 collective-permute-start.6
  105.1 1.1 collective-permute-start.5
  106.2 23.8 %collective-permute-done.6.refs_3_ = bf16[512,1024]{1,0:T(8,128)(2,1)} collective-permute-done((bf16[512,1024]{1,0:T(8,128)(2,1)}, bf16[512,1024]{1,0:T(8,128)(2,1)}, u32[]{:S(2)}, u32[]{:S(2)}) %collective-permute-start.6) | collective-permute-done | bytes 1048608 | tf_op jit(solution)/shard_map/ppermute | solution.py:710
  130.0 19.2 %collective-permute-done.5.refs_1_ = bf16[512,1024]{1,0:T(8,128)(2,1)} collective-permute-done((bf16[512,1024]{1,0:T(8,128)(2,1)S(1)}, bf16[512,1024]{1,0:T(8,128)(2,1)}, u32[]{:S(2)}, u32[]{:S(2)}) %collective-permute-start.5) | collective-permute-done | bytes 1048608 | tf_op jit(solution)/shard_map/ppermute | solution.py:710
  149.3 1.2 copy-done.10
  150.5 10.0 %middle_back.1 = (f32[1024,1024]{1,0:T(8,128)}, bf16[1024,1024]{1,0:T(8,128)(2,1)}, bf16[1024,512]{1,0:T(8,128)(2,1)S(1)}, f32[2,1024]{1,0:T(2,128)S(1)}) custom-call(bf16[512,1024]{1,0:T(8,128)(2,1)S(1)} %copy-done.9, bf16[512,1024]{1,0:T(8,128)(2,1)} %collective-permute-done.5.refs_1_, bf16[512,1024]{1,0:T(8,128)(2,1)S(1)} %copy-done.10, ...), custom_call_target="tpu_custom_call" | custom-call | flops 1073741824 | bytes 20987996 | tf_op jit(solution)/shard_map/middle_back/pallas_call | solution.py:55
  160.6 10.3 %attend_backward.1 = (bf16[1024,1536]{1,0:T(8,128)(2,1)}, f32[2,512]{1,0:T(2,128)S(1)}) custom-call(bf16[1024,512]{1,0:T(8,128)(2,1)S(1)} %get-tuple-element.50.q_ref, bf16[1024,512]{1,0:T(8,128)(2,1)S(1)} %get-tuple-element.51.k_ref, bf16[1024,512]{1,0:T(8,128)(2,1)S(1)} %copy-done.8, bf16[1024,512]{1,0:T(8,128)(2,1)S(1)} %get-tuple-element.64.g_ref, ...), custom_call_target="tpu_custom_call" | custom-call | flops 1174405120 | bytes 7344220 | tf_op jit(solution)/shard_map/attend_backward/pallas_call | solution.py:55
  170.9 8.1 %attn_grads.1 = bf16[1024,2048]{1,0:T(8,128)(2,1)} custom-call(bf16[1024,1024]{1,0:T(8,128)(2,1)S(1)} %copy-done.22, bf16[1024,1024]{1,0:T(8,128)(2,1)S(1)} %copy-done.19, bf16[1024,1536]{1,0:T(8,128)(2,1)} %get-tuple-element.65.g_ref.refs_2_, bf16[1024,512]{1,0:T(8,128)(2,1)S(1)} %copy-done.4), custom_call_target="tpu_custom_call" | custom-call | flops 4294967296 | bytes 12582912 | tf_op jit(solution)/shard_map/attn_grads/pallas_call | solution.py:55
  179.0 3.4 %dynamic-slice_bitcast_fusion = bf16[8,64,2048]{2,1,0:T(8,128)(2,1)} fusion(bf16[8,2,64,2048]{3,2,1,0:T(8,128)(2,1)} %bitcast.93, s32[]{:T(128)S(6)} %select_n.75), kind=kLoop, calls=%fused_computation.4 | loop fusion | bytes 4194308 | tf_op jit(solution)/shard_map/jit(dynamic_index_in_dim)/squeeze | solution.py:735
  182.4 4.3 %collective-permute-start.15 = (bf16[8,64,2048]{2,1,0:T(8,128)(2,1)}, bf16[8,64,2048]{2,1,0:T(8,128)(2,1)}, u32[]{:S(2)}, u32[]{:S(2)}) collective-permute-start(bf16[8,64,2048]{2,1,0:T(8,128)(2,1)} %dynamic-slice_bitcast_fusion), channel_id=1, source_target_pairs={{0,2},{2,0},{4,6},{6,4},{8,10},{10,8},{12,14},{14,12},{16,18},{18,... | collective-permute-start | bytes 6291464 | tf_op jit(solution)/shard_map/ppermute | solution.py:736
  186.7 0.3 reshape.201
  187.0 0.2 concatenate.16
  187.2 6.3 %second_projection.3 = (bf16[512,1024]{1,0:T(8,128)(2,1)}, f32[2,1024]{1,0:T(2,128)S(1)}) custom-call(bf16[1024,2048]{1,0:T(8,128)(2,1)} %get-tuple-element.58.a_ref.refs_3_, bf16[2048,1024]{1,0:T(8,128)(2,1)} %w_ref.7, bf16[1024,1024]{1,0:T(8,128)(2,1)S(1)} %copy-done.1, s32[1,23]{1,0:T(1,128)S(1)} %copy-done.15, f32[1,1024]{1,0:T(1,128)S(1)} %bitcast.72), custom_call_target="tpu_custom_call" | custom-call | flops 2147483648 | bytes 11546716 | tf_op jit(solution)/shard_map/second_projection/pallas_call | solution.py:55
  193.6 1.6 collective-permute-start.4
  195.2 6.0 %second_projection.2 = (bf16[512,1024]{1,0:T(8,128)(2,1)}, f32[2,1024]{1,0:T(2,128)S(1)}) custom-call(bf16[1024,2048]{1,0:T(8,128)(2,1)} %get-tuple-element.58.a_ref.refs_3_, bf16[2048,1024]{1,0:T(8,128)(2,1)} %w_ref.7, bf16[1024,1024]{1,0:T(8,128)(2,1)S(1)} %copy-done.2, s32[1,23]{1,0:T(1,128)S(1)} %copy-done.15, f32[1,1024]{1,0:T(1,128)S(1)} %bitcast.73), custom_call_target="tpu_custom_call" | custom-call | flops 2147483648 | bytes 11546716 | tf_op jit(solution)/shard_map/second_projection/pallas_call | solution.py:55
  201.1 0.6 collective-permute-start.3
  201.8 5.3 %first_norm_terms.3 = (bf16[512,1024]{1,0:T(8,128)(2,1)}, f32[2,1024]{1,0:T(2,128)S(1)}) custom-call(bf16[1024,1536]{1,0:T(8,128)(2,1)} %get-tuple-element.65.g_ref.refs_2_, bf16[3,1024,512]{2,1,0:T(8,128)(2,1)} %w_ref.9, bf16[1024,1024]{1,0:T(8,128)(2,1)S(1)} %copy-done), custom_call_target="tpu_custom_call" | custom-call | flops 1610612736 | bytes 9445376 | tf_op jit(solution)/shard_map/first_norm_terms/pallas_call | solution.py:55
  207.1 4.4 %first_norm_terms.2 = (bf16[512,1024]{1,0:T(8,128)(2,1)S(1)}, f32[2,1024]{1,0:T(2,128)S(1)}) custom-call(bf16[1024,1536]{1,0:T(8,128)(2,1)} %get-tuple-element.65.g_ref.refs_2_, bf16[3,1024,512]{2,1,0:T(8,128)(2,1)} %w_ref.9, bf16[1024,1024]{1,0:T(8,128)(2,1)S(1)} %copy-done), custom_call_target="tpu_custom_call" | custom-call | flops 1610612736 | bytes 9445376 | tf_op jit(solution)/shard_map/first_norm_terms/pallas_call | solution.py:55
  212.3 3.0 fusion
  215.4 1.3 copy-done.23
  216.7 1.1 dynamic-slice_bitcast_fusion.1
  217.7 2.4 collective-permute-start.16
  220.3 23.9 %collective-permute-done.10 = bf16[4,1,704]{2,1,0:T(2,128)(2,1)S(1)} collective-permute-done((bf16[4,1,704]{2,1,0:T(2,128)(2,1)S(1)}, bf16[4,1,704]{2,1,0:T(2,128)(2,1)S(1)}, u32[]{:S(2)}, u32[]{:S(2)}) %collective-permute-start.10) | collective-permute-done | bytes 5664 | tf_op jit(solution)/shard_map/ppermute | solution.py:736
  244.3 1.7 collective-permute-start.11
  246.0 3.2 collective-permute-start.12
  249.2 3.3 layer_output.2.refs_6_
  252.5 1.4 collective-permute-start.8
  253.9 3.3 layer_output.3
  257.2 0.6 collective-permute-start.7
  257.9 1.4 collective-permute-start.14
  259.6 0.7 copy.47
  260.3 0.7 copy.46
  261.0 38.7 %collective-permute-done.14 = f32[8,64]{1,0:T(8,128)S(1)} collective-permute-done((f32[8,64]{1,0:T(8,128)S(1)}, f32[8,64]{1,0:T(8,128)S(1)}, u32[]{:S(2)}, u32[]{:S(2)}) %collective-permute-start.14) | collective-permute-done | bytes 2080 | tf_op jit(solution)/shard_map/ppermute | solution.py:710
  299.7 1.9 fusion.1
  301.8 1.8 collective-permute-start.17
  303.6 2.1 collective-permute-start.18
  305.7 0.5 slice_bitcast_fusion.5
  306.3 3.9 %token_grads.2.refs_5_ = bf16[1024,1024]{1,0:T(8,128)(2,1)} custom-call(bf16[512,1024]{1,0:T(8,128)(2,1)} %get-tuple-element.68.refs_0_, bf16[512,1024]{1,0:T(8,128)(2,1)} %collective-permute-done.8.refs_1_, f32[1024,1024]{1,0:T(8,128)} %get-tuple-element.67.refs_2_, bf16[1024,1024]{1,0:T(8,128)(2,1)S(1)} %copy-done, f32[1,1024]{1,0:T(1,128)S(1)} %bitcast.88), custom_call_target="tpu_custom_call" | custom-call | bytes 10489856 | tf_op jit(solution)/shard_map/token_grads/pallas_call | solution.py:55
  310.2 3.7 %token_grads.3 = bf16[1024,1024]{1,0:T(8,128)(2,1)} custom-call(bf16[512,1024]{1,0:T(8,128)(2,1)S(1)} %get-tuple-element.66.refs_0_, bf16[512,1024]{1,0:T(8,128)(2,1)} %collective-permute-done.7.refs_1_, f32[1024,1024]{1,0:T(8,128)} %get-tuple-element.67.refs_2_, bf16[1024,1024]{1,0:T(8,128)(2,1)S(1)} %copy-done, ...), custom_call_target="tpu_custom_call", output_to_operand_aliasing={{}: (5, {})} | custom-call | bytes 12587008 | tf_op jit(solution)/shard_map/token_grads/pallas_call | solution.py:55
  313.9 7.6 %collective-permute-done.17 = bf16[1,64,2048]{2,1,0:T(8,128)(2,1)S(1)} collective-permute-done((bf16[1,64,2048]{2,1,0:T(8,128)(2,1)S(1)}, bf16[1,64,2048]{2,1,0:T(8,128)(2,1)S(1)}, u32[]{:S(2)}, u32[]{:S(2)}) %collective-permute-start.17) | collective-permute-done | bytes 262176 | tf_op jit(solution)/shard_map/ppermute | solution.py:736
  321.5 2.8 collective-permute-done.18
  324.3 2.3 collective-permute-done.19
  326.7 0.7 slice_bitcast_fusion.1
  327.4 0.8 pad_maximum_fusion
  328.2 1.2 convert_element_type.128
  329.4 0.8 slice_bitcast_fusion
  330.2 0.8 slice.106
  (108 shorter events, 2.0 us)
Async XLA Ops:
  7.2 321.0 %reduce-scatter.2.cloned.1.call-start = ((), (), s32[]{:S(2)}) async-start(), calls=%async_computation.1 | async-start | bytes 8912896 | tf_op jit(solution)/shard_map/reduce_scatter | solution.py:820
  7.2 37.6 %collective-permute-start.1 = (bf16[512,1024]{1,0:T(8,128)(2,1)}, bf16[512,1024]{1,0:T(8,128)(2,1)S(1)}, u32[]{:S(2)}, u32[]{:S(2)}) collective-permute-start(bf16[512,1024]{1,0:T(8,128)(2,1)} %refs_10_.1), channel_id=1, source_target_pairs={{0,1},{1,0},{2,3},{3,2},{4,5},{5,4},{6,7},{7,6},{8,9},{9,8},{10,11... | collective-permute-start | bytes 3145736 | tf_op jit(solution)/shard_map/ppermute | solution.py:710
  9.6 0.7 copy-start.17
  10.2 0.7 copy-start.20
  10.9 7.2 %copy-start.14 = (s32[1,23]{1,0:T(1,128)S(1)}, s32[1,23]{1,0:T(1,128)}, u32[]{:S(2)}) copy-start(s32[1,23]{1,0:T(1,128)} %lengths_ref.7) | copy-start | bytes 280
  18.1 5.2 %copy-start.7 = (bf16[1024,512]{1,0:T(8,128)(2,1)}, bf16[1024,512]{1,0:T(8,128)(2,1)S(1)}, u32[]{:S(2)}) copy-start(bf16[1024,512]{1,0:T(8,128)(2,1)S(1)} %get-tuple-element.52.v_ref) | copy-start | bytes 3145732
  18.1 5.2 %copy-start.21 = (bf16[1024,1024]{1,0:T(8,128)(2,1)}, bf16[1024,1024]{1,0:T(8,128)(2,1)S(1)}, u32[]{:S(2)}) copy-start(bf16[1024,1024]{1,0:T(8,128)(2,1)S(1)} %get-tuple-element.79.refs_0_) | copy-start | bytes 6291460
  23.3 21.5 %copy-start.3 = (bf16[1024,512]{1,0:T(8,128)(2,1)}, bf16[1024,512]{1,0:T(8,128)(2,1)S(1)}, u32[]{:S(2)}) copy-start(bf16[1024,512]{1,0:T(8,128)(2,1)S(1)} %attend_forward.1.refs_0_.refs_3_) | copy-start | bytes 3145732
  23.4 21.4 %collective-permute-start.2 = (bf16[512,512]{1,0:T(8,128)(2,1)S(1)}, bf16[512,512]{1,0:T(8,128)(2,1)S(1)}, u32[]{:S(2)}, u32[]{:S(2)}) collective-permute-start(bf16[512,512]{1,0:T(8,128)(2,1)S(1)} %get-tuple-element.119), channel_id=1, source_target_pairs={{0,1},{1,0},{2,3},{3,2},{4,5},{5,4},{6,7},{7,6},{8,9},{9,8},{10,11... | collective-permute-start | bytes 1572872 | tf_op jit(solution)/shard_map/ppermute | solution.py:710
  24.0 41.9 %collective-permute-start = (bf16[512,512]{1,0:T(8,128)(2,1)S(1)}, bf16[512,512]{1,0:T(8,128)(2,1)S(1)}, u32[]{:S(2)}, u32[]{:S(2)}) collective-permute-start(bf16[512,512]{1,0:T(8,128)(2,1)S(1)} %get-tuple-element.120), channel_id=1, source_target_pairs={{0,1},{1,0},{2,3},{3,2},{4,5},{5,4},{6,7},{7,6},{8,9},{9,8},{10,11... | collective-permute-start | bytes 1572872 | tf_op jit(solution)/shard_map/ppermute | solution.py:710
  44.8 0.8 copy-start.31
  44.8 1.2 copy-start.25
  65.9 0.8 copy-start.26
  86.3 1.6 copy-start.5
  87.9 1.6 copy-start.6
  103.5 1.6 copy-start.9
  103.5 45.8 %copy-start.13 = (f32[1024]{0:T(1024)S(1)}, f32[1024]{0:T(1024)}, u32[]{:S(2)}) copy-start(f32[1024]{0:T(1024)} %param.25) | copy-start | bytes 12292
  103.5 45.8 %copy-start.15 = (s32[1,23]{1,0:T(1,128)S(1)}, s32[1,23]{1,0:T(1,128)}, u32[]{:S(2)}) copy-start(s32[1,23]{1,0:T(1,128)} %lengths_ref.7) | copy-start | bytes 280
  103.5 45.8 %copy-start.16 = (f32[1024]{0:T(1024)S(1)}, f32[1024]{0:T(1024)}, u32[]{:S(2)}) copy-start(f32[1024]{0:T(1024)} %param.26) | copy-start | bytes 12292
  103.6 26.5 %collective-permute-start.6 = (bf16[512,1024]{1,0:T(8,128)(2,1)}, bf16[512,1024]{1,0:T(8,128)(2,1)}, u32[]{:S(2)}, u32[]{:S(2)}) collective-permute-start(bf16[512,1024]{1,0:T(8,128)(2,1)} %get-tuple-element.63.refs_2_), channel_id=1, source_target_pairs={{0,1},{1,0},{2,3},{3,2},{4,5},{5,4},{6,7},{7,6},{8,9},{9,8},{10,11... | collective-permute-start | bytes 3145736 | tf_op jit(solution)/shard_map/ppermute | solution.py:710
  105.1 44.2 %collective-permute-start.5 = (bf16[512,1024]{1,0:T(8,128)(2,1)S(1)}, bf16[512,1024]{1,0:T(8,128)(2,1)}, u32[]{:S(2)}, u32[]{:S(2)}) collective-permute-start(bf16[512,1024]{1,0:T(8,128)(2,1)S(1)} %copy-done.9), channel_id=1, source_target_pairs={{0,1},{1,0},{2,3},{3,2},{4,5},{5,4},{6,7},{7,6},{8,9},{9,8},{10,11... | collective-permute-start | bytes 3145736 | tf_op jit(solution)/shard_map/ppermute | solution.py:710
  149.3 1.2 copy-start.10
  150.5 10.0 %copy-start.8 = (bf16[1024,512]{1,0:T(8,128)(2,1)S(1)}, bf16[1024,512]{1,0:T(8,128)(2,1)}, u32[]{:S(2)}) copy-start(bf16[1024,512]{1,0:T(8,128)(2,1)} %copy-done.7) | copy-start | bytes 3145732
  150.5 20.3 %copy-start.22 = (bf16[1024,1024]{1,0:T(8,128)(2,1)S(1)}, bf16[1024,1024]{1,0:T(8,128)(2,1)}, u32[]{:S(2)}) copy-start(bf16[1024,1024]{1,0:T(8,128)(2,1)} %copy-done.21) | copy-start | bytes 6291460
  160.5 10.3 %copy-start.4 = (bf16[1024,512]{1,0:T(8,128)(2,1)S(1)}, bf16[1024,512]{1,0:T(8,128)(2,1)}, u32[]{:S(2)}) copy-start(bf16[1024,512]{1,0:T(8,128)(2,1)} %copy-done.3) | copy-start | bytes 3145732
  160.6 10.3 %copy-start.19 = (bf16[1024,1024]{1,0:T(8,128)(2,1)S(1)}, bf16[1024,1024]{1,0:T(8,128)(2,1)}, u32[]{:S(2)}) copy-start(bf16[1024,1024]{1,0:T(8,128)(2,1)} %get-tuple-element.80.refs_1_) | copy-start | bytes 6291460
  179.0 7.7 %copy-start.29 = (f32[1,2048]{1,0:T(1,128)S(1)}, f32[1,2048]{1,0:T(1,128)}, u32[]{:S(2)}) copy-start(f32[1,2048]{1,0:T(1,128)} %get-tuple-element.77) | copy-start | bytes 24580
  179.0 7.7 %copy-start.30 = (f32[1,2048]{1,0:T(1,128)S(1)}, f32[1,2048]{1,0:T(1,128)}, u32[]{:S(2)}) copy-start(f32[1,2048]{1,0:T(1,128)} %get-tuple-element.78) | copy-start | bytes 24580
  179.0 8.2 %copy-start.1 = (bf16[1024,1024]{1,0:T(8,128)(2,1)S(1)}, bf16[1024,1024]{1,0:T(8,128)(2,1)}, u32[]{:S(2)}) copy-start(bf16[1024,1024]{1,0:T(8,128)(2,1)} %refs_6_.5) | copy-start | bytes 6291460
  179.0 8.3 %copy-start.11 = (f32[1024]{0:T(1024)S(1)}, f32[1024]{0:T(1024)}, u32[]{:S(2)}) copy-start(f32[1024]{0:T(1024)} %param.32) | copy-start | bytes 12292
  182.4 30.0 %collective-permute-start.15 = (bf16[8,64,2048]{2,1,0:T(8,128)(2,1)}, bf16[8,64,2048]{2,1,0:T(8,128)(2,1)}, u32[]{:S(2)}, u32[]{:S(2)}) collective-permute-start(bf16[8,64,2048]{2,1,0:T(8,128)(2,1)} %dynamic-slice_bitcast_fusion), channel_id=1, source_target_pairs={{0,2},{2,0},{4,6},{6,4},{8,10},{10,8},{12,14},{14,12},{16,18},{18,... | collective-permute-start | bytes 6291464 | tf_op jit(solution)/shard_map/ppermute | solution.py:736
  187.2 7.9 %copy-start.2 = (bf16[1024,1024]{1,0:T(8,128)(2,1)S(1)}, bf16[1024,1024]{1,0:T(8,128)(2,1)}, u32[]{:S(2)}) copy-start(bf16[1024,1024]{1,0:T(8,128)(2,1)} %refs_6_.5) | copy-start | bytes 6291460
  193.6 8.2 %copy-start.27 = (f32[2,1024]{1,0:T(2,128)S(1)}, f32[2,1024]{1,0:T(2,128)}, u32[]{:S(2)}) copy-start(f32[2,1024]{1,0:T(2,128)} %get-tuple-element.72) | copy-start | bytes 24580
  193.6 8.2 %copy-start.28 = (f32[2,1024]{1,0:T(2,128)S(1)}, f32[2,1024]{1,0:T(2,128)}, u32[]{:S(2)}) copy-start(f32[2,1024]{1,0:T(2,128)} %get-tuple-element.73) | copy-start | bytes 24580
  193.6 8.2 %copy-start.12 = (f32[1024]{0:T(1024)S(1)}, f32[1024]{0:T(1024)}, u32[]{:S(2)}) copy-start(f32[1024]{0:T(1024)} %param.31) | copy-start | bytes 12292
  193.6 8.2 %copy-start = (bf16[1024,1024]{1,0:T(8,128)(2,1)S(1)}, bf16[1024,1024]{1,0:T(8,128)(2,1)}, u32[]{:S(2)}) copy-start(bf16[1024,1024]{1,0:T(8,128)(2,1)} %refs_3_.7) | copy-start | bytes 6291460
  193.6 55.6 %collective-permute-start.4 = (bf16[512,1024]{1,0:T(8,128)(2,1)}, bf16[512,1024]{1,0:T(8,128)(2,1)}, u32[]{:S(2)}, u32[]{:S(2)}) collective-permute-start(bf16[512,1024]{1,0:T(8,128)(2,1)} %get-tuple-element.61.refs_0_), channel_id=1, source_target_pairs={{0,1},{1,0},{2,3},{3,2},{4,5},{5,4},{6,7},{7,6},{8,9},{9,8},{10,11... | collective-permute-start | bytes 3145736 | tf_op jit(solution)/shard_map/ppermute | solution.py:710
  201.1 51.4 %collective-permute-start.3 = (bf16[512,1024]{1,0:T(8,128)(2,1)}, bf16[512,1024]{1,0:T(8,128)(2,1)}, u32[]{:S(2)}, u32[]{:S(2)}) collective-permute-start(bf16[512,1024]{1,0:T(8,128)(2,1)} %get-tuple-element.59.refs_0_), channel_id=1, source_target_pairs={{0,1},{1,0},{2,3},{3,2},{4,5},{5,4},{6,7},{7,6},{8,9},{9,8},{10,11... | collective-permute-start | bytes 3145736 | tf_op jit(solution)/shard_map/ppermute | solution.py:710
  212.3 7.9 %collective-permute-start.9 = (f32[8,1,704]{2,0,1:T(8,128)S(1)}, f32[8,1,704]{2,0,1:T(8,128)S(1)}, u32[]{:S(2)}, u32[]{:S(2)}) collective-permute-start(f32[8,1,704]{2,0,1:T(8,128)S(1)} %bitcast.98), channel_id=1, source_target_pairs={{0,2},{2,0},{4,6},{6,4},{8,10},{10,8},{12,14},{14,12},{16,18},{18,... | collective-permute-start | bytes 67592 | tf_op jit(solution)/shard_map/ppermute | solution.py:736
  215.4 1.3 copy-start.23
  217.7 82.0 %collective-permute-start.16 = (bf16[4,64,2048]{2,1,0:T(8,128)(2,1)}, bf16[4,64,2048]{2,1,0:T(8,128)(2,1)}, u32[]{:S(2)}, u32[]{:S(2)}) collective-permute-start(bf16[4,64,2048]{2,1,0:T(8,128)(2,1)} %dynamic-slice_bitcast_fusion.1), channel_id=1, source_target_pairs={{0,4},{2,6},{4,0},{6,2},{8,12},{10,14},{12,8},{14,10},{16,20},{18,... | collective-permute-start | bytes 3145736 | tf_op jit(solution)/shard_map/ppermute | solution.py:736
  220.2 24.1 %collective-permute-start.10 = (bf16[4,1,704]{2,1,0:T(2,128)(2,1)S(1)}, bf16[4,1,704]{2,1,0:T(2,128)(2,1)S(1)}, u32[]{:S(2)}, u32[]{:S(2)}) collective-permute-start(bf16[4,1,704]{2,1,0:T(2,128)(2,1)S(1)} %dynamic-slice_bitcast_fusion.2), channel_id=1, source_target_pairs={{0,4},{2,6},{4,0},{6,2},{8,12},{10,14},{12,8},{14,10},{16,20},{18,... | collective-permute-start | bytes 16904 | tf_op jit(solution)/shard_map/ppermute | solution.py:736
  244.3 12.9 %collective-permute-start.11 = (bf16[1,1,704]{2,1,0:T(2,128)(2,1)S(1)}, bf16[1,1,704]{2,1,0:T(2,128)(2,1)S(1)}, u32[]{:S(2)}, u32[]{:S(2)}) collective-permute-start(bf16[1,1,704]{2,1,0:T(2,128)(2,1)S(1)} %get-tuple-element.127), channel_id=1, source_target_pairs={{0,8},{2,10},{4,12},{6,14},{8,16},{10,18},{12,20},{14,22},{16,24},... | collective-permute-start | bytes 4232 | tf_op jit(solution)/shard_map/ppermute | solution.py:736
  246.0 11.8 %collective-permute-start.12 = (bf16[1,1,704]{2,1,0:T(2,128)(2,1)S(1)}, bf16[1,1,704]{2,1,0:T(2,128)(2,1)S(1)}, u32[]{:S(2)}, u32[]{:S(2)}) collective-permute-start(bf16[1,1,704]{2,1,0:T(2,128)(2,1)S(1)} %get-tuple-element.129), channel_id=1, source_target_pairs={{0,16},{2,18},{4,20},{6,22},{8,24},{10,26},{12,28},{14,30},{16,0},... | collective-permute-start | bytes 4232 | tf_op jit(solution)/shard_map/ppermute | solution.py:736
  249.2 8.6 %collective-permute-start.13 = (bf16[1,1,704]{2,1,0:T(2,128)(2,1)S(1)}, bf16[1,1,704]{2,1,0:T(2,128)(2,1)S(1)}, u32[]{:S(2)}, u32[]{:S(2)}) collective-permute-start(bf16[1,1,704]{2,1,0:T(2,128)(2,1)S(1)} %get-tuple-element.128), channel_id=1, source_target_pairs={{0,24},{2,26},{4,28},{6,30},{8,0},{10,2},{12,4},{14,6},{16,8},{18,... | collective-permute-start | bytes 4232 | tf_op jit(solution)/shard_map/ppermute | solution.py:736
  252.5 53.8 %collective-permute-start.8 = (bf16[512,1024]{1,0:T(8,128)(2,1)}, bf16[512,1024]{1,0:T(8,128)(2,1)}, u32[]{:S(2)}, u32[]{:S(2)}) collective-permute-start(bf16[512,1024]{1,0:T(8,128)(2,1)} %get-tuple-element.68.refs_0_), channel_id=1, source_target_pairs={{0,1},{1,0},{2,3},{3,2},{4,5},{5,4},{6,7},{7,6},{8,9},{9,8},{10,11... | collective-permute-start | bytes 3145736 | tf_op jit(solution)/shard_map/ppermute | solution.py:710
  257.2 53.0 %collective-permute-start.7 = (bf16[512,1024]{1,0:T(8,128)(2,1)S(1)}, bf16[512,1024]{1,0:T(8,128)(2,1)}, u32[]{:S(2)}, u32[]{:S(2)}) collective-permute-start(bf16[512,1024]{1,0:T(8,128)(2,1)S(1)} %get-tuple-element.66.refs_0_), channel_id=1, source_target_pairs={{0,1},{1,0},{2,3},{3,2},{4,5},{5,4},{6,7},{7,6},{8,9},{9,8},{10,11... | collective-permute-start | bytes 3145736 | tf_op jit(solution)/shard_map/ppermute | solution.py:710
  257.9 41.8 %collective-permute-start.14 = (f32[8,64]{1,0:T(8,128)S(1)}, f32[8,64]{1,0:T(8,128)S(1)}, u32[]{:S(2)}, u32[]{:S(2)}) collective-permute-start(f32[8,64]{1,0:T(8,128)S(1)} %reshape.202), channel_id=1, source_target_pairs={{0,1},{1,0},{2,3},{3,2},{4,5},{5,4},{6,7},{7,6},{8,9},{9,8},{10,11... | collective-permute-start | bytes 6152 | tf_op jit(solution)/shard_map/ppermute | solution.py:710
  299.7 6.5 %copy-start.18 = (f32[1024]{0:T(1024)S(1)}, f32[1024]{0:T(1024)}, u32[]{:S(2)}) copy-start(f32[1024]{0:T(1024)} %param.19) | copy-start | bytes 12292
  301.8 19.8 %collective-permute-start.17 = (bf16[1,64,2048]{2,1,0:T(8,128)(2,1)S(1)}, bf16[1,64,2048]{2,1,0:T(8,128)(2,1)S(1)}, u32[]{:S(2)}, u32[]{:S(2)}) collective-permute-start(bf16[1,64,2048]{2,1,0:T(8,128)(2,1)S(1)} %get-tuple-element.116), channel_id=1, source_target_pairs={{0,8},{2,10},{4,12},{6,14},{8,16},{10,18},{12,20},{14,22},{16,24},... | collective-permute-start | bytes 786440 | tf_op jit(solution)/shard_map/ppermute | solution.py:736
  303.6 20.8 %collective-permute-start.18 = (bf16[1,64,2048]{2,1,0:T(8,128)(2,1)S(1)}, bf16[1,64,2048]{2,1,0:T(8,128)(2,1)S(1)}, u32[]{:S(2)}, u32[]{:S(2)}) collective-permute-start(bf16[1,64,2048]{2,1,0:T(8,128)(2,1)S(1)} %get-tuple-element.118), channel_id=1, source_target_pairs={{0,16},{2,18},{4,20},{6,22},{8,24},{10,26},{12,28},{14,30},{16,0},... | collective-permute-start | bytes 786440 | tf_op jit(solution)/shard_map/ppermute | solution.py:736
  305.6 20.9 %collective-permute-start.19 = (bf16[1,64,2048]{2,1,0:T(8,128)(2,1)S(1)}, bf16[1,64,2048]{2,1,0:T(8,128)(2,1)S(1)}, u32[]{:S(2)}, u32[]{:S(2)}) collective-permute-start(bf16[1,64,2048]{2,1,0:T(8,128)(2,1)S(1)} %get-tuple-element.117), channel_id=1, source_target_pairs={{0,24},{2,26},{4,28},{6,30},{8,0},{10,2},{12,4},{14,6},{16,8},{18,... | collective-permute-start | bytes 786440 | tf_op jit(solution)/shard_map/ppermute | solution.py:736
  328.2 2.0 copy-start.24
Sparse Core Ops, SparseCore 0:
  103.7 105.9 reduce-scatter.1

commit v2 on v1

--- a/solution.py
+++ b/solution.py
@@ -16,6 +16,8 @@
 BF16 = jnp.bfloat16
 F32 = jnp.float32
 MIB = 1 << 20
+COST = 2300000000
+COSTS = {"last_output": 46000000000, "first_norm_terms": 23000000000}
 
 
 def dot_nn(a, b):
@@ -48,22 +50,31 @@
     return jnp.sum(values, axis=0, keepdims=True)
 
 
-def call(kernel, name, grid, in_specs, out_specs, out_shape, args, flops, scratch=(), vmem=48, alias=None):
-    moved = sum(a.size * a.dtype.itemsize for a in args) + sum(
-        o.size * jnp.dtype(o.dtype).itemsize for o in jax.tree.leaves(out_shape)
-    )
-    return pl.pallas_call(
-        kernel,
+def call(kernel, name, grid, in_specs, out_specs, out_shape, args, after=None, scratch=(), vmem=60, alias=None):
+    single = not isinstance(out_shape, list)
+    if single:
+        out_specs, out_shape = [out_specs], [out_shape]
+    n_in, n_out = len(args), len(out_shape)
+    n_after = 0 if after is None else 1
+
+    def ordered(*refs):
+        done = refs[n_in + n_after + n_out]
+        done[...] = jnp.zeros_like(done)
+        kernel(*refs[:n_in], *refs[n_in + n_after : n_in + n_after + n_out], *refs[n_in + n_after + n_out + 1 :])
+
+    out = pl.pallas_call(
+        ordered,
         grid=grid,
-        in_specs=in_specs,
-        out_specs=out_specs,
-        out_shape=out_shape,
+        in_specs=list(in_specs) + [pl.BlockSpec(memory_space=pl.ANY)] * n_after,
+        out_specs=list(out_specs) + [pl.BlockSpec((8, 128), lambda *_: (0, 0))],
+        out_shape=list(out_shape) + [shape((8, 128), F32)],
         scratch_shapes=scratch,
         input_output_aliases=alias or {},
         compiler_params=pltpu.CompilerParams(vmem_limit_bytes=vmem * MIB),
-        cost_estimate=pl.CostEstimate(flops=int(flops), bytes_accessed=int(moved), transcendentals=0),
+        cost_estimate=pl.CostEstimate(flops=COSTS.get(name, COST), bytes_accessed=COST, transcendentals=0),
         name=name,
-    )(*args)
+    )(*args, *([after] if n_after else []))
+    return (out[0] if single else out[:-1]), out[-1]
 
 
 def shape(dims, dtype):
@@ -90,7 +101,7 @@
     return (places < row_total(lengths_ref)).astype(F32)
 
 
-def project(tokens, gain, bias, weight, qv_bias, scale):
+def project(tokens, gain, bias, weight, qv_bias, scale, after=None):
     count, width = tokens.shape
     local = weight.shape[2]
     rows = 256
@@ -115,7 +126,7 @@
         [by_row_local, by_row_local, by_row_local, by_row],
         [part, part, part, shape((count, width), BF16)],
         (tokens, gain, bias, weight, qv_bias),
-        2 * count * width * 3 * local,
+        after,
     )
 
 
@@ -156,12 +167,17 @@
     return globals_ + (locals_ + GROUP - 1) // GROUP
 
 
-def attend_forward(queries, keys, values, lengths):
+def attend_forward(queries, keys, values, lengths, halves, after):
     count, local = queries.shape
     head = 64
     pair = 2 * head
 
-    def kernel(q_ref, k_ref, v_ref, lengths_ref, out_ref):
+    n_half = len(halves)
+
+    def kernel(q_ref, k_ref, v_ref, lengths_ref, *refs):
+        half_refs, out_ref, on_refs = refs[:n_half], refs[n_half], refs[n_half + 1 :]
+        for half_ref, on_ref in zip(half_refs, on_refs):
+            on_ref[...] = half_ref[...]
         globals_, locals_ = item_counts(lengths_ref)
         average = col_sum(v_ref[...].astype(F32)) * (1.0 / count)
         out_ref[...] = jnp.broadcast_to(average, (count, local)).astype(BF16)
@@ -203,15 +219,15 @@
         kernel,
         "attend_forward",
         (),
-        [vm, vm, vm, SMEM],
-        vm,
-        shape((count, local), BF16),
-        (queries, keys, values, lengths),
-        4 * count * local * WINDOW,
-    )
-
-
-def attend_backward(queries, keys, values, grad_mixed, lengths, scale):
+        [vm, vm, vm, SMEM] + [vm] * n_half,
+        [vm] + [vm] * n_half,
+        [shape((count, local), BF16)] + [shape(h.shape, BF16) for h in halves],
+        (queries, keys, values, lengths, *halves),
+        after,
+    )
+
+
+def attend_backward(queries, keys, values, grad_mixed, lengths, scale, after):
     count, local = queries.shape
     head = 64
     pair = 2 * head
@@ -263,8 +279,7 @@
         lax.fori_loop(0, item_total(globals_, locals_), step, 0)
         for part in range(3):
             out_ref[:, part * local : (part + 1) * local] = acc_ref[part].astype(BF16)
-        bias_ref[0:1] = col_sum(acc_ref[0])
-        bias_ref[1:2] = col_sum(acc_ref[2])
+            bias_ref[part : part + 1] = col_sum(acc_ref[part])
 
     vm = pl.BlockSpec(memory_space=pltpu.VMEM)
     return call(
@@ -273,9 +288,9 @@
         (),
         [vm, vm, vm, vm, SMEM],
         [vm, vm],
-        [shape((count, 3 * local), BF16), shape((2, local), F32)],
+        [shape((count, 3 * local), BF16), shape((3, local), F32)],
         (queries, keys, values, grad_mixed, lengths),
-        10 * count * local * WINDOW,
+        after,
         scratch=[pltpu.VMEM((3, count, local), F32)],
     )
 
@@ -293,41 +308,73 @@
     return value * share, share + value * (bell * 0.3989422804014327)
 
 
-def feed_forward(chunk, rows, mixed, projs, tokens, cotangent, lengths, vectors, fc1, fc1_bias, fc2, kept):
-    proj_bias, scale_attn, gain, bias, scale_mlp = vectors
+def hidden_cotangent(cotangent, lengths, scale_mlp, fc2, after):
+    count, width = cotangent.shape
+    units = fc2.shape[0]
+    block = 256
+
+    def kernel(c_ref, lengths_ref, sm_ref, w_ref, gm_ref, out_ref):
+        grad = c_ref[...].astype(F32) * valid_rows(lengths_ref, pl.program_id(0) * block, block)
+        low = (grad * sm_ref[...]).astype(BF16)
+        gm_ref[...] = low
+        out_ref[...] = dot_nt(low, w_ref[...]).astype(BF16)
+
+    by_row = pl.BlockSpec((block, width), lambda i: (i, 0))
+    return call(
+        kernel,
+        "hidden_cotangent",
+        (count // block,),
+        [by_row, SMEM, whole(scale_mlp), whole(fc2)],
+        [by_row, pl.BlockSpec((block, units), lambda i: (i, 0))],
+        [shape((count, width), BF16), shape((count, units), BF16)],
+        (cotangent, lengths, scale_mlp, fc2),
+        after,
+    )
+
+
+def feed_forward(chunk, rows, mixed, proj, halves, place, tokens, grad_act, vectors, fc1, fc1_bias, kept, after):
+    proj_bias, scale_attn, gain, bias = vectors
     count, width = tokens.shape
     units = fc1.shape[1]
     step_units = min(512, units)
     steps = units // step_units
     parts = len(mixed)
+    n_half = len(halves)
+    depth = proj.shape[0] // 2
     n_kept = 0 if kept is None else len(kept)
 
     def kernel(*refs):
         mixed_refs, refs = refs[:parts], refs[parts:]
-        proj_refs, refs = refs[:parts], refs[parts:]
-        x_ref, c_ref, lengths_ref, refs = refs[0], refs[1], refs[2], refs[3:]
-        pb_ref, sa_ref, gain_ref, bias_ref, sm_ref, refs = *refs[:5], refs[5:]
-        fc1_ref, fb_ref, fc2_ref, refs = refs[0], refs[1], refs[2], refs[3:]
-        refs = refs[n_kept:]
-        mid_ref, n2_ref, gm_ref, act_ref, gh_ref, fbg_ref, terms_ref, vec_ref, acc_ref = refs
+        p_ref, refs = refs[0], refs[1:]
+        half_refs, refs = refs[:n_half], refs[n_half:]
+        place_ref, refs = refs[0], refs[1:]
+        x_ref, ga_ref, pb_ref, sa_ref, gain_ref, bias_ref, fc1_ref, fb_ref = refs[:8]
+        mid_ref, n2_ref, act_ref, gh_ref, fbg_ref, terms_ref, vec_ref, acc_ref = refs[8 + n_kept :]
         j = pl.program_id(0)
 
         @pl.when(j == 0)
         def _():
             attn = pb_ref[...]
-            for m_ref, p_ref in zip(mixed_refs, proj_refs):
-                attn = attn + dot_nn(m_ref[...], p_ref[...]).astype(BF16).astype(F32)
+            attn = attn + dot_nn(mixed_refs[0][...], p_ref[...]).astype(BF16).astype(F32)
+            for peer in range(parts - 1):
+                m_ref = mixed_refs[peer + 1]
+                if n_half == parts - 1:
+                    term = dot_nn(m_ref[...], half_refs[peer][...])
+                else:
+                    first = pl.ds(pl.multiple_of(place_ref[0] * depth, depth), depth)
+                    other = pl.ds(pl.multiple_of((1 - place_ref[0]) * depth, depth), depth)
+                    term = dot_nn(m_ref[:, first], half_refs[2 * peer][...])
+                    term = term + dot_nn(m_ref[:, other], half_refs[2 * peer + 1][...])
+                attn = attn + term.astype(BF16).astype(F32)
             middle = x_ref[...].astype(F32) + sa_ref[...] * attn
             mid_ref[...] = middle
             scaled, _ = norm_parts(middle)
             n2_ref[...] = (scaled * gain_ref[...] + bias_ref[...]).astype(BF16)
-            grad = c_ref[...].astype(F32) * valid_rows(lengths_ref, chunk * rows, rows)
-            gm_ref[...] = (grad * sm_ref[...]).astype(BF16)
 
         hidden = dot_nn(n2_ref[...], fc1_ref[...]) + fb_ref[...]
         activated, slope = gelu_parts(hidden)
         act_ref[...] = activated.astype(BF16)
-        grad_hidden = dot_nt(gm_ref[...], fc2_ref[...]) * slope
+        grad_hidden = ga_ref[...].astype(F32) * slope
         fbg_ref[...] = col_sum(grad_hidden)
         low = grad_hidden.astype(BF16)
         gh_ref[...] = low
@@ -357,22 +404,9 @@
     mixed_specs = [of_chunk(m.shape[1]) if m.shape[0] == count else once for m in mixed]
     row = pl.BlockSpec((1, width), lambda j: (0, 0))
     unit_block = pl.BlockSpec((rows, step_units), lambda j: (chunk, j))
+    unit_row = pl.BlockSpec((1, step_units), lambda j: (0, j))
     any_spec = pl.BlockSpec(memory_space=pl.ANY)
-    args = (
-        *mixed,
-        *projs,
-        tokens,
-        cotangent,
-        lengths,
-        proj_bias,
-        scale_attn,
-        gain,
-        bias,
-        scale_mlp,
-        fc1,
-        fc1_bias,
-        fc2,
-    )
+    args = (*mixed, proj, *halves, place, tokens, grad_act, proj_bias, scale_attn, gain, bias, fc1, fc1_bias)
     alias = None
     if kept is not None:
         alias = {len(args) + i: i for i in range(n_kept)}
@@ -382,28 +416,23 @@
         "feed_forward",
         (steps,),
         mixed_specs
-        + [whole(p) for p in projs]
-        + [of_chunk(width), of_chunk(width), SMEM]
-        + [row] * 5
-        + [
-            pl.BlockSpec((width, step_units), lambda j: (0, j)),
-            pl.BlockSpec((1, step_units), lambda j: (0, j)),
-            pl.BlockSpec((step_units, width), lambda j: (j, 0)),
-        ]
+        + [whole(proj)]
+        + [whole(h) for h in halves]
+        + [SMEM, of_chunk(width), unit_block]
+        + [row] * 4
+        + [pl.BlockSpec((width, step_units), lambda j: (0, j)), unit_row]
         + [any_spec] * n_kept,
         [
             of_chunk(width),
             of_chunk(width),
-            of_chunk(width),
             unit_block,
             unit_block,
-            pl.BlockSpec((1, step_units), lambda j: (0, j)),
+            unit_row,
             pl.BlockSpec((rows, width), lambda j: (0, 0)),
             pl.BlockSpec((2, width), lambda j: (0, 0)),
         ],
         [
             shape((count, width), F32),
-            shape((count, width), BF16),
             shape((count, width), BF16),
             shape((count, units), BF16),
             shape((count, units), BF16),
@@ -412,24 +441,30 @@
             shape((2, width), F32),
         ],
         args,
-        2 * rows * width * (3 * units + parts * mixed[0].shape[1]),
+        after,
         scratch=[pltpu.VMEM((rows, width), F32)],
-        vmem=56,
         alias=alias,
     )
 
 
-def second_projection(chunk, rows, activated, fc2, cotangent, lengths, scale_mlp):
+def second_projection(chunks, activated, fc2, cotangent, lengths, after):
     count, units = activated.shape
     width = fc2.shape[1]
     block = 256
-    steps = rows // block
-
-    def kernel(a_ref, w_ref, c_ref, lengths_ref, sm_ref, out_ref, vec_ref):
+    steps = count // block
+    per = steps // chunks
+
+    def kernel(a_ref, w_ref, c_ref, lengths_ref, *refs):
+        out_refs, vec_ref = refs[:-1], refs[-1]
         i = pl.program_id(0)
         terms = dot_nn(a_ref[...], w_ref[...]).astype(BF16)
-        out_ref[...] = terms
-        grad = c_ref[...].astype(F32) * valid_rows(lengths_ref, chunk * rows + i * block, block)
+        for chunk in range(chunks):
+
+            @pl.when(i // per == chunk)
+            def _(chunk=chunk):
+                out_refs[chunk][...] = terms
+
+        grad = c_ref[...].astype(F32) * valid_rows(lengths_ref, i * block, block)
         first = col_sum(grad * terms.astype(F32))
         second = col_sum(grad)
 
@@ -443,28 +478,27 @@
             vec_ref[0:1] += first
             vec_ref[1:2] += second
 
+    def chunk_spec(chunk):
+        return pl.BlockSpec((block, width), lambda i: (jnp.clip(i - chunk * per, 0, per - 1), 0))
+
     return call(
         kernel,
         "second_projection",
         (steps,),
         [
-            pl.BlockSpec((block, units), lambda i: (chunk * steps + i, 0)),
+            pl.BlockSpec((block, units), lambda i: (i, 0)),
             whole(fc2),
-            pl.BlockSpec((block, width), lambda i: (chunk * steps + i, 0)),
+            pl.BlockSpec((block, width), lambda i: (i, 0)),
             SMEM,
-            whole(scale_mlp),
         ],
-        [
-            pl.BlockSpec((block, width), lambda i: (i, 0)),
-            pl.BlockSpec((2, width), lambda i: (0, 0)),
-        ],
-        [shape((rows, width), BF16), shape((2, width), F32)],
-        (activated, fc2, cotangent, lengths, scale_mlp),
-        2 * rows * width * units,
-    )
-
-
-def weight_grads(lefts, rights, step_columns, name):
+        [chunk_spec(c) for c in range(chunks)] + [pl.BlockSpec((2, width), lambda i: (0, 0))],
+        [shape((count // chunks, width), BF16)] * chunks + [shape((2, width), F32)],
+        (activated, fc2, cotangent, lengths),
+        after,
+    )
+
+
+def weight_grads(lefts, rights, step_columns, name, after):
     count, width = lefts[0].shape
     widths = [r.shape[1] for r in rights]
     step_columns = min([step_columns] + widths)
@@ -499,38 +533,142 @@
         pl.BlockSpec((width, step_columns), lambda j: (0, j)),
         shape((width, total * step_columns), BF16),
         (*lefts, *rights),
-        2 * count * width * total * step_columns,
-    )
-
-
-def middle_back(terms, middle, tokens, cotangent, lengths, scale_attn, gain, proj):
+        after,
+    )
+
+
+def attention_grads(normed, grads, grad_attn, mixed, weight, sums, vectors, place, radix, shard, after):
+    count, width = normed.shape
+    block = max(256, radix * shard)
+    wide, local = grads.shape[1], mixed.shape[1]
+    extra = vectors.shape[0]
+    total = wide + local + extra
+    groups = block // (radix * shard)
+
+    def kernel(n_ref, g_ref, a_ref, m_ref, w_ref, s_ref, v_ref, place_ref, *refs):
+        out_refs, hold_ref = refs[:radix], refs[radix]
+        columns = v_ref[...].T
+        first = second = None
+        product = dot_tn(n_ref[...], g_ref[...])
+        for part in range(3):
+            piece = product[:, part * local : (part + 1) * local]
+            w = w_ref[part].astype(F32)
+            one = jnp.sum(w * piece, axis=1, keepdims=True)
+            two = jnp.sum(w * s_ref[part : part + 1], axis=1, keepdims=True)
+            first = one if first is None else first + one
+            second = two if second is None else second + two
+        lane = lax.broadcasted_iota(jnp.int32, (block, extra), 1)
+        gain_grad = (first - columns[:, 1:2] * second) / columns[:, 0:1]
+        small = jnp.where(lane == 0, gain_grad, jnp.where(lane == 1, second, columns))
+        hold_ref[:, :, :, :wide] = product.astype(BF16).reshape(groups, radix, shard, wide)
+        hold_ref[:, :, :, wide : wide + local] = (
+            dot_tn(a_ref[...], m_ref[...]).astype(BF16).reshape(groups, radix, shard, local)
+        )
+        hold_ref[:, :, :, wide + local :] = small.astype(BF16).reshape(groups, radix, shard, extra)
+        for step in range(radix):
+            out_refs[step][...] = hold_ref[:, lax.rem(place_ref[0] + step, radix)]
+
+    by_column = pl.BlockSpec((count, block), lambda i: (0, i))
+    return call(
+        kernel,
+        "attention_grads",
+        (width // block,),
+        [
+            by_column,
+            whole(grads),
+            by_column,
+            whole(mixed),
+            pl.BlockSpec((3, block, local), lambda i: (0, i, 0)),
+            whole(sums),
+            pl.BlockSpec((extra, block), lambda i: (0, i)),
+            SMEM,
+        ],
+        [pl.BlockSpec((groups, shard, total), lambda i: (i, 0, 0))] * radix,
+        [shape((width // (radix * shard), shard, total), BF16)] * radix,
+        (normed, grads, grad_attn, mixed, weight, sums, vectors, place),
+        after,
+        scratch=[pltpu.VMEM((groups, radix, shard, total), BF16)],
+    )
+
+
+def add_stage(parts, place, radix, after):
+    left, shard, columns = parts[0].shape
+    n_parts = len(parts)
+
+    def kernel(*refs):
+        part_refs, place_ref = refs[:n_parts], refs[n_parts]
+        out_refs, hold_ref = refs[n_parts + 1 : n_parts + 1 + radix], refs[n_parts + 1 + radix]
+        total = None
+        for ref in part_refs:
+            term = ref[...].astype(F32)
+            total = term if total is None else total + term
+        hold_ref[...] = total.astype(BF16)
+        for step in range(radix):
+            out_refs[step][...] = hold_ref[lax.rem(place_ref[0] + step, radix)][None]
+
+    return call(
+        kernel,
+        "add_stage",
+        (left // radix,),
+        [pl.BlockSpec((radix, shard, columns), lambda i: (i, 0, 0))] * n_parts + [SMEM],
+        [pl.BlockSpec((1, shard, columns), lambda i: (i, 0, 0))] * radix,
+        [shape((left // radix, shard, columns), BF16)] * radix,
+        (*parts, place),
+        after,
+        scratch=[pltpu.VMEM((radix, shard, columns), BF16)],
+    )
+
+
+def last_stage(parts, local, after):
+    _, shard, columns = parts[0].shape
+    n_parts = len(parts)
+    extra = columns - 4 * local
+
+    def kernel(*refs):
+        part_refs, (qkv_ref, proj_ref, small_ref) = refs[:n_parts], refs[n_parts:]
+        total = None
+        for ref in part_refs:
+            term = ref[0].astype(F32)
+            total = term if total is None else total + term
+        for part in range(3):
+            qkv_ref[part] = total[:, part * local : (part + 1) * local]
+        proj_ref[...] = total[:, 3 * local : 4 * local].T
+        small_ref[...] = total[:, 4 * local :].T
+
+    vm = pl.BlockSpec(memory_space=pltpu.VMEM)
+    return call(
+        kernel,
+        "last_stage",
+        (),
+        [vm] * n_parts,
+        [vm, vm, vm],
+        [shape((3, shard, local), F32), shape((local, shard), F32), shape((extra, shard), F32)],
+        tuple(parts),
+        after,
+    )
+
+
+def middle_back(chunk, rows, terms, middle, tokens, cotangent, lengths, scale_attn, gain, proj, kept, after):
     count, width = middle.shape
     local = proj.shape[0]
     block = 256
-    parts = len(terms[0])
-    chunks = len(terms)
-    per = count // chunks // block
-    flat = [t for group in terms for t in group]
+    steps = rows // block
+    parts = len(terms)
+    n_kept = 0 if kept is None else len(kept)
 
     def kernel(*refs):
-        term_refs, refs = refs[: len(flat)], refs[len(flat) :]
-        mid_ref, x_ref, c_ref, lengths_ref, sa_ref, gain_ref, p_ref, refs = *refs[:7], refs[7:]
-        gmid_ref, low_ref, gmix_ref, vec_ref = refs
+        term_refs, refs = refs[:parts], refs[parts:]
+        mid_ref, x_ref, c_ref, lengths_ref, sa_ref, gain_ref, p_ref = refs[:7]
+        gmid_ref, low_ref, gmix_ref, vec_ref = refs[7 + n_kept :]
         i = pl.program_id(0)
-        for chunk in range(chunks):
-
-            @pl.when(i // per == chunk)
-            def _(chunk=chunk):
-                grad_norm = None
-                for part in range(parts):
-                    term = term_refs[chunk * parts + part][...].astype(F32)
-                    grad_norm = term if grad_norm is None else grad_norm + term
-                gmid_ref[...] = grad_norm
-
+        grad_norm = None
+        for ref in term_refs:
+            term = ref[...].astype(F32)
+            grad_norm = term if grad_norm is None else grad_norm + term
         middle = mid_ref[...]
         scaled, inverse = norm_parts(middle)
-        grad = c_ref[...].astype(F32) * valid_rows(lengths_ref, i * block, block)
-        grad = grad + norm_back(gmid_ref[...], scaled, inverse, gain_ref[...])
+        grad = c_ref[...].astype(F32) * valid_rows(lengths_ref, chunk * rows + i * block, block)
+        grad = grad + norm_back(grad_norm, scaled, inverse, gain_ref[...])
         gmid_ref[...] = grad
         low = (sa_ref[...] * grad).astype(BF16)
         low_ref[...] = low
@@ -548,20 +686,24 @@
             vec_ref[0:1] += first
             vec_ref[1:2] += second
 
-    def term_spec(chunk):
-        return pl.BlockSpec((block, width), lambda i: (jnp.clip(i - chunk * per, 0, per - 1), 0))
-
-    by_row = pl.BlockSpec((block, width), lambda i: (i, 0))
+    own = pl.BlockSpec((block, width), lambda i: (i, 0))
+    by_row = pl.BlockSpec((block, width), lambda i: (chunk * steps + i, 0))
+    args = (*terms, middle, tokens, cotangent, lengths, scale_attn, gain, proj)
+    alias = None
+    if kept is not None:
+        alias = {len(args) + i: i for i in range(n_kept)}
+        args = args + tuple(kept)
     return call(
         kernel,
         "middle_back",
-        (count // block,),
-        [term_spec(c) for c in range(chunks) for _ in range(parts)]
-        + [by_row, by_row, by_row, SMEM, whole(scale_attn), whole(gain), whole(proj)],
+        (steps,),
+        [own] * parts
+        + [by_row, by_row, by_row, SMEM, whole(scale_attn), whole(gain), whole(proj)]
+        + [pl.BlockSpec(memory_space=pl.ANY)] * n_kept,
         [
             by_row,
             by_row,
-            pl.BlockSpec((block, local), lambda i: (i, 0)),
+            pl.BlockSpec((block, local), lambda i: (chunk * steps + i, 0)),
             pl.BlockSpec((2, width), lambda i: (0, 0)),
         ],
         [
@@ -570,60 +712,37 @@
             shape((count, local), BF16),
             shape((2, width), F32),
         ],
-        (*flat, middle, tokens, cotangent, lengths, scale_attn, gain, proj),
-        2 * count * width * local,
-    )
-
-
-def first_norm_terms(chunk, rows, grads, weight, tokens):
-    count, width = tokens.shape
-    local = weight.shape[2]
+        args,
+        after,
+        alias=alias,
+    )
+
+
+def first_norm_terms(chunk, rows, grads, weight, after):
+    width, local = weight.shape[1:]
     block = 256
     steps = rows // block
 
-    def kernel(g_ref, w_ref, x_ref, out_ref, vec_ref):
-        i = pl.program_id(0)
+    def kernel(g_ref, w_ref, out_ref):
         total = None
         for part in range(3):
             term = dot_nt(g_ref[:, part * local : (part + 1) * local], w_ref[part])
             total = term if total is None else total + term
-        low = total.astype(BF16)
-        out_ref[...] = low
-        wide = low.astype(F32)
-        scaled, _ = norm_parts(x_ref[...].astype(F32))
-        first = col_sum(wide * scaled)
-        second = col_sum(wide)
-
-        @pl.when(i == 0)
-        def _():
-            vec_ref[0:1] = first
-            vec_ref[1:2] = second
-
-        @pl.when(i > 0)
-        def _():
-            vec_ref[0:1] += first
-            vec_ref[1:2] += second
+        out_ref[...] = total.astype(BF16)
 
     return call(
         kernel,
         "first_norm_terms",
         (steps,),
-        [
-            pl.BlockSpec((block, 3 * local), lambda i: (chunk * steps + i, 0)),
-            whole(weight),
-            pl.BlockSpec((block, width), lambda i: (chunk * steps + i, 0)),
-        ],
-        [
-            pl.BlockSpec((block, width), lambda i: (i, 0)),
-            pl.BlockSpec((2, width), lambda i: (0, 0)),
-        ],
-        [shape((rows, width), BF16), shape((2, width), F32)],
-        (grads, weight, tokens),
-        2 * rows * width * 3 * local,
-    )
-
-
-def token_grads(chunk, rows, terms, grad_middle, tokens, gain, kept):
+        [pl.BlockSpec((block, 3 * local), lambda i: (chunk * steps + i, 0)), whole(weight)],
+        pl.BlockSpec((block, width), lambda i: (i, 0)),
+        shape((rows, width), BF16),
+        (grads, weight),
+        after,
+    )
+
+
+def token_grads(chunk, rows, terms, grad_middle, tokens, gain, kept, after):
     count, width = tokens.shape
     block = 256
     steps = rows // block
@@ -659,12 +778,12 @@
         by_row,
         shape((count, width), BF16),
         args,
-        0,
+        after,
         alias=alias,
     )
 
 
-def layer_output(chunk, rows, terms, middle, lengths, bias, scale, kept):
+def layer_output(chunk, rows, terms, middle, lengths, bias, scale, kept, after, name="layer_output"):
     count, width = middle.shape
     block = 256
     steps = rows // block
@@ -691,7 +810,7 @@
         args = args + (kept,)
     return call(
         kernel,
-        "layer_output",
+        name,
         (steps,),
         [own] * parts
         + [by_row, SMEM, whole(bias), whole(scale)]
@@ -699,7 +818,7 @@
         by_row,
         shape((count, width), BF16),
         args,
-        0,
+        after,
         alias=alias,
     )
 
@@ -712,32 +831,32 @@
     ]
 
 
-def scatter_sum(array):
+def other_of_pair(array):
+    return lax.ppermute(array, "dp", [(i, i ^ 1) for i in range(lax.axis_size("dp"))])
+
+
+def radices(size):
+    found = []
+    if size % 2 == 0:
+        found.append(2)
+        size //= 2
+    while size > 1:
+        step = 2 if size % 4 and size % 2 == 0 or size == 8 else next((r for r in (4, 3) if size % r == 0), size)
+        found.append(step)
+        size //= step
+    return found
+
+
+def exchange(parts, stride, radix):
     size = lax.axis_size("dp")
-    index = lax.axis_index("dp")
-    stride = 1
-    wide = None
-    while stride < size:
-        left = size // stride
-        radix = 2 if stride == 1 and left % 2 == 0 else next(r for r in (2, 4, 3, left) if left % r == 0)
-        if stride > 1 and left % 4 == 0 and left != 8:
-            radix = 4
-        rows = array.shape[0] // left
-        view = array.reshape(left // radix, radix, rows, array.shape[1])
-        place = (index // stride) % radix
-        total = lax.dynamic_index_in_dim(view, place, 1, keepdims=False).astype(F32)
-        for step in range(1, radix):
-            to = lax.rem(place + step, radix)
-            moves = []
-            for i in range(size):
-                at = (i // stride) % radix
-                moves.append((i, i + ((at + step) % radix - at) * stride))
-            sent = lax.dynamic_index_in_dim(view, to, 1, keepdims=False)
-            total = total + lax.ppermute(sent, "dp", moves).astype(F32)
-        stride *= radix
-        wide = total.reshape(-1, array.shape[1])
-        array = wide.astype(BF16)
-    return wide
+    arrived = []
+    for step in range(1, radix):
+        moves = []
+        for i in range(size):
+            at = (i // stride) % radix
+            moves.append((i, i + ((at + step) % radix - at) * stride))
+        arrived.append(lax.ppermute(parts[step], "dp", moves))
+    return [parts[0]] + arrived
 
 
 def body(
@@ -775,121 +894,176 @@
     gain1, shift1, gain2, shift2 = map(flat, (norm1_gain, norm1_bias, norm2_gain, norm2_bias))
     bias_p, scale_a, bias_2, scale_m = map(flat, (proj_bias, scale_attn, fc2_bias, scale_mlp))
 
-    projs = [proj_weight] + from_peers(proj_weight)
-    queries, keys, values, normed1 = project(
+    index = lax.axis_index("dp")
+    steps = radices(dp)
+    strides = [1]
+    for step in steps:
+        strides.append(strides[-1] * step)
+    places = [((index // stride) % step).reshape(1) for stride, step in zip(strides, steps)]
+
+    half_rows = local // 2
+    paired = dp % 2 == 0 and half_rows % 128 == 0
+    half_place = (index % 2).reshape(1)
+    half = proj_weight
+    if paired:
+        half = lax.dynamic_slice_in_dim(proj_weight, half_place[0] * half_rows, half_rows, 0)
+    halves = from_peers(half)
+    (queries, keys, values, normed1), done = project(
         tokens, gain1, shift1, qkv_weight, qv_bias.reshape(2, local), scale
     )
-    mixed = attend_forward(queries, keys, values, lengths)
+    (mixed, *halves), done = attend_forward(queries, keys, values, lengths, halves, done)
+    mixed_parts = [
+        from_peers(lax.slice_in_dim(mixed, chunk * rows, (chunk + 1) * rows, axis=0))
+        for chunk in range(chunks)
+    ]
+    if paired:
+        halves = [part for half in halves for part in (half, other_of_pair(half))]
+    (grad_mlp, grad_act), done = hidden_cotangent(cotangent, lengths, scale_m, fc2_weight, done)
 
     kept = None
-    norm2_groups = []
+    norm2_parts = []
     fc1_bias_sum = 0.0
     norm2_sums = 0.0
     for chunk in range(chunks):
-        sent = lax.slice_in_dim(mixed, chunk * rows, (chunk + 1) * rows, axis=0)
-        out = feed_forward(
+        out, done = feed_forward(
             chunk,
             rows,
-            [mixed] + from_peers(sent),
-            projs,
+            [mixed] + mixed_parts[chunk],
+            proj_weight,
+            halves,
+            half_place,
+            tokens,
+            grad_act,
+            (bias_p, scale_a, gain2, shift2),
+            fc1_weight,
+            flat(fc1_bias),
+            kept,
+            done,
+        )
+        kept = out[:4]
+        fc1_bias_sum = fc1_bias_sum + out[4]
+        norm2_sums = norm2_sums + out[6]
+        norm2_parts.append([out[5]] + from_peers(out[5]))
+    middle, normed2, activated, grad_hidden = kept
+
+    fc_grads, done = weight_grads(
+        [normed2, grad_mlp], [grad_hidden, activated], 512, "fc_grads", done
+    )
+    fc_shares = lax.psum_scatter(fc_grads, "dp", scatter_dimension=0, tiled=True).astype(F32)
+
+    (*mlp_terms, result_sums), done = second_projection(
+        chunks, activated, fc2_weight, cotangent, lengths, done
+    )
+    mlp_parts = [[terms] + from_peers(terms) for terms in mlp_terms]
+
+    kept = None
+    middle_sums = 0.0
+    for chunk in range(chunks):
+        out, done = middle_back(
+            chunk,
+            rows,
+            norm2_parts[chunk],
+            middle,
             tokens,
             cotangent,
             lengths,
-            (bias_p, scale_a, gain2, shift2, scale_m),
-            fc1_weight,
-            flat(fc1_bias),
-            fc2_weight,
+            scale_a,
+            gain2,
+            proj_weight,
             kept,
+            done,
         )
-        kept = out[:5]
-        fc1_bias_sum = fc1_bias_sum + out[5]
-        norm2_sums = norm2_sums + out[7]
-        norm2_groups.append([out[6]] + from_peers(out[6]))
-    middle, normed2, grad_mlp, activated, grad_hidden = kept
-
-    mlp_groups = []
-    result_sums = 0.0
-    for chunk in range(chunks):
-        terms, sums = second_projection(
-            chunk, rows, activated, fc2_weight, cotangent, lengths, scale_m
-        )
-        result_sums = result_sums + sums
-        mlp_groups.append([terms] + from_peers(terms))
-
-    fc_grads = weight_grads([normed2, grad_mlp], [grad_hidden, activated], 512, "fc_grads")
-    fc_shares = lax.psum_scatter(fc_grads, "dp", scatter_dimension=0, tiled=True).astype(F32)
-
-    grad_middle, grad_attn, grad_mixed, middle_sums = middle_back(
-        norm2_groups, middle, tokens, cotangent, lengths, scale_a, gain2, proj_weight
-    )
-    grads, bias_sums = attend_backward(queries, keys, values, grad_mixed, lengths, scale)
-
-    norm1_groups = []
-    norm1_sums = 0.0
-    for chunk in range(chunks):
-        terms, sums = first_norm_terms(chunk, rows, grads, qkv_weight, tokens)
-        norm1_sums = norm1_sums + sums
-        norm1_groups.append([terms] + from_peers(terms))
-
-    attn_grads = weight_grads([normed1, grad_attn], [grads, mixed], 512, "attn_grads")
-    attn_shares = scatter_sum(attn_grads)
-
-    output = None
-    grad_tokens = None
-    for chunk in range(chunks):
-        output = layer_output(
-            chunk, rows, mlp_groups[chunk], middle, lengths, bias_2, scale_m, output
-        )
-    for chunk in range(chunks):
-        grad_tokens = token_grads(
-            chunk, rows, norm1_groups[chunk], grad_middle, tokens, gain1, grad_tokens
-        )
+        kept = out[:3]
+        middle_sums = middle_sums + out[3]
+    grad_middle, grad_attn, grad_mixed = kept
+    (grads, grad_sums), done = attend_backward(
+        queries, keys, values, grad_mixed, lengths, scale, done
+    )
 
     once = 1.0 / tensor
+    shard = width // dp
+
+    def by_shard(array):
+        entries = array.reshape(-1, dp, array.shape[-1] // dp).transpose(1, 0, 2).reshape(dp, -1)
+        entries = jnp.pad(entries, ((0, 0), (0, -entries.shape[1] % shard)))
+        return entries.reshape(dp, -1, shard).transpose(1, 0, 2).reshape(-1, width)
+
+    bias_rows = by_shard(grad_sums.reshape(3, heads, head_size)[jnp.array([0, 2])])
+    fc1_rows = by_shard(fc1_bias_sum.reshape(-1, head_size))
     vectors = jnp.concatenate(
         [
-            norm1_sums,
+            gain1,
+            shift1,
             middle_sums[0:1] / scale_a * once,
             middle_sums[1:2] * scale_a * once,
             norm2_sums,
             result_sums[0:1] + result_sums[1:2] * bias_2 * once,
             result_sums[1:2] * scale_m * once,
+            bias_rows,
+            fc1_rows,
         ]
     )
-    small = jnp.concatenate(
-        [
-            vectors.reshape(8, dp, -1).transpose(1, 0, 2).reshape(dp, -1),
-            bias_sums.reshape(2 * heads, dp, -1).transpose(1, 0, 2).reshape(dp, -1),
-            fc1_bias_sum.reshape(-1, dp, head_size // dp).transpose(1, 0, 2).reshape(dp, -1),
-        ],
-        axis=1,
-    )
-    small_share = scatter_sum(small)[0]
-    first_end = 8 * width // dp
-    second_end = first_end + 2 * local // dp
-    vector_share = small_share[:first_end].reshape(8, width // dp)
+    vectors = jnp.pad(vectors, ((0, 128 - vectors.shape[0]), (0, 0)))
+    parts, done = attention_grads(
+        normed1, grads, grad_attn, mixed, qkv_weight, grad_sums, vectors, places[0], steps[0], shard, done
+    )
+    parts = exchange(parts, 1, steps[0])
+
+    def norm1_terms(chunk, done):
+        terms, done = first_norm_terms(chunk, rows, grads, qkv_weight, done)
+        return [terms] + from_peers(terms), done
+
+    output = grad_tokens = None
+    stage = 1
+    norm1_parts = []
+    for chunk in range(chunks):
+        if chunk < chunks - 1:
+            output, done = layer_output(
+                chunk, rows, mlp_parts[chunk], middle, lengths, bias_2, scale_m, output, done
+            )
+        terms, done = norm1_terms(chunk, done)
+        norm1_parts.append(terms)
+        if chunk == 0 and stage < len(steps):
+            parts, done = add_stage(parts, places[stage], steps[stage], done)
+            parts = exchange(parts, strides[stage], steps[stage])
+            stage += 1
+    for chunk in range(chunks):
+        grad_tokens, done = token_grads(
+            chunk, rows, norm1_parts[chunk], grad_middle, tokens, gain1, grad_tokens, done
+        )
+        if chunk == 0:
+            while stage < len(steps):
+                parts, done = add_stage(parts, places[stage], steps[stage], done)
+                parts = exchange(parts, strides[stage], steps[stage])
+                stage += 1
+    (qkv_grad, proj_grad, small), done = last_stage(parts, local, done)
+    output, done = layer_output(
+        chunks - 1, rows, mlp_parts[-1], middle, lengths, bias_2, scale_m, output, done, "last_output"
+    )
+
+    vector_share = small[:8]
     for other in from_peers(vector_share):
         vector_share = vector_share + other
-    vector_share = lax.dynamic_slice_in_dim(
-        vector_share, lax.axis_index("tensor") * (width // dp // tensor), width // dp // tensor, 1
-    )
-    bias_share = small_share[first_end:second_end].reshape(2, heads, -1)
-    fc1_bias_share = small_share[second_end:].reshape(-1, head_size // dp)
+    own = shard // tensor
+    vector_share = lax.dynamic_slice_in_dim(vector_share, lax.axis_index("tensor") * own, own, 1)
+    end = 8 + bias_rows.shape[0]
+    bias_share = small[8:end].reshape(-1)[: 2 * local // dp].reshape(2, heads, -1)
+    fc1_share = small[end : end + fc1_rows.shape[0]].reshape(-1)[: units // dp].reshape(-1, head_size // dp)
 
     return (
         output,
         grad_tokens,
         vector_share[0],
         vector_share[1],
-        jnp.stack([attn_shares[:, i * local : (i + 1) * local] for i in range(3)]),
+        qkv_grad,
         bias_share,
-        attn_shares[:, 3 * local :].T,
+        proj_grad,
         vector_share[3],
         vector_share[2],
         vector_share[4],
         vector_share[5],
         fc_shares[:, :units],
-        fc1_bias_share,
+        fc1_share,
         fc_shares[:, units:].T,
         vector_share[7],
         vector_share[6],

time: 339 us -> 271 us (0.80)
  waiting for transfers between devices: 138 us -> 45.7 us
  Pallas kernels: 130 us -> 165 us
  starting transfers between devices: 27.5 us -> 19.4 us
  other arithmetic: 7.25 us -> 2.72 us
    ppermute x10, waiting for transfers between devices: 101 us -> 14.7 us  [from_peers(): lax.ppermute(array, 'tensor', [(i, (i + step) % size) for i in range(size)])]
    pallas_call x16 -> x20, Pallas kernels: 130 us -> 165 us  [call(): pl.pallas_call(ordered, grid=grid, in_specs=list(in_specs) + [pl.BlockSpe...]
    ppermute x10 -> x6, starting transfers between devices: 15.6 us -> 7.91 us  [the longest x5 7.91 us: exchange(): arrived.append(lax.ppermute(parts[step], 'dp', moves))]
    ppermute x10 -> x6, waiting for transfers between devices: 36.6 us -> 31 us  [the longest x5 31 us: exchange(): arrived.append(lax.ppermute(parts[step], 'dp', moves))]
    convert_element_type x4 -> x0, other arithmetic: 4.98 us -> none  [scatter_sum(): array = wide.astype(BF16)]
    squeeze x4 -> x0, local copies, waits for them, and re-layouts: 4.53 us -> none  [scatter_sum(): sent = lax.dynamic_index_in_dim(view, to, 1, keepdims=False)]
    unnamed x67 -> x57, local copies, waits for them, and re-layouts: 10.5 us -> 11.9 us
  transfers between devices with their start and end apart: 21 -> 17, of which waited for: 8 -> 7; matrix products, arithmetic and copies ran while one was open for 5% -> 4% of each run, Pallas kernels for 29% -> 57%
where the time goes in v2:
time: 271 us
  Pallas kernels  165 us (61%)
  waiting for transfers between devices  45.7 us (17%)
  local copies, waits for them, and re-layouts  23.5 us (9%)
  starting transfers between devices  19.4 us (7%)
  between operations  14.4 us (5%)
  other arithmetic  2.72 us (1%)
    pallas_call x20, Pallas kernels, call(): pl.pallas_call(ordered, grid=grid, in_specs=list(in_specs) + [pl.BlockSpe...  165 us
    ppermute x5, waiting for transfers between devices, exchange(): arrived.append(lax.ppermute(parts[step], 'dp', moves))  31 us
    ppermute x10, waiting for transfers between devices, from_peers(): lax.ppermute(array, 'tensor', [(i, (i + step) % size) for i in range(size)])  14.7 us
    unnamed x57, local copies, waits for them, and re-layouts  11.9 us
    ppermute x10, starting transfers between devices, from_peers(): lax.ppermute(array, 'tensor', [(i, (i + step) % size) for i in range(size)])  11.4 us
    ppermute x5, starting transfers between devices, exchange(): arrived.append(lax.ppermute(parts[step], 'dp', moves))  7.91 us
  transfers between devices with their start and end apart: 17, of which 7 were waited for; matrix products, arithmetic and copies ran while one was open for 4% of the time, Pallas kernels for 57%

profile of v2, /device:TPU:8, one launch (start us, length us, event | category | flops | bytes accessed | tf_op | source)
XLA Modules:
  0.0 270.8 jit_solution(17454198102565437016)
XLA Ops:
  7.2 1.1 constant_dynamic-slice_fusion.1
  8.3 1.6 collective-permute-start
  9.9 1.4 reshape.91.refs_4_
  11.2 7.9 %project.1 = (bf16[1024,512]{1,0:T(8,128)(2,1)}, bf16[1024,512]{1,0:T(8,128)(2,1)}, bf16[1024,512]{1,0:T(8,128)(2,1)}, bf16[1024,1024]{1,0:T(8,128)(2,1)}, f32[8,128]{1,0:T(8,128)}) custom-call(bf16[1024,1024]{1,0:T(8,128)(2,1)} %refs_3_.18, f32[1,1024]{1,0:T(1,128)} %bitcast.51, f32[1,1024]{1,0:T(1,128)} %bitcast.59, bf16[3,1024,512]{2,1,0:T(8,128)(2,1)} %refs_1_.7, ...), custom_call_target="tpu_custom_call" | custom-call | flops 2300000000 | bytes 2300000000 | tf_op jit(solution)/shard_map/project/pallas_call | solution.py:65
  19.2 2.9 %collective-permute-done.refs_4_ = bf16[256,1024]{1,0:T(8,128)(2,1)S(1)} collective-permute-done((bf16[256,1024]{1,0:T(8,128)(2,1)S(1)}, bf16[256,1024]{1,0:T(8,128)(2,1)S(1)}, u32[]{:S(2)}, u32[]{:S(2)}) %collective-permute-start) | collective-permute-done | bytes 524320 | tf_op jit(solution)/shard_map/ppermute | solution.py:829
  22.1 0.8 copy-done.23
  22.9 10.6 %attend_forward.1 = (bf16[1024,512]{1,0:T(8,128)(2,1)}, bf16[256,1024]{1,0:T(8,128)(2,1)}, f32[8,128]{1,0:T(8,128)}) custom-call(bf16[1024,512]{1,0:T(8,128)(2,1)} %get-tuple-element.88.refs_0_, bf16[1024,512]{1,0:T(8,128)(2,1)} %get-tuple-element.89.refs_1_, bf16[1024,512]{1,0:T(8,128)(2,1)} %get-tuple-element.90.refs_2_, s32[1,23]{1,0:T(1,128)} %refs_3_.19, ...), custom_call_target="tpu_custom_call" | custom-call | flops 2300000000 | bytes 2300000000 | tf_op jit(solution)/shard_map/attend_forward/pallas_call | solution.py:65
  33.4 1.3 fusion.2
  34.7 1.6 collective-permute-start.3
  36.8 8.8 %hidden_cotangent.1 = (bf16[1024,1024]{1,0:T(8,128)(2,1)}, bf16[1024,2048]{1,0:T(8,128)(2,1)}, f32[8,128]{1,0:T(8,128)}) custom-call(bf16[1024,1024]{1,0:T(8,128)(2,1)} %refs_4_.5, s32[1,23]{1,0:T(1,128)} %refs_3_.19, f32[1,1024]{1,0:T(1,128)} %bitcast.61, bf16[2048,1024]{1,0:T(8,128)(2,1)} %refs_1_.5, f32[8,128]{1,0:T(8,128)} %get-tuple-element.94.refs_4_), custom_call_target="tpu_custom_call" | custom-call | flops 2300000000 | bytes 2300000000 | tf_op jit(solution)/shard_map/hidden_cotangent/pallas_call | solution.py:65
  45.6 4.1 %collective-permute-done.3.refs_1_ = bf16[512,512]{1,0:T(8,128)(2,1)S(1)} collective-permute-done((bf16[512,512]{1,0:T(8,128)(2,1)S(1)}, bf16[512,512]{1,0:T(8,128)(2,1)S(1)}, u32[]{:S(2)}, u32[]{:S(2)}) %collective-permute-start.3) | collective-permute-done | bytes 524320 | tf_op jit(solution)/shard_map/ppermute | solution.py:829
  49.6 0.8 copy-done.6
  50.6 17.7 %feed_forward.2 = (f32[1024,1024]{1,0:T(8,128)}, bf16[1024,1024]{1,0:T(8,128)(2,1)}, bf16[1024,2048]{1,0:T(8,128)(2,1)}, bf16[1024,2048]{1,0:T(8,128)(2,1)}, f32...) custom-call(bf16[1024,512]{1,0:T(8,128)(2,1)} %get-tuple-element.92.refs_0_.refs_3_, ...), custom_call_target="tpu_custom_call" | custom-call | flops 2300000000 | bytes 2300000000 | tf_op jit(solution)/shard_map/feed_forward/pallas_call | solution.py:65
  68.3 1.6 collective-permute-start.7
  69.8 0.8 copy-done.5
  70.6 17.7 %feed_forward.3 = (f32[1024,1024]{1,0:T(8,128)}, bf16[1024,1024]{1,0:T(8,128)(2,1)}, bf16[1024,2048]{1,0:T(8,128)(2,1)}, bf16[1024,2048]{1,0:T(8,128)(2,1)}, f32...) custom-call(bf16[1024,512]{1,0:T(8,128)(2,1)} %get-tuple-element.92., ...), custom_call_target="tpu_custom_call", output_to_operand_aliasing={{0}: (14, {}), {1}: (15, {}), {2}: (16, {}), {3}: (17, {})} | custom-call | flops 2300000000 | bytes 2300000000 | tf_op jit(solution)/shard_map/feed_forward/pallas_call | solution.py:65
  88.4 0.6 collective-permute-start.6
  89.0 15.6 %fc_grads.1 = (bf16[1024,4096]{1,0:T(8,128)(2,1)}, f32[8,128]{1,0:T(8,128)}) custom-call(bf16[1024,1024]{1,0:T(8,128)(2,1)} %get-tuple-element.103.refs_0_, bf16[1024,1024]{1,0:T(8,128)(2,1)} %get-tuple-element.104.refs_1_, bf16[1024,2048]{1,0:T(8,128)(2,1)} %get-tuple-element.105.refs_2_, bf16[1024,2048]{1,0:T(8,128)(2,1)} %get-tuple-element.102.refs_3_.refs_0_, ...), custom_call_target="tpu_custom_call" | custom-call | flops 2300000000 | bytes 2300000000 | tf_op jit(solution)/shard_map/fc_grads/pallas_call | solution.py:65
  104.7 10.5 %second_projection.1 = (bf16[512,1024]{1,0:T(8,128)(2,1)}, bf16[512,1024]{1,0:T(8,128)(2,1)}, f32[2,1024]{1,0:T(2,128)}, f32[8,128]{1,0:T(8,128)}) custom-call(bf16[1024,2048]{1,0:T(8,128)(2,1)} %get-tuple-element.102.refs_3_.refs_0_, bf16[2048,1024]{1,0:T(8,128)(2,1)} %refs_1_.5, bf16[1024,1024]{1,0:T(8,128)(2,1)} %refs_4_.5, s32[1,23]{1,0:T(1,128)} %refs_3_.19, ...), custom_call_target="tpu_custom_call" | custom-call | flops 2300000000 | bytes 2300000000 | tf_op jit(solution)/shard_map/second_projection/pallas_call | solution.py:65
  116.0 1.5 collective-permute-start.5
  117.5 0.8 multiply_multiply_fusion
  118.3 1.0 copy-done.3
  119.3 6.8 %middle_back.2 = (f32[1024,1024]{1,0:T(8,128)}, bf16[1024,1024]{1,0:T(8,128)(2,1)}, bf16[1024,512]{1,0:T(8,128)(2,1)}, f32[2,1024]{1,0:T(2,128)}, f32[8,128]{1,0:T(8,128)}) custom-call(bf16[512,1024]{1,0:T(8,128)(2,1)} %get-tuple-element.113.refs_0_, bf16[512,1024]{1,0:T(8,128)(2,1)} %copy-done.3, f32[1024,1024]{1,0:T(8,128)} %get-tuple-element.109.refs_2_, ...), custom_call_target="tpu_custom_call" | custom-call | flops 2300000000 | bytes 2300000000 | tf_op jit(solution)/shard_map/middle_back/pallas_call | solution.py:65
  126.1 1.0 copy-done.4
  127.1 6.4 %middle_back.3 = (f32[1024,1024]{1,0:T(8,128)}, bf16[1024,1024]{1,0:T(8,128)(2,1)}, bf16[1024,512]{1,0:T(8,128)(2,1)}, f32[2,1024]{1,0:T(2,128)}, f32[8,128]{1,0:T(8,128)}) custom-call(bf16[512,1024]{1,0:T(8,128)(2,1)} %get-tuple-element.112.refs_0_, bf16[512,1024]{1,0:T(8,128)(2,1)} %copy-done.4, ...), custom_call_target="tpu_custom_call", output_to_operand_aliasing={{0}: (9, {}), {1}: (10, {}), {2}: (11, {})} | custom-call | flops 2300000000 | bytes 2300000000 | tf_op jit(solution)/shard_map/middle_back/pallas_call | solution.py:65
  133.6 17.1 %attend_backward.1 = (bf16[1024,1536]{1,0:T(8,128)(2,1)}, f32[3,512]{1,0:T(4,128)}, f32[8,128]{1,0:T(8,128)}) custom-call(bf16[1024,512]{1,0:T(8,128)(2,1)} %get-tuple-element.88.refs_0_, bf16[1024,512]{1,0:T(8,128)(2,1)} %get-tuple-element.89.refs_1_, bf16[1024,512]{1,0:T(8,128)(2,1)} %get-tuple-element.90.refs_2_, ...), custom_call_target="tpu_custom_call" | custom-call | flops 2300000000 | bytes 2300000000 | tf_op jit(solution)/shard_map/attend_backward/pallas_call | solution.py:65
  150.8 0.8 reshape.100
  151.5 0.5 gather_fusion
  152.8 0.8 pad.4.refs_6_
  153.6 10.8 %attention_grads.1 = (bf16[8,64,2176]{2,1,0:T(8,128)(2,1)}, bf16[8,64,2176]{2,1,0:T(8,128)(2,1)}, f32[8,128]{1,0:T(8,128)}) custom-call(bf16[1024,1024]{1,0:T(8,128)(2,1)} %get-tuple-element.111.refs_0_, bf16[1024,1536]{1,0:T(8,128)(2,1)} %get-tuple-element.121.refs_1_.refs_0_, bf16[1024,1024]{1,0:T(8,128)(2,1)} %get-tuple-element.122.refs_2_, ...), custom_call_target="tpu_custom_call" | custom-call | flops 2300000000 | bytes 2300000000 | tf_op jit(solution)/shard_map/attention_grads/pallas_call | solution.py:65
  164.4 1.0 copy-done.22
  165.4 3.3 %layer_output.1 = (bf16[1024,1024]{1,0:T(8,128)(2,1)}, f32[8,128]{1,0:T(8,128)}) custom-call(bf16[512,1024]{1,0:T(8,128)(2,1)} %get-tuple-element.110.refs_0_, bf16[512,1024]{1,0:T(8,128)(2,1)} %copy-done.22, f32[1024,1024]{1,0:T(8,128)} %get-tuple-element.109.refs_2_, s32[1,23]{1,0:T(1,128)} %refs_3_.19, f32[1,1024]{1,0:T(1,128)} %bitcast.65, ...), custom_call_target="tpu_custom_call" | custom-call | flops 2300000000 | bytes 2300000000 | tf_op jit(solution)/shard_map/layer_output/pallas_call | solution.py:65
  168.7 5.0 %first_norm_terms.2 = (bf16[512,1024]{1,0:T(8,128)(2,1)}, f32[8,128]{1,0:T(8,128)}) custom-call(bf16[1024,1536]{1,0:T(8,128)(2,1)} %get-tuple-element.121.refs_1_.refs_0_, bf16[3,1024,512]{2,1,0:T(8,128)(2,1)} %refs_1_.7, f32[8,128]{1,0:T(8,128)} %get-tuple-element.136.refs_2_), custom_call_target="tpu_custom_call" | custom-call | flops 23000000512 | bytes 2300000000 | tf_op jit(solution)/shard_map/first_norm_terms/pallas_call | solution.py:65
  173.7 0.8 collective-permute-start.10
  174.5 1.4 copy-done.19
  175.9 4.7 %add_stage.2 = (bf16[4,64,2176]{2,1,0:T(8,128)(2,1)}, bf16[4,64,2176]{2,1,0:T(8,128)(2,1)}, f32[8,128]{1,0:T(8,128)}) custom-call(bf16[8,64,2176]{2,1,0:T(8,128)(2,1)} %get-tuple-element.134.refs_0_, bf16[8,64,2176]{2,1,0:T(8,128)(2,1)} %copy-done.19, s32[1]{0:T(128)} %bitcast.14.refs_2_, f32[8,128]{1,0:T(8,128)} %get-tuple-element.137.refs_3_), custom_call_target="tpu_custom_call" | custom-call | flops 2300000000 | bytes 2300000000 | tf_op jit(solution)/shard_map/add_stage/pallas_call | solution.py:65
  180.6 4.6 %collective-permute-start.9 = (bf16[4,64,2176]{2,1,0:T(8,128)(2,1)}, bf16[4,64,2176]{2,1,0:T(8,128)(2,1)S(1)}, u32[]{:S(2)}, u32[]{:S(2)}) collective-permute-start(bf16[4,64,2176]{2,1,0:T(8,128)(2,1)} %get-tuple-element.139), channel_id=1, source_target_pairs={{0,4},{2,6},{4,0},{6,2},{8,12},{10,14},{12,8},{14,10},{16,20},{18,... | collective-permute-start | bytes 3342344 | tf_op jit(solution)/shard_map/ppermute | solution.py:858
  185.2 5.1 %first_norm_terms.3 = (bf16[512,1024]{1,0:T(8,128)(2,1)}, f32[8,128]{1,0:T(8,128)}) custom-call(bf16[1024,1536]{1,0:T(8,128)(2,1)} %get-tuple-element.121.refs_1_.refs_0_, bf16[3,1024,512]{2,1,0:T(8,128)(2,1)} %refs_1_.7, f32[8,128]{1,0:T(8,128)} %get-tuple-element.142.refs_2_), custom_call_target="tpu_custom_call" | custom-call | flops 23000000512 | bytes 2300000000 | tf_op jit(solution)/shard_map/first_norm_terms/pallas_call | solution.py:65
  190.3 1.9 collective-permute-start.14
  192.3 7.7 %collective-permute-done.10.refs_1_ = bf16[512,1024]{1,0:T(8,128)(2,1)} collective-permute-done((bf16[512,1024]{1,0:T(8,128)(2,1)}, bf16[512,1024]{1,0:T(8,128)(2,1)}, u32[]{:S(2)}, u32[]{:S(2)}) %collective-permute-start.10) | collective-permute-done | bytes 1048608 | tf_op jit(solution)/shard_map/ppermute | solution.py:829
  200.0 4.1 %token_grads.2 = (bf16[1024,1024]{1,0:T(8,128)(2,1)}, f32[8,128]{1,0:T(8,128)}) custom-call(bf16[512,1024]{1,0:T(8,128)(2,1)} %get-tuple-element.140.refs_0_, bf16[512,1024]{1,0:T(8,128)(2,1)} %collective-permute-done.10.refs_1_, f32[1024,1024]{1,0:T(8,128)} %get-tuple-element.141.refs_2_, bf16[1024,1024]{1,0:T(8,128)(2,1)} %refs_3_.18, f32[1,1024]{1,0:T(1,128)} %bitcast.52, ...), custom_call_target="tpu_custom_call" | custom-call | flops 2300000000 | bytes 2300000000 | tf_op jit(solution)/shard_map/token_grads/pallas_call | solution.py:65
  204.2 11.9 %collective-permute-done.9.refs_1_ = bf16[4,64,2176]{2,1,0:T(8,128)(2,1)S(1)} collective-permute-done((bf16[4,64,2176]{2,1,0:T(8,128)(2,1)}, bf16[4,64,2176]{2,1,0:T(8,128)(2,1)S(1)}, u32[]{:S(2)}, u32[]{:S(2)}) %collective-permute-start.9) | collective-permute-done | bytes 1114144 | tf_op jit(solution)/shard_map/ppermute | solution.py:858
  216.1 1.0 copy-done.20
  217.2 3.1 %add_stage.3 = (bf16[1,64,2176]{2,1,0:T(8,128)(2,1)}, bf16[1,64,2176]{2,1,0:T(8,128)(2,1)}, bf16[1,64,2176]{2,1,0:T(8,128)(2,1)}, bf16[1,64,2176]{2,1,0:T(8,128)(2,1)}, f32[8,128]{1,0:T(8,128)}) custom-call(bf16[4,64,2176]{2,1,0:T(8,128)(2,1)} %get-tuple-element.138.refs_0_, bf16[4,64,2176]{2,1,0:T(8,128)(2,1)} %copy-done.20, s32[1]{0:T(128)} %bitcast.15.refs_2_, ...), custom_call_target="tpu_custom_call" | custom-call | flops 2300000000 | bytes 2300000000 | tf_op jit(solution)/shard_map/add_stage/pallas_call | solution.py:65
  220.3 3.3 %collective-permute-start.12 = (bf16[1,64,2176]{2,1,0:T(8,128)(2,1)}, bf16[1,64,2176]{2,1,0:T(8,128)(2,1)S(1)}, u32[]{:S(2)}, u32[]{:S(2)}) collective-permute-start(bf16[1,64,2176]{2,1,0:T(8,128)(2,1)} %get-tuple-element.147), channel_id=1, source_target_pairs={{0,16},{2,18},{4,20},{6,22},{8,24},{10,26},{12,28},{14,30},{16,0},... | collective-permute-start | bytes 835592 | tf_op jit(solution)/shard_map/ppermute | solution.py:858
  223.6 1.0 copy-done.2
  224.7 4.1 %token_grads.3 = (bf16[1024,1024]{1,0:T(8,128)(2,1)}, f32[8,128]{1,0:T(8,128)}) custom-call(bf16[512,1024]{1,0:T(8,128)(2,1)} %get-tuple-element.149.refs_0_, bf16[512,1024]{1,0:T(8,128)(2,1)} %copy-done.2, f32[1024,1024]{1,0:T(8,128)} %get-tuple-element.141.refs_2_, bf16[1024,1024]{1,0:T(8,128)(2,1)} %refs_3_.18, ...), custom_call_target="tpu_custom_call", output_to_operand_aliasing={{0}: (5, {})} | custom-call | flops 2300000000 | bytes 2300000000 | tf_op jit(solution)/shard_map/token_grads/pallas_call | solution.py:65
  228.8 1.3 collective-permute-done.11.refs_1_
  230.1 14.6 %collective-permute-done.12.refs_2_ = bf16[1,64,2176]{2,1,0:T(8,128)(2,1)S(1)} collective-permute-done((bf16[1,64,2176]{2,1,0:T(8,128)(2,1)}, bf16[1,64,2176]{2,1,0:T(8,128)(2,1)S(1)}, u32[]{:S(2)}, u32[]{:S(2)}) %collective-permute-start.12) | collective-permute-done | bytes 278560 | tf_op jit(solution)/shard_map/ppermute | solution.py:858
  244.7 3.2 %collective-permute-done.13.refs_3_ = bf16[1,64,2176]{2,1,0:T(8,128)(2,1)S(1)} collective-permute-done((bf16[1,64,2176]{2,1,0:T(8,128)(2,1)}, bf16[1,64,2176]{2,1,0:T(8,128)(2,1)S(1)}, u32[]{:S(2)}, u32[]{:S(2)}) %collective-permute-start.13) | collective-permute-done | bytes 278560 | tf_op jit(solution)/shard_map/ppermute | solution.py:858
  247.9 0.7 copy-done.26
  248.5 2.2 last_stage.1
  250.8 0.7 slice.64
  251.5 1.3 collective-permute-start.15
  252.8 3.3 %last_output.1 = (bf16[1024,1024]{1,0:T(8,128)(2,1)}, f32[8,128]{1,0:T(8,128)}) custom-call(bf16[512,1024]{1,0:T(8,128)(2,1)} %get-tuple-element.108.refs_0_, bf16[512,1024]{1,0:T(8,128)(2,1)} %collective-permute-done.4.refs_1_, f32[1024,1024]{1,0:T(8,128)} %get-tuple-element.109.refs_2_, s32[1,23]{1,0:T(1,128)} %refs_3_.19, ...), custom_call_target="tpu_custom_call", output_to_operand_aliasing={{0}: (6, {})} | custom-call | flops 46000001024 | bytes 2300000000 | tf_op jit(solution)/shard_map/last_output/pallas_call | solution.py:65
  256.1 0.7 slice_reduce_fusion
  256.8 0.7 slice.73
  257.5 0.8 copy.57
  258.4 0.7 copy.58
  259.1 0.7 copy.56
  259.8 0.7 slice_add_fusion
  261.1 1.2 convert_element_type.5
  262.3 0.8 slice_bitcast_fusion
  263.1 0.8 slice.81
  (81 shorter events, 3.2 us)
Async XLA Ops:
  7.2 253.9 %reduce-scatter.2.cloned.1.call-start = ((), (), s32[]{:S(2)}) async-start(), calls=%async_computation.1 | async-start | bytes 8912896 | tf_op jit(solution)/shard_map/reduce_scatter | solution.py:952
  8.3 13.7 %collective-permute-start = (bf16[256,1024]{1,0:T(8,128)(2,1)S(1)}, bf16[256,1024]{1,0:T(8,128)(2,1)S(1)}, u32[]{:S(2)}, u32[]{:S(2)}) collective-permute-start(bf16[256,1024]{1,0:T(8,128)(2,1)S(1)} %constant_dynamic-slice_fusion.1), channel_id=1, source_target_pairs={{0,1},{1,0},{2,3},{3,2},{4,5},{5,4},{6,7},{7,6},{8,9},{9,8},{10,11... | collective-permute-start | bytes 1572872 | tf_op jit(solution)/shard_map/ppermute | solution.py:829
  22.1 0.8 copy-start.23
  34.7 14.9 %collective-permute-start.3 = (bf16[512,512]{1,0:T(8,128)(2,1)S(1)}, bf16[512,512]{1,0:T(8,128)(2,1)S(1)}, u32[]{:S(2)}, u32[]{:S(2)}) collective-permute-start(bf16[512,512]{1,0:T(8,128)(2,1)S(1)} %get-tuple-element.208), channel_id=1, source_target_pairs={{0,1},{1,0},{2,3},{3,2},{4,5},{5,4},{6,7},{7,6},{8,9},{9,8},{10,11... | collective-permute-start | bytes 1572872 | tf_op jit(solution)/shard_map/ppermute | solution.py:829
  36.3 13.4 %collective-permute-start.2 = (bf16[256,1024]{1,0:T(8,128)(2,1)}, bf16[256,1024]{1,0:T(8,128)(2,1)S(1)}, u32[]{:S(2)}, u32[]{:S(2)}) collective-permute-start(bf16[256,1024]{1,0:T(8,128)(2,1)} %get-tuple-element.93.refs_3_), channel_id=1, source_target_pairs={{0,2},{2,0},{4,6},{6,4},{8,10},{10,8},{12,14},{14,12},{16,18},{18,... | collective-permute-start | bytes 1572872 | tf_op jit(solution)/shard_map/ppermute | solution.py:835
  36.3 33.6 %collective-permute-start.1 = (bf16[512,512]{1,0:T(8,128)(2,1)S(1)}, bf16[512,512]{1,0:T(8,128)(2,1)S(1)}, u32[]{:S(2)}, u32[]{:S(2)}) collective-permute-start(bf16[512,512]{1,0:T(8,128)(2,1)S(1)} %get-tuple-element.209), channel_id=1, source_target_pairs={{0,1},{1,0},{2,3},{3,2},{4,5},{5,4},{6,7},{7,6},{8,9},{9,8},{10,11... | collective-permute-start | bytes 1572872 | tf_op jit(solution)/shard_map/ppermute | solution.py:829
  49.6 0.8 copy-start.6
  49.6 1.0 copy-start
  68.3 50.0 %collective-permute-start.7 = (bf16[512,1024]{1,0:T(8,128)(2,1)}, bf16[512,1024]{1,0:T(8,128)(2,1)S(1)}, u32[]{:S(2)}, u32[]{:S(2)}) collective-permute-start(bf16[512,1024]{1,0:T(8,128)(2,1)} %get-tuple-element.113.refs_0_), channel_id=1, source_target_pairs={{0,1},{1,0},{2,3},{3,2},{4,5},{5,4},{6,7},{7,6},{8,9},{9,8},{10,11... | collective-permute-start | bytes 3145736 | tf_op jit(solution)/shard_map/ppermute | solution.py:829
  69.8 0.8 copy-start.5
  88.4 37.7 %collective-permute-start.6 = (bf16[512,1024]{1,0:T(8,128)(2,1)}, bf16[512,1024]{1,0:T(8,128)(2,1)S(1)}, u32[]{:S(2)}, u32[]{:S(2)}) collective-permute-start(bf16[512,1024]{1,0:T(8,128)(2,1)} %get-tuple-element.112.refs_0_), channel_id=1, source_target_pairs={{0,1},{1,0},{2,3},{3,2},{4,5},{5,4},{6,7},{7,6},{8,9},{9,8},{10,11... | collective-permute-start | bytes 3145736 | tf_op jit(solution)/shard_map/ppermute | solution.py:829
  104.7 10.6 %copy-start.11 = (f32[1,2048]{1,0:T(1,128)S(1)}, f32[1,2048]{1,0:T(1,128)}, u32[]{:S(2)}) copy-start(f32[1,2048]{1,0:T(1,128)} %get-tuple-element.129) | copy-start | bytes 24580
  104.7 10.6 %copy-start.13 = (f32[1,2048]{1,0:T(1,128)S(1)}, f32[1,2048]{1,0:T(1,128)}, u32[]{:S(2)}) copy-start(f32[1,2048]{1,0:T(1,128)} %get-tuple-element.130) | copy-start | bytes 24580
  104.7 12.8 %copy-start.10 = (f32[2,1024]{1,0:T(2,128)S(1)}, f32[2,1024]{1,0:T(2,128)}, u32[]{:S(2)}) copy-start(f32[2,1024]{1,0:T(2,128)} %get-tuple-element.126) | copy-start | bytes 24580
  104.7 12.8 %copy-start.12 = (f32[2,1024]{1,0:T(2,128)S(1)}, f32[2,1024]{1,0:T(2,128)}, u32[]{:S(2)}) copy-start(f32[2,1024]{1,0:T(2,128)} %get-tuple-element.127) | copy-start | bytes 24580
  104.7 12.8 %copy-start.17 = (f32[1024]{0:T(1024)S(1)}, f32[1024]{0:T(1024)}, u32[]{:S(2)}) copy-start(f32[1024]{0:T(1024)} %param.33) | copy-start | bytes 12292
  104.7 12.8 %copy-start.18 = (f32[1024]{0:T(1024)S(1)}, f32[1024]{0:T(1024)}, u32[]{:S(2)}) copy-start(f32[1024]{0:T(1024)} %param.32) | copy-start | bytes 12292
  116.0 48.5 %collective-permute-start.5 = (bf16[512,1024]{1,0:T(8,128)(2,1)}, bf16[512,1024]{1,0:T(8,128)(2,1)S(1)}, u32[]{:S(2)}, u32[]{:S(2)}) collective-permute-start(bf16[512,1024]{1,0:T(8,128)(2,1)} %get-tuple-element.110.refs_0_), channel_id=1, source_target_pairs={{0,1},{1,0},{2,3},{3,2},{4,5},{5,4},{6,7},{7,6},{8,9},{9,8},{10,11... | collective-permute-start | bytes 3145736 | tf_op jit(solution)/shard_map/ppermute | solution.py:829
  118.3 1.0 copy-start.3
  126.1 1.0 copy-start.4
  133.6 19.0 %copy-start.14 = (f32[2,1024]{1,0:T(2,128)S(1)}, f32[2,1024]{1,0:T(2,128)}, u32[]{:S(2)}) copy-start(f32[2,1024]{1,0:T(2,128)} %get-tuple-element.124) | copy-start | bytes 24580
  133.6 19.0 %copy-start.15 = (f32[2,1024]{1,0:T(2,128)S(1)}, f32[2,1024]{1,0:T(2,128)}, u32[]{:S(2)}) copy-start(f32[2,1024]{1,0:T(2,128)} %get-tuple-element.125) | copy-start | bytes 24580
  133.6 19.0 %copy-start.8 = (f32[1024]{0:T(1024)S(1)}, f32[1024]{0:T(1024)}, u32[]{:S(2)}) copy-start(f32[1024]{0:T(1024)} %param.26) | copy-start | bytes 12292
  133.6 19.1 %copy-start.9 = (f32[1024]{0:T(1024)S(1)}, f32[1024]{0:T(1024)}, u32[]{:S(2)}) copy-start(f32[1024]{0:T(1024)} %param.20) | copy-start | bytes 12292
  133.6 19.1 %copy-start.16 = (f32[1024]{0:T(1024)S(1)}, f32[1024]{0:T(1024)}, u32[]{:S(2)}) copy-start(f32[1024]{0:T(1024)} %param.21) | copy-start | bytes 12292
  164.4 10.1 %collective-permute-start.8 = (bf16[8,64,2176]{2,1,0:T(8,128)(2,1)}, bf16[8,64,2176]{2,1,0:T(8,128)(2,1)S(1)}, u32[]{:S(2)}, u32[]{:S(2)}) collective-permute-start(bf16[8,64,2176]{2,1,0:T(8,128)(2,1)} %get-tuple-element.135), channel_id=1, source_target_pairs={{0,2},{2,0},{4,6},{6,4},{8,10},{10,8},{12,14},{14,12},{16,18},{18,... | collective-permute-start | bytes 6684680 | tf_op jit(solution)/shard_map/ppermute | solution.py:858
  164.4 1.0 copy-start.22
  173.7 26.3 %collective-permute-start.10 = (bf16[512,1024]{1,0:T(8,128)(2,1)}, bf16[512,1024]{1,0:T(8,128)(2,1)}, u32[]{:S(2)}, u32[]{:S(2)}) collective-permute-start(bf16[512,1024]{1,0:T(8,128)(2,1)} %get-tuple-element.140.refs_0_), channel_id=1, source_target_pairs={{0,1},{1,0},{2,3},{3,2},{4,5},{5,4},{6,7},{7,6},{8,9},{9,8},{10,11... | collective-permute-start | bytes 3145736 | tf_op jit(solution)/shard_map/ppermute | solution.py:829
  174.5 1.4 copy-start.19
  180.6 35.5 %collective-permute-start.9 = (bf16[4,64,2176]{2,1,0:T(8,128)(2,1)}, bf16[4,64,2176]{2,1,0:T(8,128)(2,1)S(1)}, u32[]{:S(2)}, u32[]{:S(2)}) collective-permute-start(bf16[4,64,2176]{2,1,0:T(8,128)(2,1)} %get-tuple-element.139), channel_id=1, source_target_pairs={{0,4},{2,6},{4,0},{6,2},{8,12},{10,14},{12,8},{14,10},{16,20},{18,... | collective-permute-start | bytes 3342344 | tf_op jit(solution)/shard_map/ppermute | solution.py:858
  185.2 6.9 %copy-start.21 = (bf16[512,1024]{1,0:T(8,128)(2,1)S(1)}, bf16[512,1024]{1,0:T(8,128)(2,1)}, u32[]{:S(2)}) copy-start(bf16[512,1024]{1,0:T(8,128)(2,1)} %get-tuple-element.108.refs_0_) | copy-start | bytes 3145732
  190.3 33.3 %collective-permute-start.14 = (bf16[512,1024]{1,0:T(8,128)(2,1)}, bf16[512,1024]{1,0:T(8,128)(2,1)S(1)}, u32[]{:S(2)}, u32[]{:S(2)}) collective-permute-start(bf16[512,1024]{1,0:T(8,128)(2,1)} %get-tuple-element.149.refs_0_), channel_id=1, source_target_pairs={{0,1},{1,0},{2,3},{3,2},{4,5},{5,4},{6,7},{7,6},{8,9},{9,8},{10,11... | collective-permute-start | bytes 3145736 | tf_op jit(solution)/shard_map/ppermute | solution.py:829
  192.2 60.6 %collective-permute-start.4 = (bf16[512,1024]{1,0:T(8,128)(2,1)S(1)}, bf16[512,1024]{1,0:T(8,128)(2,1)}, u32[]{:S(2)}, u32[]{:S(2)}) collective-permute-start(bf16[512,1024]{1,0:T(8,128)(2,1)S(1)} %copy-done.21), channel_id=1, source_target_pairs={{0,1},{1,0},{2,3},{3,2},{4,5},{5,4},{6,7},{7,6},{8,9},{9,8},{10,11... | collective-permute-start | bytes 3145736 | tf_op jit(solution)/shard_map/ppermute | solution.py:829
  216.1 1.0 copy-start.20
  220.3 9.8 %collective-permute-start.11 = (bf16[1,64,2176]{2,1,0:T(8,128)(2,1)}, bf16[1,64,2176]{2,1,0:T(8,128)(2,1)S(1)}, u32[]{:S(2)}, u32[]{:S(2)}) collective-permute-start(bf16[1,64,2176]{2,1,0:T(8,128)(2,1)} %get-tuple-element.146), channel_id=1, source_target_pairs={{0,8},{2,10},{4,12},{6,14},{8,16},{10,18},{12,20},{14,22},{16,24},... | collective-permute-start | bytes 835592 | tf_op jit(solution)/shard_map/ppermute | solution.py:858
  220.3 24.4 %collective-permute-start.12 = (bf16[1,64,2176]{2,1,0:T(8,128)(2,1)}, bf16[1,64,2176]{2,1,0:T(8,128)(2,1)S(1)}, u32[]{:S(2)}, u32[]{:S(2)}) collective-permute-start(bf16[1,64,2176]{2,1,0:T(8,128)(2,1)} %get-tuple-element.147), channel_id=1, source_target_pairs={{0,16},{2,18},{4,20},{6,22},{8,24},{10,26},{12,28},{14,30},{16,0},... | collective-permute-start | bytes 835592 | tf_op jit(solution)/shard_map/ppermute | solution.py:858
  223.6 24.2 %collective-permute-start.13 = (bf16[1,64,2176]{2,1,0:T(8,128)(2,1)}, bf16[1,64,2176]{2,1,0:T(8,128)(2,1)S(1)}, u32[]{:S(2)}, u32[]{:S(2)}) collective-permute-start(bf16[1,64,2176]{2,1,0:T(8,128)(2,1)} %get-tuple-element.148), channel_id=1, source_target_pairs={{0,24},{2,26},{4,28},{6,30},{8,0},{10,2},{12,4},{14,6},{16,8},{18,... | collective-permute-start | bytes 835592 | tf_op jit(solution)/shard_map/ppermute | solution.py:858
  223.6 1.0 copy-start.2
  230.1 17.8 %copy-start.24 = (bf16[1,64,2176]{2,1,0:T(8,128)(2,1)}, bf16[1,64,2176]{2,1,0:T(8,128)(2,1)S(1)}, u32[]{:S(2)}) copy-start(bf16[1,64,2176]{2,1,0:T(8,128)(2,1)S(1)} %collective-permute-done.11.refs_1_) | copy-start | bytes 835588
  244.7 3.2 %copy-start.25 = (bf16[1,64,2176]{2,1,0:T(8,128)(2,1)}, bf16[1,64,2176]{2,1,0:T(8,128)(2,1)S(1)}, u32[]{:S(2)}) copy-start(bf16[1,64,2176]{2,1,0:T(8,128)(2,1)S(1)} %collective-permute-done.12.refs_2_) | copy-start | bytes 835588
  247.9 0.7 copy-start.26
  251.5 8.3 %collective-permute-start.15 = (f32[8,64]{1,0:T(8,128)S(1)}, f32[8,64]{1,0:T(8,128)S(1)}, u32[]{:S(2)}, u32[]{:S(2)}) collective-permute-start(f32[8,64]{1,0:T(8,128)S(1)} %slice.64), channel_id=1, source_target_pairs={{0,1},{1,0},{2,3},{3,2},{4,5},{5,4},{6,7},{7,6},{8,9},{9,8},{10,11... | collective-permute-start | bytes 6152 | tf_op jit(solution)/shard_map/ppermute | solution.py:829
  252.8 4.7 %copy-start.7 = (f32[512,64]{1,0:T(8,128)S(1)}, f32[512,64]{1,0:T(8,128)}, u32[]{:S(2)}) copy-start(f32[512,64]{1,0:T(8,128)} %get-tuple-element.198) | copy-start | bytes 393220
  261.1 2.0 copy-start.1
Sparse Core Ops, SparseCore 0:
  104.8 109.5 reduce-scatter.1

commit v3 on v2

v3 whole, which is shorter than its diff:
```python
from functools import partial

import jax
import jax.numpy as jnp
from jax import lax
from jax.experimental import pallas as pl
from jax.experimental.pallas import tpu as pltpu
from jax.sharding import PartitionSpec as P

EPS = 1e-06
NEGATIVE = -1e30
GLOBAL_LEN = 197
LOCAL_LEN = 37
GROUP = GLOBAL_LEN // LOCAL_LEN
WINDOW = 224
BF16 = jnp.bfloat16
F32 = jnp.float32
MIB = 1 << 20
VMEM_MIB = 16
SPARE = 6
LIMITS = {
    "attend_forward": 14,
    "hidden_cotangent": 6,
    "feed_forward": 15,
    "weight_grads": 17,
    "second_projection": 18,
    "middle_back": 13,
    "attend_backward": 11,
    "attention_grads": 11,
    "layer_output": 13,
    "first_norm_terms": 5,
    "add_stage": 4,
    "token_grads": 9,
    "last_stage": 4,
    "last_far_stage": 6,
    "add_far_stage": 16,
}
COST = 2300000000
COSTS = {"middle_back_1": 46000000000, "add_far_stage_1": 23000000000}


def dot_nn(a, b):
    return lax.dot_general(a, b, (((1,), (0,)), ((), ())), preferred_element_type=F32)


def dot_nt(a, b):
    return lax.dot_general(a, b, (((1,), (1,)), ((), ())), preferred_element_type=F32)


def dot_tn(a, b):
    return lax.dot_general(a, b, (((0,), (0,)), ((), ())), preferred_element_type=F32)


def norm_parts(values):
    average = jnp.mean(values, axis=-1, keepdims=True)
    centered = values - average
    inverse = lax.rsqrt(jnp.mean(centered * centered, axis=-1, keepdims=True) + EPS)
    return centered * inverse, inverse


def norm_back(grad_norm, scaled, inverse, gain):
    grad_hat = grad_norm * gain
    first_mean = jnp.mean(grad_hat, axis=-1, keepdims=True)
    second_mean = jnp.mean(grad_hat * scaled, axis=-1, keepdims=True)
    return inverse * (grad_hat - first_mean - scaled * second_mean)


def col_sum(values):
    return jnp.sum(values, axis=0, keepdims=True)


def call(kernel, name, in_specs, out_specs, out_shape, args, after=None, scratch=(), vmem=VMEM_MIB, alias=None, bring=(), late=False):
    single = not isinstance(out_shape, list)
    if single:
        out_specs, out_shape = [out_specs], [out_shape]
    n_in, n_out, n_bring = len(args), len(out_shape), len(bring)
    n_after = 0 if after is None else 1
    args = [
        pltpu.with_memory_space_constraint(arg, pltpu.VMEM if spec is VMEM else pltpu.HBM)
        if spec is VMEM or spec is ANY
        else arg
        for arg, spec in zip(args, in_specs)
    ]
    args += [pltpu.with_memory_space_constraint(arg, pltpu.HBM) for arg in bring]
    out_shape = [
        pltpu.VMEM(o.shape, o.dtype) if spec is VMEM else o for o, spec in zip(out_shape, out_specs)
    ]

    def ordered(*refs):
        ins, refs = refs[:n_in], refs[n_in:]
        bring_hbm, refs = refs[:n_bring], refs[n_bring + n_after :]
        outs, refs = refs[:n_out], refs[n_out:]
        bring_refs, done, refs = refs[:n_bring], refs[n_bring], refs[n_bring + 1 :]
        done[...] = jnp.zeros_like(done)
        loads = []
        if n_bring:
            refs, sems = refs[:-1], refs[-1]

        def begin():
            for i in range(n_bring):
                loads.append(pltpu.make_async_copy(bring_hbm[i], bring_refs[i], sems.at[i]))
                loads[-1].start()

        if late:
            kernel(begin, *ins, *outs, *refs)
        else:
            begin()
            kernel(*ins, *outs, *refs)
        for load in loads:
            load.wait()

    out = pl.pallas_call(
        ordered,
        in_specs=list(in_specs) + [ANY] * (n_bring + n_after),
        out_specs=list(out_specs) + [VMEM] * (n_bring + 1),
        out_shape=list(out_shape) + [pltpu.VMEM(a.shape, a.dtype) for a in bring] + [pltpu.VMEM((8, 128), F32)],
        scratch_shapes=list(scratch) + ([pltpu.SemaphoreType.DMA((n_bring,))] if n_bring else []),
        input_output_aliases=alias or {},
        compiler_params=pltpu.CompilerParams(vmem_limit_bytes=(LIMITS.get(name.rstrip("_0123456789"), vmem) + SPARE) * MIB),
        cost_estimate=pl.CostEstimate(flops=COSTS.get(name, COST), bytes_accessed=COST, transcendentals=0),
        name=name,
    )(*args, *([after] if n_after else []))
    return (out[0] if single and not n_bring else out[:-1]), out[-1]


class Copies:
    def __init__(self, sems):
        self.sems = sems
        self.used = 0

    def start(self, source, target):
        copy = pltpu.make_async_copy(source, target, self.sems.at[self.used])
        self.used += 1
        copy.start()
        return copy


def shape(dims, dtype):
    return jax.ShapeDtypeStruct(dims, dtype)


SMEM = pl.BlockSpec(memory_space=pltpu.SMEM)
VMEM = pl.BlockSpec(memory_space=pltpu.VMEM)
ANY = pl.BlockSpec(memory_space=pl.ANY)
COPIED = pl.BlockSpec(memory_space=pltpu.VMEM)

GAIN1, SHIFT1, GAIN2, SHIFT2, PROJ_BIAS, SCALE_ATTN, FC2_BIAS, SCALE_MLP = range(8)


def row_total(lengths_ref):
    total = jnp.int32(0)
    for slot in range(lengths_ref.shape[1]):
        total = total + lengths_ref[0, slot]
    return total


def valid_rows(lengths_ref, first, rows):
    places = lax.broadcasted_iota(jnp.int32, (rows, 1), 0) + first
    return (places < row_total(lengths_ref)).astype(F32)


def item_counts(lengths_ref):
    globals_ = jnp.int32(0)
    locals_ = jnp.int32(0)
    for slot in range(lengths_ref.shape[1]):
        value = lengths_ref[0, slot]
        globals_ = globals_ + jnp.where(value == GLOBAL_LEN, 1, 0)
        locals_ = locals_ + jnp.where(value == LOCAL_LEN, 1, 0)
    return globals_, locals_


def item_place(item, globals_, locals_, count):
    is_global = item < globals_
    group = item - globals_
    start = jnp.where(
        is_global, item * GLOBAL_LEN, globals_ * GLOBAL_LEN + group * (GROUP * LOCAL_LEN)
    )
    length = jnp.where(
        is_global, GLOBAL_LEN, jnp.minimum(locals_ - group * GROUP, GROUP) * LOCAL_LEN
    )
    crop = jnp.where(is_global, GLOBAL_LEN, LOCAL_LEN)
    first = jnp.minimum((start // 16) * 16, count - WINDOW)
    return pl.multiple_of(first, 16), start - first, length, crop


def crop_of(places, offset, length, crop, outside):
    inside = (places >= offset) & (places < offset + length)
    index = places - offset
    label = jnp.zeros_like(places)
    for step in range(1, GROUP):
        label = label + jnp.where(index >= step * crop, 1, 0)
    return jnp.where(inside, label, outside)


def item_total(globals_, locals_):
    return globals_ + (locals_ + GROUP - 1) // GROUP


def attend_forward(tokens, lengths, vectors, weight, qv_bias, scale, chunks, later):
    count, width = tokens.shape
    local = weight.shape[2]
    head = 64
    pair = 2 * head
    block = 256
    blocks = count // block
    rows = count // chunks
    n_vec, n_later = len(vectors), len(later)

    def kernel(x_hbm, w_hbm, *refs):
        later_hbm, refs = refs[:n_later], refs[n_later:]
        vec_hbm, refs = refs[:n_vec], refs[n_vec:]
        qv_hbm, lengths_ref, refs = refs[0], refs[1], refs[2:]
        q_hbm, k_hbm, v_hbm, n_hbm, table_ref, refs = *refs[:5], refs[5:]
        later_refs, refs = refs[:n_later], refs[n_later:]
        mixed_refs, vec_refs, refs = refs[:chunks], refs[chunks : chunks + n_vec], refs[chunks + n_vec :]
        heads_ref, x_ref, w_ref, q_ref, k_ref, v_ref, n_ref, out_ref, sems = refs
        copies = Copies(sems)

        def part(ref, index):
            return ref.at[pl.ds(index * block, block)]

        loads = [copies.start(part(x_hbm, 0), part(x_ref, 0))]
        small_loads = [copies.start(hbm, ref) for hbm, ref in zip(vec_hbm, vec_refs)]
        small_loads.append(copies.start(qv_hbm, heads_ref))
        weight_loads = [copies.start(w_hbm.at[i], w_ref.at[i]) for i in range(3)]
        loads += [copies.start(part(x_hbm, i), part(x_ref, i)) for i in range(1, blocks)]
        later_loads = [copies.start(hbm, ref) for hbm, ref in zip(later_hbm, later_refs)]
        for load in small_loads:
            load.wait()
        for i in range(n_vec):
            table_ref[i : i + 1] = vec_refs[i][...]
        qv = [
            jnp.concatenate([heads_ref[i, h : h + 1] for h in range(local // head)], axis=1)
            for i in range(2)
        ]
        for i in range(blocks):
            loads[i].wait()
            rows_i = slice(i * block, (i + 1) * block)
            scaled, _ = norm_parts(x_ref[rows_i].astype(F32))
            normed = (scaled * vec_refs[GAIN1][...] + vec_refs[SHIFT1][...]).astype(BF16)
            n_ref[rows_i] = normed
            if i == 0:
                weight_loads[0].wait()
            queries = (dot_nn(normed, w_ref[0]) + qv[0]).astype(BF16)
            q_ref[rows_i] = queries * BF16(scale)
            if i == 0:
                weight_loads[1].wait()
            k_ref[rows_i] = dot_nn(normed, w_ref[1]).astype(BF16)
            if i == 0:
                weight_loads[2].wait()
            v_ref[rows_i] = (dot_nn(normed, w_ref[2]) + qv[1]).astype(BF16)
        stores = [
            copies.start(ref, hbm)
            for ref, hbm in ((q_ref, q_hbm), (k_ref, k_hbm), (v_ref, v_hbm), (n_ref, n_hbm))
        ]

        globals_, locals_ = item_counts(lengths_ref)
        average = col_sum(v_ref[...].astype(F32)) * (1.0 / count)
        out_ref[...] = jnp.broadcast_to(average, (count, local)).astype(BF16)
        low_half = lax.broadcasted_iota(jnp.int32, (1, pair), 1) < head

        def step(item, carry):
            first, offset, length, crop = item_place(item, globals_, locals_, count)
            window = pl.ds(first, WINDOW)
            by_query = lax.broadcasted_iota(jnp.int32, (WINDOW, 1), 0)
            by_key = lax.broadcasted_iota(jnp.int32, (1, WINDOW), 1)
            query_crop = crop_of(by_query, offset, length, crop, -2)
            key_crop = crop_of(by_key, offset, length, crop, -1)
            mask = jnp.where(query_crop == key_crop, 0.0, NEGATIVE)
            inside = query_crop >= 0
            for index in range(local // pair):
                columns = slice(index * pair, (index + 1) * pair)
                q2 = q_ref[window, columns]
                k2 = k_ref[window, columns]
                v2 = v_ref[window, columns]
                out = None
                for keep in (low_half, jnp.logical_not(low_half)):
                    kept_k = jnp.where(keep, k2, BF16(0))
                    kept_v = jnp.where(keep, v2, BF16(0))
                    scores = dot_nt(q2, kept_k) + mask
                    weights = jnp.exp(scores - jnp.max(scores, axis=1, keepdims=True))
                    total = jnp.sum(weights, axis=1, keepdims=True)
                    low = (weights * (1.0 / total)).astype(BF16)
                    term = dot_nn(low, kept_v)
                    out = term if out is None else out + term
                out_ref[window, columns] = jnp.where(
                    inside, out, out_ref[window, columns].astype(F32)
                ).astype(BF16)
            return carry

        lax.fori_loop(0, item_total(globals_, locals_), step, 0)
        for chunk in range(chunks):
            mixed_refs[chunk][...] = out_ref[chunk * rows : (chunk + 1) * rows]
        for copy in later_loads + stores:
            copy.wait()

    part = pltpu.HBM((count, local), BF16)
    wide = pltpu.HBM((count, width), BF16)
    hbm = (tokens, weight, *later)
    outs = [part, part, part, wide, shape((n_vec, width), F32)]
    outs = outs + [shape(a.shape, a.dtype) for a in later] + [shape((rows, local), BF16)] * chunks
    return call(
        kernel,
        "attend_forward",
        [ANY] * (len(hbm) + n_vec + 1) + [SMEM],
        [ANY] * 4 + [VMEM] * (len(outs) - 4),
        outs,
        (*hbm, *vectors, qv_bias, lengths),
        scratch=[pltpu.VMEM((1, width), F32)] * n_vec
        + [
            pltpu.VMEM(qv_bias.shape, F32),
            pltpu.VMEM((count, width), BF16),
            pltpu.VMEM(weight.shape, BF16),
            pltpu.VMEM((count, local), BF16),
            pltpu.VMEM((count, local), BF16),
            pltpu.VMEM((count, local), BF16),
            pltpu.VMEM((count, width), BF16),
            pltpu.VMEM((count, local), BF16),
            pltpu.SemaphoreType.DMA((blocks + 8 + n_later + n_vec,)),
        ],
    )


def attend_backward(queries, keys, values, grad_mixed, lengths, scale, after, bring):
    count, local = queries.shape
    head = 64
    pair = 2 * head

    chunks = len(grad_mixed)
    rows = count // chunks

    def kernel(q_ref, k_ref, v_ref, *refs):
        chunk_refs, refs = refs[:chunks], refs[chunks:]
        lengths_ref, out_ref, bias_ref, acc_ref, g_ref = refs
        for chunk in range(chunks):
            g_ref[chunk * rows : (chunk + 1) * rows] = chunk_refs[chunk][...]
        globals_, locals_ = item_counts(lengths_ref)
        acc_ref[...] = jnp.zeros_like(acc_ref)
        low_half = lax.broadcasted_iota(jnp.int32, (1, pair), 1) < head

        def step(item, carry):
            first, offset, length, crop = item_place(item, globals_, locals_, count)
            window = pl.ds(first, WINDOW)
            by_key = lax.broadcasted_iota(jnp.int32, (WINDOW, 1), 0)
            by_query = lax.broadcasted_iota(jnp.int32, (1, WINDOW), 1)
            query_crop = crop_of(by_query, offset, length, crop, -2)
            key_crop = crop_of(by_key, offset, length, crop, -1)
            mask = jnp.where(query_crop == key_crop, 0.0, NEGATIVE)
            inside = key_crop >= 0
            for index in range(local // pair):
                columns = slice(index * pair, (index + 1) * pair)
                q2 = q_ref[window, columns]
                k2 = k_ref[window, columns]
                v2 = v_ref[window, columns]
                g2 = jnp.where(inside, g_ref[window, columns], BF16(0))
                grad_q = grad_k = grad_v = None
                for keep in (low_half, jnp.logical_not(low_half)):
                    kept_k = jnp.where(keep, k2, BF16(0))
                    kept_v = jnp.where(keep, v2, BF16(0))
                    kept_q = jnp.where(keep, q2, BF16(0))
                    kept_g = jnp.where(keep, g2, BF16(0))
                    scores = dot_nt(kept_k, q2) + mask
                    weights = jnp.exp(scores - jnp.max(scores, axis=0, keepdims=True))
                    total = jnp.sum(weights, axis=0, keepdims=True)
                    probability = weights * (1.0 / total)
                    grad_probability = dot_nt(kept_v, g2)
                    delta = jnp.sum(probability * grad_probability, axis=0, keepdims=True)
                    grad_scores = (probability * (grad_probability - delta)).astype(BF16)
                    term_v = dot_nn(probability.astype(BF16), kept_g)
                    term_k = dot_nn(grad_scores, kept_q)
                    term_q = dot_tn(grad_scores, kept_k)
                    grad_v = term_v if grad_v is None else grad_v + term_v
                    grad_k = term_k if grad_k is None else grad_k + term_k
                    grad_q = term_q if grad_q is None else grad_q + term_q
                acc_ref[0, window, columns] += grad_q * scale
                acc_ref[1, window, columns] += grad_k
                acc_ref[2, window, columns] += grad_v
            return carry

        lax.fori_loop(0, item_total(globals_, locals_), step, 0)
        for part in range(3):
            out_ref[:, part * local : (part + 1) * local] = acc_ref[part].astype(BF16)
            bias_ref[part : part + 1] = col_sum(acc_ref[part])

    return call(
        kernel,
        "attend_backward",
        [VMEM, VMEM, VMEM] + [VMEM] * chunks + [SMEM],
        [VMEM, VMEM],
        [shape((count, 3 * local), BF16), shape((3, local), F32)],
        (queries, keys, values, *grad_mixed, lengths),
        after,
        scratch=[pltpu.VMEM((3, count, local), F32), pltpu.VMEM((count, local), BF16)],
        bring=bring,
    )


def gelu_parts(value):
    size = jnp.abs(value)
    bell = jnp.exp(value * value * -0.5)
    t = 1.0 / (1.0 + size * (0.3275911 * 0.7071067811865476))
    poly = t * (
        0.254829592
        + t * (-0.284496736 + t * (1.421413741 + t * (-1.453152027 + t * 1.061405429)))
    )
    tail = 0.5 * poly * bell
    share = jnp.where(value >= 0, 1.0 - tail, tail)
    return value * share, share + value * (bell * 0.3989422804014327)


def hidden_cotangent(cotangent, lengths, table, fc2, halves, chunks, after):
    count, width = cotangent.shape
    units = fc2.shape[0]
    rows = count // chunks
    n_half = len(halves)

    def kernel(c_ref, w_ref, table_ref, lengths_ref, *refs):
        half_refs, refs = refs[:n_half], refs[n_half:]
        gm_hbm, ga_refs, on_refs = refs[0], refs[1 : 1 + chunks], refs[1 + chunks : 1 + chunks + n_half]
        gm_ref, sems = refs[1 + chunks + n_half :]
        copies = Copies(sems)
        stores = []
        for half_ref, on_ref in zip(half_refs, on_refs):
            on_ref[...] = half_ref[...]
        for chunk in range(chunks):
            place = chunk * rows
            grad = c_ref[place : place + rows].astype(F32) * valid_rows(lengths_ref, place, rows)
            low = (grad * table_ref[SCALE_MLP : SCALE_MLP + 1]).astype(BF16)
            gm_ref[place : place + rows] = low
            own = pl.ds(place, rows)
            stores.append(copies.start(gm_ref.at[own], gm_hbm.at[own]))
            ga_refs[chunk][...] = dot_nt(low, w_ref[...]).astype(BF16)
        for copy in stores:
            copy.wait()

    return call(
        kernel,
        "hidden_cotangent",
        [VMEM, VMEM, VMEM, SMEM] + [VMEM] * n_half,
        [ANY] + [VMEM] * (chunks + n_half),
        [pltpu.HBM((count, width), BF16)]
        + [shape((rows, units), BF16)] * chunks
        + [shape(half.shape, BF16) for half in halves],
        (cotangent, fc2, table, lengths, *halves),
        after,
        scratch=[pltpu.VMEM((count, width), BF16), pltpu.SemaphoreType.DMA((chunks,))],
    )


def feed_forward(chunk, rows, mixed, proj, halves, place, tokens, grad_act, table, fc1, fc1_bias, after):
    width = tokens.shape[1]
    units = fc1.shape[1]
    step_units = min(512, units)
    steps = units // step_units
    parts = len(mixed)
    n_half = len(halves)
    depth = proj.shape[0] // 2

    def kernel(*refs):
        mixed_refs, p_ref, half_refs, refs = refs[:parts], refs[parts], refs[parts + 1 : parts + 1 + n_half], refs[parts + 1 + n_half :]
        place_ref, x_hbm, ga_ref, table_ref, fc1_ref, fb_ref = refs[:6]
        mid_hbm, n2_hbm, act_hbm, gh_hbm, fbg_ref, terms_ref, vec_ref, refs = *refs[6:13], refs[13:]
        mid_ref, n2_ref, act_ref, gh_ref, x_ref, sems = refs
        copies = Copies(sems)
        load = copies.start(x_hbm.at[pl.ds(chunk * rows, rows)], x_ref)

        def vector(row):
            return table_ref[row : row + 1]

        attn = vector(PROJ_BIAS) + dot_nn(mixed_refs[0][...], p_ref[...]).astype(BF16).astype(F32)
        for peer in range(parts - 1):
            m_ref = mixed_refs[peer + 1]
            if n_half == parts - 1:
                term = dot_nn(m_ref[...], half_refs[peer][...])
            else:
                first = pl.ds(pl.multiple_of(place_ref[0] * depth, depth), depth)
                other = pl.ds(pl.multiple_of((1 - place_ref[0]) * depth, depth), depth)
                term = dot_nn(m_ref[:, first], half_refs[2 * peer][...])
                term = term + dot_nn(m_ref[:, other], half_refs[2 * peer + 1][...])
            attn = attn + term.astype(BF16).astype(F32)
        load.wait()
        middle = x_ref[...].astype(F32) + vector(SCALE_ATTN) * attn
        mid_ref[...] = middle
        stores = [copies.start(mid_ref, mid_hbm)]
        scaled, _ = norm_parts(middle)
        n2_ref[...] = (scaled * vector(GAIN2) + vector(SHIFT2)).astype(BF16)
        stores.append(copies.start(n2_ref, n2_hbm))

        def hidden_of(j):
            units_j = slice(j * step_units, (j + 1) * step_units)
            return dot_nn(n2_ref[...], fc1_ref[:, units_j]) + fb_ref[:, units_j]

        total = None
        hidden = hidden_of(0)
        for j in range(steps):
            units_j = slice(j * step_units, (j + 1) * step_units)
            later = hidden_of(j + 1) if j + 1 < steps else None
            activated, slope = gelu_parts(hidden)
            own = pl.ds(j * step_units, step_units)
            act_ref[:, units_j] = activated.astype(BF16)
            stores.append(copies.start(act_ref.at[:, own], act_hbm.at[:, own]))
            grad_hidden = ga_ref[:, units_j].astype(F32) * slope
            fbg_ref[:, units_j] = col_sum(grad_hidden)
            low = grad_hidden.astype(BF16)
            gh_ref[:, units_j] = low
            stores.append(copies.start(gh_ref.at[:, own], gh_hbm.at[:, own]))
            term = dot_nt(low, fc1_ref[:, units_j])
            total = term if total is None else total + term
            hidden = later
        low_terms = total.astype(BF16)
        terms_ref[...] = low_terms
        wide = low_terms.astype(F32)
        scaled, _ = norm_parts(mid_ref[...])
        vec_ref[0:1] = col_sum(wide * scaled)
        vec_ref[1:2] = col_sum(wide)
        for copy in stores:
            copy.wait()

    args = (*mixed, proj, *halves, place, tokens, grad_act, table, fc1, fc1_bias)
    return call(
        kernel,
        "feed_forward",
        [VMEM] * (parts + 1 + n_half) + [SMEM, ANY] + [VMEM] * 3 + [COPIED],
        [ANY] * 4 + [VMEM] * 3,
        [
            pltpu.HBM((rows, width), F32),
            pltpu.HBM((rows, width), BF16),
            pltpu.HBM((rows, units), BF16),
            pltpu.HBM((rows, units), BF16),
            shape((1, units), F32),
            shape((rows, width), BF16),
            shape((2, width), F32),
        ],
        args,
        after,
        scratch=[
            pltpu.VMEM((rows, width), F32),
            pltpu.VMEM((rows, width), BF16),
            pltpu.VMEM((rows, units), BF16),
            pltpu.VMEM((rows, units), BF16),
            pltpu.VMEM((rows, width), BF16),
            pltpu.SemaphoreType.DMA((3 + 2 * steps,)),
        ],
    )


def second_projection(activated, fc2, cotangent, lengths, after, bring):
    units, width = fc2.shape
    chunks = len(activated)
    rows = activated[0].shape[0]
    block = min(512, units)
    steps = units // block

    def kernel(begin, *refs):
        a_hbm, refs = refs[:chunks], refs[chunks:]
        w_hbm, c_hbm, lengths_ref, refs = refs[0], refs[1], refs[2], refs[3:]
        out_ref, vec_ref, refs = refs[0], refs[1], refs[2:]
        a_refs, (w_ref, c_ref, sems) = refs[:chunks], refs[chunks:]
        copies = Copies(sems)
        loads = []
        for j in range(steps):
            own = pl.ds(j * block, block)
            loads.append([copies.start(w_hbm.at[own], w_ref.at[own])])
            loads[j].append(copies.start(a_hbm[0].at[:, own], a_refs[0].at[:, own]))
        late = [copies.start(hbm, ref) for hbm, ref in zip(a_hbm[1:], a_refs[1:])]
        late.append(copies.start(c_hbm, c_ref))
        begin()
        for chunk in range(chunks):
            total = None
            if chunk == 0:
                for j in range(steps):
                    for load in loads[j]:
                        load.wait()
                    place = slice(j * block, (j + 1) * block)
                    term = dot_nn(a_refs[0][:, place], w_ref[place])
                    total = term if total is None else total + term
                for load in late:
                    load.wait()
            else:
                total = dot_nn(a_refs[chunk][...], w_ref[...])
            terms = total.astype(BF16)
            place = slice(chunk * rows, (chunk + 1) * rows)
            out_ref[place] = terms
            grad = c_ref[place].astype(F32) * valid_rows(lengths_ref, chunk * rows, rows)
            first, second = col_sum(grad * terms.astype(F32)), col_sum(grad)
            vec_ref[0:1] = first if chunk == 0 else vec_ref[0:1] + first
            vec_ref[1:2] = second if chunk == 0 else vec_ref[1:2] + second

    return call(
        kernel,
        "second_projection",
        [ANY] * (chunks + 2) + [SMEM],
        [VMEM] * 2,
        [shape(cotangent.shape, BF16), shape((2, width), F32)],
        (*activated, fc2, cotangent, lengths),
        after,
        scratch=[pltpu.VMEM((rows, units), BF16)] * chunks
        + [
            pltpu.VMEM(fc2.shape, BF16),
            pltpu.VMEM(cotangent.shape, BF16),
            pltpu.SemaphoreType.DMA((2 * steps + chunks,)),
        ],
        bring=bring,
        late=True,
    )


def weight_grads(normed, grad_hidden, grad_mlp, activated, place, radix, shard, after):
    width = normed[0].shape[1]
    chunks = len(normed)
    rows = normed[0].shape[0]
    units = activated[0].shape[1]
    block = min(512, units)
    slots = 2
    steps = 2 * units // block
    half = steps // 2
    groups = width // (radix * shard)

    def kernel(*refs):
        n_hbm, h_hbm, a_hbm = refs[:chunks], refs[chunks : 2 * chunks], refs[2 * chunks : 3 * chunks]
        g_hbm, place_ref, refs = refs[3 * chunks], refs[3 * chunks + 1], refs[3 * chunks + 2 :]
        out_hbm, (n_ref, g_ref, right_ref, hold_ref, sems) = refs[:radix], refs[radix:]
        copies = Copies(sems)

        def rows_of(chunk):
            return pl.ds(chunk * rows, rows)

        loads = [[] for _ in range(steps)]
        for c in range(chunks):
            loads[0].append(copies.start(n_hbm[c], n_ref.at[rows_of(c)]))
        for step in range(steps):
            own = pl.ds(step % half * block, block)
            if step == half:
                loads[step].append(copies.start(g_hbm, g_ref))
            for c in range(chunks):
                source = (h_hbm if step < half else a_hbm)[c].at[:, own]
                loads[step].append(copies.start(source, right_ref.at[step, rows_of(c)]))
        flying = [[] for _ in range(slots)]
        for step in range(steps):
            for load in loads[step]:
                load.wait()
            total = dot_tn((n_ref if step < half else g_ref)[...], right_ref[step])
            slot = step % slots
            for copy in flying[slot]:
                copy.wait()
            hold_ref[slot] = total.astype(BF16).reshape(groups, radix, shard, block)
            columns = pl.ds(step * block, block)
            flying[slot] = [
                copies.start(
                    hold_ref.at[slot, :, lax.rem(place_ref[0] + part, radix)], out_hbm[part].at[:, :, columns]
                )
                for part in range(radix)
            ]
        for group in flying:
            for copy in group:
                copy.wait()

    return call(
        kernel,
        "weight_grads",
        [ANY] * (3 * chunks + 1) + [SMEM],
        [ANY] * radix,
        [pltpu.HBM((groups, shard, 2 * units), BF16)] * radix,
        (*normed, *grad_hidden, *activated, grad_mlp, place),
        after,
        scratch=[
            pltpu.VMEM((chunks * rows, width), BF16),
            pltpu.VMEM((chunks * rows, width), BF16),
            pltpu.VMEM((steps, chunks * rows, block), BF16),
            pltpu.VMEM((slots, groups, radix, shard, block), BF16),
            pltpu.SemaphoreType.DMA((chunks + 1 + (chunks + radix) * steps,)),
        ],
    )


def attention_grads(normed, grads, grad_attn, mixed, weight, sums, table, raw, share, place, radix, shard, after):
    count, width = normed.shape
    block = max(256, radix * shard)
    wide, local = grads.shape[1], mixed[0].shape[1]
    extra = 128
    total = wide + local + extra
    groups = block // (radix * shard)
    chunks = len(mixed)
    head = 64
    flat_raw = [part for group in raw for part in group]
    n_raw = len(flat_raw)
    units = raw[3][0].shape[1]

    def kernel(n_ref, g_ref, *refs):
        a_refs, m_refs, refs = refs[:chunks], refs[chunks : 2 * chunks], refs[2 * chunks :]
        raw_refs, refs = refs[:n_raw], refs[n_raw:]
        w_ref, s_ref, table_ref, place_ref = refs[:4]
        out_refs, hold_ref, v_ref = refs[4 : 4 + radix], refs[4 + radix], refs[5 + radix]

        def vector(row):
            return table_ref[row : row + 1]

        def both(group):
            first = sum(len(g) for g in raw[:group])
            return sum(ref[...] for ref in raw_refs[first : first + len(raw[group])])

        middle, norm2, result, hidden = both(0), both(1), both(2), both(3)
        v_ref[...] = jnp.zeros_like(v_ref)
        v_ref[0:1] = vector(GAIN1)
        v_ref[1:2] = vector(SHIFT1)
        v_ref[2:3] = middle[0:1] / vector(SCALE_ATTN) * share
        v_ref[3:4] = middle[1:2] * vector(SCALE_ATTN) * share
        v_ref[4:6] = norm2
        v_ref[6:7] = result[0:1] + result[1:2] * vector(FC2_BIAS) * share
        v_ref[7:8] = result[1:2] * vector(SCALE_MLP) * share

        def spread(flats, first):
            stack = [f[:, i * head : (i + 1) * head] for f in flats for i in range(f.shape[1] // head)]
            stack = jnp.concatenate(stack, axis=0)
            for group in range(head // shard):
                piece = stack[:, group * shard : (group + 1) * shard]
                repeat = max(1, 128 // shard)
                piece = jnp.concatenate([piece] * repeat, axis=1)
                piece = jnp.concatenate([piece] * (width // (repeat * shard)), axis=1)
                v_ref[first : first + stack.shape[0]] = piece
                first += stack.shape[0]
            return first

        spread([hidden], spread([s_ref[0:1], s_ref[2:3]], 8))
        lane = lax.broadcasted_iota(jnp.int32, (block, extra), 1)
        for i in range(width // block):
            blk = slice(i * block, (i + 1) * block)
            columns = v_ref[:, blk].T
            first = second = None
            product = dot_tn(n_ref[:, blk], g_ref[...])
            for part in range(3):
                piece = product[:, part * local : (part + 1) * local]
                w = w_ref[part, blk].astype(F32)
                one = jnp.sum(w * piece, axis=1, keepdims=True)
                two = jnp.sum(w * s_ref[part : part + 1], axis=1, keepdims=True)
                first = one if first is None else first + one
                second = two if second is None else second + two
            gain_grad = (first - columns[:, 1:2] * second) / columns[:, 0:1]
            small = jnp.where(lane == 0, gain_grad, jnp.where(lane == 1, second, columns))
            product_p = None
            for c in range(chunks):
                term = dot_tn(a_refs[c][:, blk], m_refs[c][...])
                product_p = term if product_p is None else product_p + term
            hold_ref[:, :, :, :wide] = product.astype(BF16).reshape(groups, radix, shard, wide)
            hold_ref[:, :, :, wide : wide + local] = product_p.astype(BF16).reshape(groups, radix, shard, local)
            hold_ref[:, :, :, wide + local :] = small.astype(BF16).reshape(groups, radix, shard, extra)
            for step in range(radix):
                out_refs[step][i * groups : (i + 1) * groups] = hold_ref[:, lax.rem(place_ref[0] + step, radix)]

    return call(
        kernel,
        "attention_grads",
        [VMEM, VMEM] + [VMEM] * (2 * chunks + n_raw) + [VMEM, VMEM, VMEM, SMEM],
        [VMEM] * radix,
        [shape((width // (radix * shard), shard, total), BF16)] * radix,
        (normed, grads, *grad_attn, *mixed, *flat_raw, weight, sums, table, place),
        after,
        scratch=[pltpu.VMEM((groups, radix, shard, total), BF16), pltpu.VMEM((extra, width), F32)],
    )


def add_stage(parts, place, radix, after):
    left, shard, columns = parts[0].shape
    n_parts = len(parts)

    def kernel(*refs):
        part_refs, place_ref, out_refs = refs[:n_parts], refs[n_parts], refs[n_parts + 1 :]
        for group in range(left // radix):
            for step in range(radix):
                source = group * radix + lax.rem(place_ref[0] + step, radix)
                total = None
                for ref in part_refs:
                    term = ref[source].astype(F32)
                    total = term if total is None else total + term
                out_refs[step][group] = total.astype(BF16)

    return call(
        kernel,
        "add_stage",
        [VMEM] * n_parts + [SMEM],
        [VMEM] * radix,
        [shape((left // radix, shard, columns), BF16)] * radix,
        (*parts, place),
        after,
    )


def add_far_stage(ways, after, name):
    sizes = [(len(way[0]), *way[0][0].shape[:2], way[2], way[3]) for way in ways]
    n_out = sum(size[4] for size in sizes)
    n_ways = len(ways)
    kept = [way[0][0] for way in ways]
    arrived = []
    for way in ways:
        arrived += [array for array in way[0][1:] if not any(array is other for other in arrived)]

    def kernel(*refs):
        hbm, refs = refs[:n_ways], refs[n_ways:]
        arrived_refs, place_refs, refs = refs[: len(arrived)], refs[len(arrived) :][:n_ways], refs[len(arrived) + n_ways :]
        out_hbm, refs = refs[:n_out], refs[n_out:]
        in_refs, out_refs, sems = refs[:n_ways], refs[n_ways : 2 * n_ways], refs[2 * n_ways]
        copies = Copies(sems)
        loads = []
        for w, (_, left, _, columns, radix) in enumerate(sizes):
            _, first, _, _, _, below = ways[w]
            span = radix * below
            loads.append(
                [
                    copies.start(
                        hbm[w].at[pl.ds(high * span, span), :, pl.ds(first, columns)],
                        in_refs[w].at[pl.ds(high * span, span)],
                    )
                    for high in range(left // span)
                ]
            )
        stores = []
        given = 0
        for w, (_, left, _, columns, radix) in enumerate(sizes):
            arrays, first, _, _, _, below = ways[w]
            others = [
                arrived_refs[next(i for i, other in enumerate(arrived) if other is array)] for array in arrays[1:]
            ]
            for group in range(left // radix):
                high, low = divmod(group, below)
                if low == 0:
                    loads[w][high].wait()
                for step in range(radix):
                    digit = lax.rem(place_refs[w][0] + step, radix)
                    source = (high * radix + digit) * below + low
                    total = in_refs[w][source].astype(F32)
                    for ref in others:
                        total = total + ref[source, :, first : first + columns].astype(F32)
                    out_refs[w][step, group] = total.astype(BF16)
                    stores.append(copies.start(out_refs[w].at[step, group], out_hbm[given + step].at[group]))
            given += radix
        for copy in stores:
            copy.wait()

    count = sum(left // (radix * way[5]) + left for (_, left, _, _, radix), way in zip(sizes, ways))
    out, done = call(
        kernel,
        name,
        [ANY] * n_ways + [VMEM] * len(arrived) + [SMEM] * n_ways,
        [ANY] * n_out,
        [pltpu.HBM((left // radix, rows, columns), BF16) for _, left, rows, columns, radix in sizes for _ in range(radix)],
        (*kept, *arrived, *[way[4] for way in ways]),
        after,
        scratch=[pltpu.VMEM((left, rows, columns), BF16) for _, left, rows, columns, _ in sizes]
        + [pltpu.VMEM((radix, left // radix, rows, columns), BF16) for _, left, rows, columns, radix in sizes]
        + [pltpu.SemaphoreType.DMA((count,))],
    )
    split = []
    for size in sizes:
        split.append(out[: size[4]])
        out = out[size[4] :]
    return split, done


def last_far_stage(firsts, seconds, after):
    _, shard, units = firsts[0].shape
    n_first = len(firsts)

    def total_of(refs):
        total = None
        for ref in refs:
            term = ref[0].astype(F32)
            total = term if total is None else total + term
        return total

    def kernel(*refs):
        first_ref, second_ref = refs[-2:]
        first_ref[...] = total_of(refs[:n_first])
        second_ref[...] = total_of(refs[n_first:-2]).T

    return call(
        kernel,
        "last_far_stage",
        [VMEM] * (n_first + len(seconds)),
        [COPIED] * 2,
        [shape((shard, units), F32), shape((units, shard), F32)],
        (*firsts, *seconds),
        after,
    )


def last_stage(parts, local, after):
    _, shard, columns = parts[0].shape
    n_parts = len(parts)
    extra = columns - 4 * local

    def kernel(*refs):
        part_refs, (qkv_ref, proj_ref, small_ref) = refs[:n_parts], refs[n_parts:]
        total = None
        for ref in part_refs:
            term = ref[0].astype(F32)
            total = term if total is None else total + term
        for part in range(3):
            qkv_ref[part] = total[:, part * local : (part + 1) * local]
        proj_ref[...] = total[:, 3 * local : 4 * local].T
        small_ref[...] = total[:, 4 * local :].T

    return call(
        kernel,
        "last_stage",
        [VMEM] * n_parts,
        [COPIED] * 3,
        [shape((3, shard, local), F32), shape((local, shard), F32), shape((extra, shard), F32)],
        tuple(parts),
        after,
    )


def middle_back(chunk, rows, terms, middle, tokens, cotangent, lengths, table, proj, after, bring):
    width = middle.shape[1]
    local = proj.shape[0]
    parts = len(terms)

    def kernel(*refs):
        term_refs, refs = refs[:parts], refs[parts:]
        mid_ref, x_hbm, c_hbm, lengths_ref, table_ref, p_ref = refs[:6]
        gmid_hbm, low_ref, gmix_ref, vec_ref, gmid_ref, x_ref, c_ref, sems = refs[6:]
        copies = Copies(sems)
        own = pl.ds(chunk * rows, rows)
        loads = [copies.start(c_hbm.at[own], c_ref), copies.start(x_hbm.at[own], x_ref)]
        grad_norm = None
        for ref in term_refs:
            term = ref[...].astype(F32)
            grad_norm = term if grad_norm is None else grad_norm + term
        middle = mid_ref[...]
        scaled, inverse = norm_parts(middle)
        back = norm_back(grad_norm, scaled, inverse, table_ref[GAIN2 : GAIN2 + 1])
        loads[0].wait()
        grad = c_ref[...].astype(F32) * valid_rows(lengths_ref, chunk * rows, rows) + back
        gmid_ref[...] = grad
        store = copies.start(gmid_ref, gmid_hbm)
        low = (table_ref[SCALE_ATTN : SCALE_ATTN + 1] * grad).astype(BF16)
        low_ref[...] = low
        gmix_ref[...] = dot_nt(low, p_ref[...]).astype(BF16)
        loads[1].wait()
        vec_ref[0:1] = col_sum(grad * (middle - x_ref[...].astype(F32)))
        vec_ref[1:2] = col_sum(grad)
        store.wait()

    return call(
        kernel,
        f"middle_back_{chunk}",
        [VMEM] * parts + [VMEM, ANY, ANY, SMEM, VMEM, VMEM],
        [ANY] + [VMEM] * 3,
        [
            pltpu.HBM((rows, width), F32),
            shape((rows, width), BF16),
            shape((rows, local), BF16),
            shape((2, width), F32),
        ],
        (*terms, middle, tokens, cotangent, lengths, table, proj),
        after,
        scratch=[
            pltpu.VMEM((rows, width), F32),
            pltpu.VMEM((rows, width), BF16),
            pltpu.VMEM((rows, width), BF16),
            pltpu.SemaphoreType.DMA((3,)),
        ],
        bring=bring,
    )


def first_norm_terms(chunk, rows, grads, weight, after):
    width, local = weight.shape[1:]

    def kernel(g_ref, w_ref, out_ref):
        place = slice(chunk * rows, (chunk + 1) * rows)
        total = None
        for part in range(3):
            term = dot_nt(g_ref[place, part * local : (part + 1) * local], w_ref[part])
            total = term if total is None else total + term
        out_ref[...] = total.astype(BF16)

    return call(
        kernel,
        "first_norm_terms",
        [VMEM, VMEM],
        VMEM,
        shape((rows, width), BF16),
        (grads, weight),
        after,
    )


def to_rows(chunk, rows, compute, args, specs, dims, kept, after, name, sources=()):
    extra = 0 if kept is None else 1
    blocks = 2
    block = rows // blocks
    n_args = len(args)
    n_source = len(sources)
    args, specs = args + tuple(array for array, _ in sources), specs + [ANY] * n_source

    def kernel(*refs):
        ins, refs = refs[:n_args], refs[n_args:]
        source_hbm, refs = refs[:n_source], refs[n_source:]
        out_hbm, hold_ref, sems = refs[extra : extra + 3]
        source_refs = refs[extra + 3 :]
        copies = Copies(sems)
        loads = [
            [
                copies.start(hbm.at[pl.ds(first + i * block, block)], ref.at[i])
                for hbm, ref, (_, first) in zip(source_hbm, source_refs, sources)
            ]
            for i in range(blocks)
        ]
        stores = []
        for i in range(blocks):
            for load in loads[i]:
                load.wait()
            hold_ref[i] = compute(i * block, block, *[ref[i] for ref in source_refs], *ins).astype(BF16)
            place = pl.ds(chunk * rows + i * block, block)
            stores.append(copies.start(hold_ref.at[i], out_hbm.at[place]))
        for copy in stores:
            copy.wait()

    alias = None
    if extra:
        alias = {len(args): 0}
        args = args + (kept,)
    scratch = [
        pltpu.VMEM((blocks, block, dims[1]), BF16),
        pltpu.SemaphoreType.DMA(((1 + n_source) * blocks,)),
        *[pltpu.VMEM((blocks, block, dims[1]), array.dtype) for array, _ in sources],
    ]
    return call(
        kernel,
        name,
        specs + [ANY] * extra,
        ANY,
        pltpu.HBM(dims, BF16),
        args,
        after,
        scratch=scratch,
        alias=alias,
    )


def token_grads(chunk, rows, terms, grad_middle, tokens, table, kept, after):
    parts = len(terms)

    def compute(first, block, x, grad, *refs):
        table_ref = refs[parts]
        place = slice(first, first + block)
        grad_norm = None
        for ref in refs[:parts]:
            term = ref[place].astype(F32)
            grad_norm = term if grad_norm is None else grad_norm + term
        scaled, inverse = norm_parts(x.astype(F32))
        return grad + norm_back(grad_norm, scaled, inverse, table_ref[GAIN1 : GAIN1 + 1])

    args = (*terms, table)
    specs = [VMEM] * (parts + 1)
    sources = ((tokens, chunk * rows), (grad_middle, 0))
    return to_rows(chunk, rows, compute, args, specs, tokens.shape, kept, after, "token_grads", sources)


def layer_output(terms, middle, lengths, table, after):
    parts = len(terms)
    count, width = terms[0].shape
    chunks = len(middle)
    rows = count // chunks
    blocks = 2
    block = rows // blocks

    def kernel(*refs):
        term_refs, mid_hbm, refs = refs[:parts], refs[parts : parts + chunks], refs[parts + chunks :]
        lengths_ref, table_ref, out_hbm, mid_ref, hold_ref, sems = refs
        copies = Copies(sems)
        loads = [
            copies.start(
                mid_hbm[i // blocks].at[pl.ds(i % blocks * block, block)], mid_ref.at[pl.ds(i * block, block)]
            )
            for i in range(chunks * blocks)
        ]
        stores = []
        for i in range(chunks * blocks):
            place = slice(i * block, (i + 1) * block)
            mlp = table_ref[FC2_BIAS : FC2_BIAS + 1]
            for ref in term_refs:
                mlp = mlp + ref[place].astype(F32)
            loads[i].wait()
            valid = valid_rows(lengths_ref, i * block, block)
            full = mid_ref[place] + table_ref[SCALE_MLP : SCALE_MLP + 1] * mlp
            hold_ref[place] = (valid * full).astype(BF16)
            own = pl.ds(i * block, block)
            stores.append(copies.start(hold_ref.at[own], out_hbm.at[own]))
        for copy in stores:
            copy.wait()

    return call(
        kernel,
        "layer_output",
        [VMEM] * parts + [ANY] * chunks + [SMEM, VMEM],
        ANY,
        pltpu.HBM((count, width), BF16),
        (*terms, *middle, lengths, table),
        after,
        scratch=[
            pltpu.VMEM((count, width), F32),
            pltpu.VMEM((count, width), BF16),
            pltpu.SemaphoreType.DMA((2 * chunks * blocks,)),
        ],
    )


def from_peers(array):
    size = lax.axis_size("tensor")
    return [
        lax.ppermute(array, "tensor", [(i, (i + step) % size) for i in range(size)])
        for step in range(1, size)
    ]


def other_of_pair(array):
    return lax.ppermute(array, "dp", [(i, i ^ 1) for i in range(lax.axis_size("dp"))])


def radices(size):
    found = []
    if size % 2 == 0:
        found.append(2)
        size //= 2
    while size > 1:
        step = 2 if size % 4 and size % 2 == 0 or size == 8 else next((r for r in (4, 3) if size % r == 0), size)
        found.append(step)
        size //= step
    return found


def small_digits(size, stride):
    digits = []
    while stride < size:
        left = size // stride
        radix = next(r for r in (2, 3, 5, left) if left % r == 0)
        digits.append((stride, radix))
        stride *= radix
    return digits


def exchange(parts, stride, radix):
    size = lax.axis_size("dp")
    arrived = []
    for step in range(1, radix):
        moves = []
        for i in range(size):
            at = (i // stride) % radix
            moves.append((i, i + ((at + step) % radix - at) * stride))
        arrived.append(lax.ppermute(parts[step], "dp", moves))
    return [parts[0]] + arrived


def body(
    tokens,
    lengths,
    norm1_gain,
    norm1_bias,
    qkv_weight,
    qv_bias,
    proj_weight,
    proj_bias,
    scale_attn,
    norm2_gain,
    norm2_bias,
    fc1_weight,
    fc1_bias,
    fc2_weight,
    fc2_bias,
    scale_mlp,
    cotangent,
):
    count, width = tokens.shape
    heads, head_size = qv_bias.shape[1:]
    local = heads * head_size
    units = fc1_weight.shape[1]
    tensor = lax.axis_size("tensor")
    dp = lax.axis_size("dp")
    chunks = 2
    rows = count // chunks
    scale = head_size**-0.5

    def flat(vector):
        return vector.reshape(1, -1)

    index = lax.axis_index("dp")
    steps = radices(dp)
    strides = [1]
    for step in steps:
        strides.append(strides[-1] * step)
    places = [((index // stride) % step).reshape(1) for stride, step in zip(strides, steps)]

    half_rows = local // 2
    paired = dp % 2 == 0 and half_rows % 128 == 0
    half_place = (index % 2).reshape(1)
    half = proj_weight
    if paired:
        half = lax.dynamic_slice_in_dim(proj_weight, half_place[0] * half_rows, half_rows, 0)
    halves = from_peers(half)
    vectors = (norm1_gain, norm1_bias, norm2_gain, norm2_bias, proj_bias, scale_attn, fc2_bias, scale_mlp)
    out, done = attend_forward(
        tokens,
        lengths,
        [flat(vector) for vector in vectors],
        qkv_weight,
        qv_bias,
        scale,
        chunks,
        (cotangent, fc2_weight, proj_weight, fc1_weight),
    )
    queries, keys, values, normed1, table, cotangent_near, fc2_near, proj_weight, fc1_weight = out[:9]
    mixed = out[9:]
    mixed_parts = [[part] + from_peers(part) for part in mixed]
    out, done = hidden_cotangent(cotangent_near, lengths, table, fc2_near, halves, chunks, done)
    grad_mlp, grad_act, halves = out[0], out[1 : 1 + chunks], out[1 + chunks :]
    if paired:
        halves = [part for half in halves for part in (half, other_of_pair(half))]

    middle, normed2, activated, grad_hidden, norm2_parts = [], [], [], [], []
    raw = [[], [], [], []]
    for chunk in range(chunks):
        out, done = feed_forward(
            chunk,
            rows,
            mixed_parts[chunk],
            proj_weight,
            halves,
            half_place,
            tokens,
            grad_act[chunk],
            table,
            fc1_weight,
            flat(fc1_bias),
            done,
        )
        for group, part in zip((middle, normed2, activated, grad_hidden), out[:4]):
            group.append(part)
        raw[3].append(out[4])
        raw[1].append(out[6])
        norm2_parts.append([out[5]] + from_peers(out[5]))

    shard = width // dp
    fc_parts, done = weight_grads(
        normed2, grad_hidden, grad_mlp, activated, places[0], steps[0], shard, done
    )
    fc_parts = exchange(fc_parts, 1, steps[0])

    def near_stage(parts, stage, done):
        parts, done = add_stage(parts, places[stage], steps[stage], done)
        return exchange(parts, strides[stage], steps[stage]), done

    out, done = second_projection(activated, fc2_weight, cotangent, lengths, done, middle)
    mlp_parts = [out[0]] + from_peers(out[0])
    raw[2].append(out[1])
    middle_near = out[2:]

    grad_middle, grad_attn, grad_mixed = [], [], []
    for chunk in range(chunks):
        out, done = middle_back(
            chunk,
            rows,
            norm2_parts[chunk],
            middle_near[chunk],
            tokens,
            cotangent,
            lengths,
            table,
            proj_weight,
            done,
            (queries, keys, values) if chunk == 0 else (),
        )
        if chunk == 0:
            queries, keys, values = out[4:]
        for group, part in zip((grad_middle, grad_attn, grad_mixed), out[:3]):
            group.append(part)
        raw[0].append(out[3])
    stages = len(steps)
    digits = small_digits(dp, strides[1])
    orders = [digits, digits[1:] + digits[:1]]

    def far_stage(at, firsts, seconds, start, done):
        ways = []
        for arrays, first, order in ((firsts, 0, orders[0]), (seconds, start, orders[1])):
            stride, radix = order[at]
            below = 1
            for other_stride, other_radix in order[at:]:
                below *= other_radix if other_stride < stride else 1
            place = ((index // stride) % radix).reshape(1)
            ways.append((arrays, first, units, radix, place, below))
        split, done = add_far_stage(ways, done, f"add_far_stage_{at}")
        return [exchange(parts, *order[at]) for parts, order in zip(split, orders)], done

    (firsts, seconds), done = far_stage(0, fc_parts, fc_parts, units, done)
    (grads, grad_sums, qkv_weight, normed1), done = attend_backward(
        queries, keys, values, grad_mixed, lengths, scale, done, (qkv_weight, normed1)
    )
    parts, done = attention_grads(
        normed1,
        grads,
        grad_attn,
        mixed,
        qkv_weight,
        grad_sums,
        table,
        raw,
        1.0 / tensor,
        places[0],
        steps[0],
        shard,
        done,
    )
    parts = exchange(parts, 1, steps[0])
    norm1_parts = []
    for chunk in range(chunks):
        terms, done = first_norm_terms(chunk, rows, grads, qkv_weight, done)
        norm1_parts.append([terms] + from_peers(terms))
    output, done = layer_output(mlp_parts, middle, lengths, table, done)
    at = 1
    if at < len(digits):
        (firsts, seconds), done = far_stage(at, firsts, seconds, 0, done)
        at += 1
    stage = 1
    if stage < stages:
        parts, done = near_stage(parts, stage, done)
        stage += 1
    grad_tokens = None
    for chunk in range(chunks - 1):
        grad_tokens, done = token_grads(
            chunk, rows, norm1_parts[chunk], grad_middle[chunk], tokens, table, grad_tokens, done
        )
    while at < len(digits):
        (firsts, seconds), done = far_stage(at, firsts, seconds, 0, done)
        at += 1
    while stage < stages:
        parts, done = near_stage(parts, stage, done)
        stage += 1
    grad_tokens, done = token_grads(
        chunks - 1, rows, norm1_parts[-1], grad_middle[-1], tokens, table, grad_tokens, done
    )
    (fc1_grad, fc2_grad), done = last_far_stage(firsts, seconds, done)
    (qkv_grad, proj_grad, small), done = last_stage(parts, local, done)

    vector_share = small[:8]
    for other in from_peers(vector_share):
        vector_share = vector_share + other
    own = shard // tensor
    vector_share = lax.dynamic_slice_in_dim(vector_share, lax.axis_index("tensor") * own, own, 1)

    def columns_of(first, heads_in):
        groups = head_size // shard
        pieces = [small[first + i * heads_in : first + (i + 1) * heads_in] for i in range(groups)]
        every = pieces[0] if groups == 1 else jnp.concatenate(pieces, axis=1)
        return lax.dynamic_slice_in_dim(every, index * (head_size // dp), head_size // dp, 1)

    bias_share = columns_of(8, 2 * heads).reshape(2, heads, -1)
    fc1_share = columns_of(8 + 2 * heads * (head_size // shard), units // head_size)

    return (
        output,
        grad_tokens,
        vector_share[0],
        vector_share[1],
        qkv_grad,
        bias_share,
        proj_grad,
        vector_share[3],
        vector_share[2],
        vector_share[4],
        vector_share[5],
        fc1_grad,
        fc1_share,
        fc2_grad,
        vector_share[7],
        vector_share[6],
    )


def solution(mesh):
    in_specs = (
        P("dp", None),
        P("dp", None),
        P(),
        P(),
        P(None, None, "tensor"),
        P(None, "tensor", None),
        P("tensor", None),
        P(),
        P(),
        P(),
        P(),
        P(None, "tensor"),
        P("tensor"),
        P("tensor", None),
        P(),
        P(),
        P("dp", None),
    )
    out_specs = (
        P("dp", None),
        P("dp", None),
        P(("dp", "tensor")),
        P(("dp", "tensor")),
        P(None, "dp", "tensor"),
        P(None, "tensor", "dp"),
        P("tensor", "dp"),
        P(("dp", "tensor")),
        P(("dp", "tensor")),
        P(("dp", "tensor")),
        P(("dp", "tensor")),
        P("dp", "tensor"),
        P("tensor", "dp"),
        P("tensor", "dp"),
        P(("dp", "tensor")),
        P(("dp", "tensor")),
    )
    return jax.shard_map(body, mesh=mesh, in_specs=in_specs, out_specs=out_specs, check_vma=False)
```

time: 271 us -> 224 us (0.83)
  the two profiles are of different devices: /device:TPU:8 before, /device:TPU:12 now
where the time goes in v3:
time: 224 us; the launch traced here: 220 us
  Pallas kernels  132 us (59%)
  waiting for transfers between devices  61.1 us (27%)
  starting transfers between devices  18.8 us (8%)
  local copies, waits for them, and re-layouts  6.73 us (3%)
    pallas_call x22, Pallas kernels, call(): pl.pallas_call(ordered, in_specs=list(in_specs) + [ANY] * (n_bring + n_af...  132 us
    ppermute x9, waiting for transfers between devices, from_peers(): lax.ppermute(array, 'tensor', [(i, (i + step) % size) for i in range(size)])  35.6 us
    ppermute x12, waiting for transfers between devices, exchange(): arrived.append(lax.ppermute(parts[step], 'dp', moves))  25.5 us
    ppermute x12, starting transfers between devices, exchange(): arrived.append(lax.ppermute(parts[step], 'dp', moves))  11.1 us
    ppermute x9, starting transfers between devices, from_peers(): lax.ppermute(array, 'tensor', [(i, (i + step) % size) for i in range(size)])  7.64 us
    unnamed x18, local copies, waits for them, and re-layouts  4.87 us
  transfers between devices with their start and end apart: 22, of which 10 were waited for; matrix products, arithmetic and copies ran while one was open for 2% of the time, Pallas kernels for 60%

profile of v3, /device:TPU:12, one launch (start us, length us, event | category | flops | bytes accessed | tf_op | source)
XLA Modules:
  0.0 220.0 jit_solution(6057278380186338003)
XLA Ops:
  0.7 1.1 constant_dynamic-slice_fusion.2
  1.7 1.6 collective-permute-start.1
  3.3 0.7 copy-done.1
  4.0 14.7 %attend_forward.1 = (bf16[1024,512]{1,0:T(8,128)(2,1)}, bf16[1024,512]{1,0:T(8,128)(2,1)}, bf16[1024,512]{1,0:T(8,128)(2,1)}, bf16[1024,1024]{1,0:T(8,128)(2,1)}...) custom-call(bf16[1024,1024]{1,0:T(8,128)(2,1)} %refs_3_.13, ...), custom_call_target="tpu_custom_call" | custom-call | flops 2300000000 | bytes 2300000000 | tf_op jit(solution)/shard_map/attend_forward/pallas_call | solution.py:112
  18.7 0.6 collective-permute-start
  19.3 6.2 %hidden_cotangent.1 = (bf16[1024,1024]{1,0:T(8,128)(2,1)}, bf16[512,2048]{1,0:T(8,128)(2,1)S(1)}, bf16[512,2048]{1,0:T(8,128)(2,1)S(1)}, bf16[256,1024]{1,0:T(8,128)(2,1)S(1)}, f32[8,128]{1,0:T(8,128)S(1)}) custom-call(bf16[1024,1024]{1,0:T(8,128)(2,1)S(1)} %get-tuple-element.119.refs_0_, bf16[2048,1024]{1,0:T(8,128)(2,1)S(1)} %get-tuple-element.120.refs_1_, ...), custom_call_target="tpu_custom_call" | custom-call | flops 2300000000 | bytes 2300000000 | tf_op jit(solution)/shard_map/hidden_cotangent/pallas_call | solution.py:112
  25.5 0.1 collective-permute-start.2
  25.6 1.6 collective-permute-start.3
  27.1 6.5 %collective-permute-done.refs_1_ = bf16[512,512]{1,0:T(8,128)(2,1)S(1)} collective-permute-done((bf16[512,512]{1,0:T(8,128)(2,1)S(1)}, bf16[512,512]{1,0:T(8,128)(2,1)S(1)}, u32[]{:S(2)}, u32[]{:S(2)}) %collective-permute-start) | collective-permute-done | bytes 524320 | tf_op jit(solution)/shard_map/ppermute | solution.py:1113
  33.6 12.5 %feed_forward.2 = (f32[512,1024]{1,0:T(8,128)}, bf16[512,1024]{1,0:T(8,128)(2,1)}, bf16[512,2048]{1,0:T(8,128)(2,1)}, bf16[512,2048]{1,0:T(8,128)(2,1)}, f32[1,2...) custom-call(bf16[512,512]{1,0:T(8,128)(2,1)S(1)} %get-tuple-element.117.refs_0_.re, ...), custom_call_target="tpu_custom_call" | custom-call | flops 2300000000 | bytes 2300000000 | tf_op jit(solution)/shard_map/feed_forward/pallas_call | solution.py:112
  46.1 0.6 collective-permute-start.5
  46.7 12.9 %feed_forward.3 = (f32[512,1024]{1,0:T(8,128)}, bf16[512,1024]{1,0:T(8,128)(2,1)}, bf16[512,2048]{1,0:T(8,128)(2,1)}, bf16[512,2048]{1,0:T(8,128)(2,1)}, f32[1,2...) custom-call(bf16[512,512]{1,0:T(8,128)(2,1)S(1)} %get-tuple-element.128.refs_0_.refs_5, ...), custom_call_target="tpu_custom_call" | custom-call | flops 2300000000 | bytes 2300000000 | tf_op jit(solution)/shard_map/feed_forward/pallas_call | solution.py:112
  59.7 1.6 collective-permute-start.6
  61.2 14.3 %weight_grads.1 = (bf16[8,64,4096]{2,1,0:T(8,128)(2,1)}, bf16[8,64,4096]{2,1,0:T(8,128)(2,1)}, f32[8,128]{1,0:T(8,128)S(1)}) custom-call(bf16[512,1024]{1,0:T(8,128)(2,1)} %get-tuple-element.134.refs_0_, bf16[512,1024]{1,0:T(8,128)(2,1)} %get-tuple-element.135.refs_1_, bf16[512,2048]{1,0:T(8,128)(2,1)} %get-tuple-element.136.refs_2_, ...), custom_call_target="tpu_custom_call" | custom-call | flops 2300000000 | bytes 2300000000 | tf_op jit(solution)/shard_map/weight_grads/pallas_call | solution.py:112
  75.5 0.1 collective-permute-start.7
  75.6 8.1 %second_projection.1 = (bf16[1024,1024]{1,0:T(8,128)(2,1)S(1)}, f32[2,1024]{1,0:T(2,128)S(1)}, f32[512,1024]{1,0:T(8,128)S(1)}, f32[512,1024]{1,0:T(8,128)S(1)}, f32[8,128]{1,0:T(8,128)S(1)}) custom-call(bf16[512,2048]{1,0:T(8,128)(2,1)} %get-tuple-element.127.refs_4_.refs_0_, bf16[512,2048]{1,0:T(8,128)(2,1)} %get-tuple-element.131.refs_5_.refs_1_, ...), custom_call_target="tpu_custom_call" | custom-call | flops 2300000000 | bytes 2300000000 | tf_op jit(solution)/shard_map/second_projection/pallas_call | solution.py:112
  83.7 0.6 collective-permute-start.4
  84.4 0.0 collective-permute-done.5.refs_1_
  84.4 5.0 %middle_back_0.1 = (f32[512,1024]{1,0:T(8,128)}, bf16[512,1024]{1,0:T(8,128)(2,1)S(1)}, bf16[512,512]{1,0:T(8,128)(2,1)S(1)}, f32[2,1024]{1,0:T(2,128)S(1)}, bf1...) custom-call(bf16[512,1024]{1,0:T(8,128)(2,1)S(1)} %get-tuple-element, ...), custom_call_target="tpu_custom_call" | custom-call | flops 2300000000 | bytes 2300000000 | tf_op jit(solution)/shard_map/middle_back_0/pallas_call | solution.py:112
  89.4 5.4 %collective-permute-done.6.refs_1_ = bf16[512,1024]{1,0:T(8,128)(2,1)} collective-permute-done((bf16[512,1024]{1,0:T(8,128)(2,1)}, bf16[512,1024]{1,0:T(8,128)(2,1)}, u32[]{:S(2)}, u32[]{:S(2)}) %collective-permute-start.6) | collective-permute-done | bytes 1048608 | tf_op jit(solution)/shard_map/ppermute | solution.py:1113
  94.9 5.0 %middle_back_1.1 = (f32[512,1024]{1,0:T(8,128)}, bf16[512,1024]{1,0:T(8,128)(2,1)S(1)}, bf16[512,512]{1,0:T(8,128)(2,1)S(1)}, f32[2,1024]{1,0:T(2,128)S(1)}, f32[8,128]{1,0:T(8,128)S(1)}) custom-call(bf16[512,1024]{1,0:T(8,128)(2,1)} %get-tuple-element.152.refs_0_, bf16[512,1024]{1,0:T(8,128)(2,1)} %collective-permute-done.6.refs_1_, ...), custom_call_target="tpu_custom_call" | custom-call | flops 46000001024 | bytes 2300000000 | tf_op jit(solution)/shard_map/middle_back_1/pallas_call | solution.py:112
  99.8 3.8 %add_far_stage_0.1 = (bf16[4,64,2048]{2,1,0:T(8,128)(2,1)}, bf16[4,64,2048]{2,1,0:T(8,128)(2,1)}, bf16[4,64,2048]{2,1,0:T(8,128)(2,1)}, bf16[4,64,2048]{2,1,0:T(8,128)(2,1)}, f32[8,128]{1,0:T(8,128)S(1)}) custom-call(bf16[8,64,4096]{2,1,0:T(8,128)(2,1)} %get-tuple-element.157.refs_0_.refs_1_, bf16[8,64,4096]{2,1,0:T(8,128)(2,1)} %get-tuple-element.157.refs_0_.refs_1_, ...), custom_call_target="tpu_custom_call" | custom-call | flops 2300000000 | bytes 2300000000 | tf_op jit(solution)/shard_map/add_far_stage_0/pallas_call | solution.py:112
  103.7 0.1 collective-permute-start.11
  103.8 0.5 collective-permute-start.12
  104.3 14.4 %attend_backward.1 = (bf16[1024,1536]{1,0:T(8,128)(2,1)S(1)}, f32[3,512]{1,0:T(4,128)S(1)}, bf16[3,1024,512]{2,1,0:T(8,128)(2,1)S(1)}, bf16[1024,1024]{1,0:T(8,128)(2,1)S(1)}, f32[8,128]{1,0:T(8,128)S(1)}) custom-call(bf16[1024,512]{1,0:T(8,128)(2,1)S(1)} %get-tuple-element.148.refs_0_, bf16[1024,512]{1,0:T(8,128)(2,1)S(1)} %get-tuple-element.149.refs_1_, ...), custom_call_target="tpu_custom_call" | custom-call | flops 2300000000 | bytes 2300000000 | tf_op jit(solution)/shard_map/attend_backward/pallas_call | solution.py:112
  118.7 6.1 %attention_grads.1 = (bf16[8,64,2176]{2,1,0:T(8,128)(2,1)S(1)}, bf16[8,64,2176]{2,1,0:T(8,128)(2,1)S(1)}, f32[8,128]{1,0:T(8,128)S(1)}) custom-call(bf16[1024,1024]{1,0:T(8,128)(2,1)S(1)} %get-tuple-element.163.refs_0_, bf16[1024,1536]{1,0:T(8,128)(2,1)S(1)} %get-tuple-element.161.refs_1_.refs_0_, bf16[512,1024]{1,0:T(8,128)(2,1)S(1)} %get-tuple-element.164.refs_2_, ...), custom_call_target="tpu_custom_call" | custom-call | flops 2300000000 | bytes 2300000000 | tf_op jit(solution)/shard_map/attention_grads/pallas_call | solution.py:112
  124.8 0.1 collective-permute-start.10
  124.9 2.8 %first_norm_terms.2 = (bf16[512,1024]{1,0:T(8,128)(2,1)}, f32[8,128]{1,0:T(8,128)S(1)}) custom-call(bf16[1024,1536]{1,0:T(8,128)(2,1)S(1)} %get-tuple-element.161.refs_1_.refs_0_, bf16[3,1024,512]{2,1,0:T(8,128)(2,1)S(1)} %get-tuple-element.162.refs_13_.refs_1_, f32[8,128]{1,0:T(8,128)S(1)} %get-tuple-element.175.refs_2_), custom_call_target="tpu_custom_call" | custom-call | flops 2300000000 | bytes 2300000000 | tf_op jit(solution)/shard_map/first_norm_terms/pallas_call | solution.py:112
  127.7 0.6 collective-permute-start.9
  128.3 2.8 %first_norm_terms.3 = (bf16[512,1024]{1,0:T(8,128)(2,1)}, f32[8,128]{1,0:T(8,128)S(1)}) custom-call(bf16[1024,1536]{1,0:T(8,128)(2,1)S(1)} %get-tuple-element.161.refs_1_.refs_0_, bf16[3,1024,512]{2,1,0:T(8,128)(2,1)S(1)} %get-tuple-element.162.refs_13_.refs_1_, f32[8,128]{1,0:T(8,128)S(1)} %get-tuple-element.176.refs_2_), custom_call_target="tpu_custom_call" | custom-call | flops 2300000000 | bytes 2300000000 | tf_op jit(solution)/shard_map/first_norm_terms/pallas_call | solution.py:112
  131.1 8.6 %collective-permute-done.4.refs_1_ = bf16[1024,1024]{1,0:T(8,128)(2,1)S(1)} collective-permute-done((bf16[1024,1024]{1,0:T(8,128)(2,1)S(1)}, bf16[1024,1024]{1,0:T(8,128)(2,1)S(1)}, u32[]{:S(2)}, u32[]{:S(2)}) %collective-permute-start.4) | collective-permute-done | bytes 2097184 | tf_op jit(solution)/shard_map/ppermute | solution.py:1113
  139.7 3.9 %layer_output.1 = (bf16[1024,1024]{1,0:T(8,128)(2,1)}, f32[8,128]{1,0:T(8,128)S(1)}) custom-call(bf16[1024,1024]{1,0:T(8,128)(2,1)S(1)} %get-tuple-element.141.refs_0_, bf16[1024,1024]{1,0:T(8,128)(2,1)S(1)} %collective-permute-done.4.refs_1_, f32[512,1024]{1,0:T(8,128)} %get-tuple-element.132.refs_5_.refs_2_, ...), custom_call_target="tpu_custom_call" | custom-call | flops 2300000000 | bytes 2300000000 | tf_op jit(solution)/shard_map/layer_output/pallas_call | solution.py:112
  143.6 2.7 %add_far_stage_1.1 = (bf16[2,64,2048]{2,1,0:T(8,128)(2,1)}, bf16[2,64,2048]{2,1,0:T(8,128)(2,1)}, bf16[2,64,2048]{2,1,0:T(8,128)(2,1)}, bf16[2,64,2048]{2,1,0:T(8,128)(2,1)}, f32[8,128]{1,0:T(8,128)S(1)}) custom-call(bf16[4,64,2048]{2,1,0:T(8,128)(2,1)} %get-tuple-element.185.refs_0_, bf16[4,64,2048]{2,1,0:T(8,128)(2,1)} %get-tuple-element.186.refs_1_, ...), custom_call_target="tpu_custom_call" | custom-call | flops 23000000512 | bytes 2300000000 | tf_op jit(solution)/shard_map/add_far_stage_1/pallas_call | solution.py:112
  146.3 0.5 add_stage.2
  146.8 1.0 copy-done.3
  147.8 0.5 collective-permute-start.8
  148.4 0.2 collective-permute-start.14
  148.5 13.7 %collective-permute-done.9.refs_1_ = bf16[512,1024]{1,0:T(8,128)(2,1)} collective-permute-done((bf16[512,1024]{1,0:T(8,128)(2,1)}, bf16[512,1024]{1,0:T(8,128)(2,1)}, u32[]{:S(2)}, u32[]{:S(2)}) %collective-permute-start.9) | collective-permute-done | bytes 1048608 | tf_op jit(solution)/shard_map/ppermute | solution.py:1113
  162.3 5.4 %token_grads.2 = (bf16[1024,1024]{1,0:T(8,128)(2,1)}, f32[8,128]{1,0:T(8,128)S(1)}) custom-call(bf16[512,1024]{1,0:T(8,128)(2,1)} %get-tuple-element.181.refs_0_, bf16[512,1024]{1,0:T(8,128)(2,1)} %collective-permute-done.9.refs_1_, f32[8,1024]{1,0:T(8,128)S(1)} %get-tuple-element.121.refs_2_.refs_8_.refs_6_.refs_15_.refs_5_, bf16[1024,1024]{1,0:T(8,128)(2,1)} %refs_3_.13, ...), custom_call_target="tpu_custom_call" | custom-call | flops 2300000000 | bytes 2300000000 | tf_op jit(solution)/shard_map/token_grads/pallas_call | solution.py:112
  167.7 4.1 %collective-permute-done.15.refs_3_ = bf16[2,64,2048]{2,1,0:T(8,128)(2,1)} collective-permute-done((bf16[2,64,2048]{2,1,0:T(8,128)(2,1)}, bf16[2,64,2048]{2,1,0:T(8,128)(2,1)}, u32[]{:S(2)}, u32[]{:S(2)}) %collective-permute-start.15) | collective-permute-done | bytes 524320 | tf_op jit(solution)/shard_map/ppermute | solution.py:1152
  171.8 3.3 %add_far_stage_2.1 = (bf16[1,64,2048]{2,1,0:T(8,128)(2,1)}, bf16[1,64,2048]{2,1,0:T(8,128)(2,1)}, bf16[1,64,2048]{2,1,0:T(8,128)(2,1)}, bf16[1,64,2048]{2,1,0:T(8,128)(2,1)}, f32[8,128]{1,0:T(8,128)S(1)}) custom-call(bf16[2,64,2048]{2,1,0:T(8,128)(2,1)} %get-tuple-element.195.refs_0_, bf16[2,64,2048]{2,1,0:T(8,128)(2,1)} %get-tuple-element.196.refs_1_, ...), custom_call_target="tpu_custom_call" | custom-call | flops 2300000000 | bytes 2300000000 | tf_op jit(solution)/shard_map/add_far_stage_2/pallas_call | solution.py:112
  175.0 3.4 %collective-permute-start.19 = (bf16[1,64,2048]{2,1,0:T(8,128)(2,1)}, bf16[1,64,2048]{2,1,0:T(8,128)(2,1)S(1)}, u32[]{:S(2)}, u32[]{:S(2)}) collective-permute-start(bf16[1,64,2048]{2,1,0:T(8,128)(2,1)} %get-tuple-element.208), channel_id=1, source_target_pairs={{0,16},{2,18},{4,20},{6,22},{8,24},{10,26},{12,28},{14,30},{16,0},... | collective-permute-start | bytes 786440 | tf_op jit(solution)/shard_map/ppermute | solution.py:1152
  178.5 4.5 %collective-permute-start.20 = (bf16[1,64,2048]{2,1,0:T(8,128)(2,1)}, bf16[1,64,2048]{2,1,0:T(8,128)(2,1)S(1)}, u32[]{:S(2)}, u32[]{:S(2)}) collective-permute-start(bf16[1,64,2048]{2,1,0:T(8,128)(2,1)} %get-tuple-element.210), channel_id=1, source_target_pairs={{0,4},{2,6},{4,0},{6,2},{8,12},{10,14},{12,8},{14,10},{16,20},{18,... | collective-permute-start | bytes 786440 | tf_op jit(solution)/shard_map/ppermute | solution.py:1152
  183.0 0.3 add_stage.3
  183.3 0.1 collective-permute-start.16
  183.4 0.1 collective-permute-start.17
  183.5 1.9 collective-permute-start.18
  185.5 5.3 %token_grads.3 = (bf16[1024,1024]{1,0:T(8,128)(2,1)}, f32[8,128]{1,0:T(8,128)S(1)}) custom-call(bf16[512,1024]{1,0:T(8,128)(2,1)} %get-tuple-element.179.refs_0_, bf16[512,1024]{1,0:T(8,128)(2,1)} %collective-permute-done.8.refs_1_, f32[8,1024]{1,0:T(8,128)S(1)} %get-tuple-element.121.refs_2_.refs_8_.refs_6_.refs_15_.refs_5_, ...), custom_call_target="tpu_custom_call", output_to_operand_aliasing={{0}: (5, {})} | custom-call | flops 2300000000 | bytes 2300000000 | tf_op jit(solution)/shard_map/token_grads/pallas_call | solution.py:112
  190.8 0.4 collective-permute-done.19.refs_1_
  191.2 1.2 last_far_stage.1
  192.3 1.1 copy.38
  193.5 12.8 %collective-permute-done.16.refs_1_ = bf16[1,64,2176]{2,1,0:T(8,128)(2,1)S(1)} collective-permute-done((bf16[1,64,2176]{2,1,0:T(8,128)(2,1)S(1)}, bf16[1,64,2176]{2,1,0:T(8,128)(2,1)S(1)}, u32[]{:S(2)}, u32[]{:S(2)}) %collective-permute-start.16) | collective-permute-done | bytes 278560 | tf_op jit(solution)/shard_map/ppermute | solution.py:1152
  206.3 6.0 %collective-permute-done.17.refs_2_ = bf16[1,64,2176]{2,1,0:T(8,128)(2,1)S(1)} collective-permute-done((bf16[1,64,2176]{2,1,0:T(8,128)(2,1)S(1)}, bf16[1,64,2176]{2,1,0:T(8,128)(2,1)S(1)}, u32[]{:S(2)}, u32[]{:S(2)}) %collective-permute-start.17) | collective-permute-done | bytes 278560 | tf_op jit(solution)/shard_map/ppermute | solution.py:1152
  212.3 2.2 %collective-permute-done.18.refs_3_ = bf16[1,64,2176]{2,1,0:T(8,128)(2,1)S(1)} collective-permute-done((bf16[1,64,2176]{2,1,0:T(8,128)(2,1)S(1)}, bf16[1,64,2176]{2,1,0:T(8,128)(2,1)S(1)}, u32[]{:S(2)}, u32[]{:S(2)}) %collective-permute-start.18) | collective-permute-done | bytes 278560 | tf_op jit(solution)/shard_map/ppermute | solution.py:1152
  214.5 1.0 last_stage.1
  215.5 0.1 collective-permute-start.21
  215.5 0.1 constant_dynamic-slice_fusion
  215.6 0.1 dynamic-slice_bitcast_fusion
  215.7 0.8 copy.36
  216.5 0.7 copy.37
  217.1 0.7 copy.35
  217.8 1.3 collective-permute-done.21
  219.1 0.1 constant_dynamic-slice_fusion.1
  219.2 0.5 slice_bitcast_fusion
  (29 shorter events, 0.1 us)
Async XLA Ops:
  1.7 17.6 %collective-permute-start.1 = (bf16[256,1024]{1,0:T(8,128)(2,1)S(1)}, bf16[256,1024]{1,0:T(8,128)(2,1)S(1)}, u32[]{:S(2)}, u32[]{:S(2)}) collective-permute-start(bf16[256,1024]{1,0:T(8,128)(2,1)S(1)} %constant_dynamic-slice_fusion.2), channel_id=1, source_target_pairs={{0,1},{1,0},{2,3},{3,2},{4,5},{5,4},{6,7},{7,6},{8,9},{9,8},{10,11... | collective-permute-start | bytes 1572872 | tf_op jit(solution)/shard_map/ppermute | solution.py:1113
  3.3 0.7 copy-start.1
  18.7 14.9 %collective-permute-start = (bf16[512,512]{1,0:T(8,128)(2,1)S(1)}, bf16[512,512]{1,0:T(8,128)(2,1)S(1)}, u32[]{:S(2)}, u32[]{:S(2)}) collective-permute-start(bf16[512,512]{1,0:T(8,128)(2,1)S(1)} %get-tuple-element.117.refs_0_.refs_4_), channel_id=1, source_target_pairs={{0,1},{1,0},{2,3},{3,2},{4,5},{5,4},{6,7},{7,6},{8,9},{9,8},{10,11... | collective-permute-start | bytes 1572872 | tf_op jit(solution)/shard_map/ppermute | solution.py:1113
  19.3 14.3 %copy-start = (f32[2048]{0:T(1024)S(1)}, f32[2048]{0:T(1024)}, u32[]{:S(2)}) copy-start(f32[2048]{0:T(1024)} %param.29) | copy-start | bytes 24580
  25.5 8.1 %collective-permute-start.2 = (bf16[256,1024]{1,0:T(8,128)(2,1)S(1)}, bf16[256,1024]{1,0:T(8,128)(2,1)S(1)}, u32[]{:S(2)}, u32[]{:S(2)}) collective-permute-start(bf16[256,1024]{1,0:T(8,128)(2,1)S(1)} %get-tuple-element.123.refs_3_), channel_id=1, source_target_pairs={{0,2},{2,0},{4,6},{6,4},{8,10},{10,8},{12,14},{14,12},{16,18},{18,... | collective-permute-start | bytes 1572872 | tf_op jit(solution)/shard_map/ppermute | solution.py:1119
  25.6 21.1 %collective-permute-start.3 = (bf16[512,512]{1,0:T(8,128)(2,1)S(1)}, bf16[512,512]{1,0:T(8,128)(2,1)S(1)}, u32[]{:S(2)}, u32[]{:S(2)}) collective-permute-start(bf16[512,512]{1,0:T(8,128)(2,1)S(1)} %get-tuple-element.128.refs_0_.refs_5_), channel_id=1, source_target_pairs={{0,1},{1,0},{2,3},{3,2},{4,5},{5,4},{6,7},{7,6},{8,9},{9,8},{10,11... | collective-permute-start | bytes 1572872 | tf_op jit(solution)/shard_map/ppermute | solution.py:1113
  46.1 38.2 %collective-permute-start.5 = (bf16[512,1024]{1,0:T(8,128)(2,1)S(1)}, bf16[512,1024]{1,0:T(8,128)(2,1)}, u32[]{:S(2)}, u32[]{:S(2)}) collective-permute-start(bf16[512,1024]{1,0:T(8,128)(2,1)S(1)} %get-tuple-element.142.refs_0_), channel_id=1, source_target_pairs={{0,1},{1,0},{2,3},{3,2},{4,5},{5,4},{6,7},{7,6},{8,9},{9,8},{10,11... | collective-permute-start | bytes 3145736 | tf_op jit(solution)/shard_map/ppermute | solution.py:1113
  59.7 35.2 %collective-permute-start.6 = (bf16[512,1024]{1,0:T(8,128)(2,1)}, bf16[512,1024]{1,0:T(8,128)(2,1)}, u32[]{:S(2)}, u32[]{:S(2)}) collective-permute-start(bf16[512,1024]{1,0:T(8,128)(2,1)} %get-tuple-element.152.refs_0_), channel_id=1, source_target_pairs={{0,1},{1,0},{2,3},{3,2},{4,5},{5,4},{6,7},{7,6},{8,9},{9,8},{10,11... | collective-permute-start | bytes 3145736 | tf_op jit(solution)/shard_map/ppermute | solution.py:1113
  61.2 14.4 %copy-start.2 = (s32[1,23]{1,0:T(1,128)S(1)}, s32[1,23]{1,0:T(1,128)}, u32[]{:S(2)}) copy-start(s32[1,23]{1,0:T(1,128)} %refs_4_.9) | copy-start | bytes 280
  75.5 24.3 %collective-permute-start.7 = (bf16[8,64,4096]{2,1,0:T(8,128)(2,1)}, bf16[8,64,4096]{2,1,0:T(8,128)(2,1)S(1)}, u32[]{:S(2)}, u32[]{:S(2)}) collective-permute-start(bf16[8,64,4096]{2,1,0:T(8,128)(2,1)} %get-tuple-element.158), channel_id=1, source_target_pairs={{0,2},{2,0},{4,6},{6,4},{8,10},{10,8},{12,14},{14,12},{16,18},{18,... | collective-permute-start | bytes 12582920 | tf_op jit(solution)/shard_map/ppermute | solution.py:1152
  83.7 55.9 %collective-permute-start.4 = (bf16[1024,1024]{1,0:T(8,128)(2,1)S(1)}, bf16[1024,1024]{1,0:T(8,128)(2,1)S(1)}, u32[]{:S(2)}, u32[]{:S(2)}) collective-permute-start(bf16[1024,1024]{1,0:T(8,128)(2,1)S(1)} %get-tuple-element.141.refs_0_), channel_id=1, source_target_pairs={{0,1},{1,0},{2,3},{3,2},{4,5},{5,4},{6,7},{7,6},{8,9},{9,8},{10,11... | collective-permute-start | bytes 6291464 | tf_op jit(solution)/shard_map/ppermute | solution.py:1113
  103.7 39.9 %collective-permute-start.11 = (bf16[4,64,2048]{2,1,0:T(8,128)(2,1)}, bf16[4,64,2048]{2,1,0:T(8,128)(2,1)S(1)}, u32[]{:S(2)}, u32[]{:S(2)}) collective-permute-start(bf16[4,64,2048]{2,1,0:T(8,128)(2,1)} %get-tuple-element.187), channel_id=1, source_target_pairs={{0,4},{2,6},{4,0},{6,2},{8,12},{10,14},{12,8},{14,10},{16,20},{18,... | collective-permute-start | bytes 3145736 | tf_op jit(solution)/shard_map/ppermute | solution.py:1152
  103.8 39.8 %collective-permute-start.12 = (bf16[4,64,2048]{2,1,0:T(8,128)(2,1)}, bf16[4,64,2048]{2,1,0:T(8,128)(2,1)S(1)}, u32[]{:S(2)}, u32[]{:S(2)}) collective-permute-start(bf16[4,64,2048]{2,1,0:T(8,128)(2,1)} %get-tuple-element.188), channel_id=1, source_target_pairs={{0,8},{2,10},{4,12},{6,14},{8,0},{10,2},{12,4},{14,6},{16,24},{18,... | collective-permute-start | bytes 3145736 | tf_op jit(solution)/shard_map/ppermute | solution.py:1152
  124.8 21.4 %collective-permute-start.10 = (bf16[8,64,2176]{2,1,0:T(8,128)(2,1)S(1)}, bf16[8,64,2176]{2,1,0:T(8,128)(2,1)S(1)}, u32[]{:S(2)}, u32[]{:S(2)}) collective-permute-start(bf16[8,64,2176]{2,1,0:T(8,128)(2,1)S(1)} %get-tuple-element.184), channel_id=1, source_target_pairs={{0,2},{2,0},{4,6},{6,4},{8,10},{10,8},{12,14},{14,12},{16,18},{18,... | collective-permute-start | bytes 6684680 | tf_op jit(solution)/shard_map/ppermute | solution.py:1152
  127.7 34.5 %collective-permute-start.9 = (bf16[512,1024]{1,0:T(8,128)(2,1)}, bf16[512,1024]{1,0:T(8,128)(2,1)}, u32[]{:S(2)}, u32[]{:S(2)}) collective-permute-start(bf16[512,1024]{1,0:T(8,128)(2,1)} %get-tuple-element.181.refs_0_), channel_id=1, source_target_pairs={{0,1},{1,0},{2,3},{3,2},{4,5},{5,4},{6,7},{7,6},{8,9},{9,8},{10,11... | collective-permute-start | bytes 3145736 | tf_op jit(solution)/shard_map/ppermute | solution.py:1113
  146.8 1.0 copy-start.3
  147.8 35.2 %collective-permute-start.13 = (bf16[4,64,2176]{2,1,0:T(8,128)(2,1)S(1)}, bf16[4,64,2176]{2,1,0:T(8,128)(2,1)S(1)}, u32[]{:S(2)}, u32[]{:S(2)}) collective-permute-start(bf16[4,64,2176]{2,1,0:T(8,128)(2,1)S(1)} %get-tuple-element.194), channel_id=1, source_target_pairs={{0,4},{2,6},{4,0},{6,2},{8,12},{10,14},{12,8},{14,10},{16,20},{18,... | collective-permute-start | bytes 3342344 | tf_op jit(solution)/shard_map/ppermute | solution.py:1152
  147.8 35.7 %collective-permute-start.8 = (bf16[512,1024]{1,0:T(8,128)(2,1)}, bf16[512,1024]{1,0:T(8,128)(2,1)}, u32[]{:S(2)}, u32[]{:S(2)}) collective-permute-start(bf16[512,1024]{1,0:T(8,128)(2,1)} %get-tuple-element.179.refs_0_), channel_id=1, source_target_pairs={{0,1},{1,0},{2,3},{3,2},{4,5},{5,4},{6,7},{7,6},{8,9},{9,8},{10,11... | collective-permute-start | bytes 3145736 | tf_op jit(solution)/shard_map/ppermute | solution.py:1113
  148.4 19.3 %collective-permute-start.14 = (bf16[2,64,2048]{2,1,0:T(8,128)(2,1)}, bf16[2,64,2048]{2,1,0:T(8,128)(2,1)S(1)}, u32[]{:S(2)}, u32[]{:S(2)}) collective-permute-start(bf16[2,64,2048]{2,1,0:T(8,128)(2,1)} %get-tuple-element.197), channel_id=1, source_target_pairs={{0,8},{2,10},{4,12},{6,14},{8,0},{10,2},{12,4},{14,6},{16,24},{18,... | collective-permute-start | bytes 1572872 | tf_op jit(solution)/shard_map/ppermute | solution.py:1152
  148.5 23.2 %collective-permute-start.15 = (bf16[2,64,2048]{2,1,0:T(8,128)(2,1)}, bf16[2,64,2048]{2,1,0:T(8,128)(2,1)}, u32[]{:S(2)}, u32[]{:S(2)}) collective-permute-start(bf16[2,64,2048]{2,1,0:T(8,128)(2,1)} %get-tuple-element.198), channel_id=1, source_target_pairs={{0,16},{2,18},{4,20},{6,22},{8,24},{10,26},{12,28},{14,30},{16,0},... | collective-permute-start | bytes 1572872 | tf_op jit(solution)/shard_map/ppermute | solution.py:1152
  171.8 11.3 %copy-start.4 = (bf16[4,64,2176]{2,1,0:T(8,128)(2,1)S(1)}, bf16[4,64,2176]{2,1,0:T(8,128)(2,1)}, u32[]{:S(2)}) copy-start(bf16[4,64,2176]{2,1,0:T(8,128)(2,1)} %copy-done.3) | copy-start | bytes 3342340
  175.0 16.2 %collective-permute-start.19 = (bf16[1,64,2048]{2,1,0:T(8,128)(2,1)}, bf16[1,64,2048]{2,1,0:T(8,128)(2,1)S(1)}, u32[]{:S(2)}, u32[]{:S(2)}) collective-permute-start(bf16[1,64,2048]{2,1,0:T(8,128)(2,1)} %get-tuple-element.208), channel_id=1, source_target_pairs={{0,16},{2,18},{4,20},{6,22},{8,24},{10,26},{12,28},{14,30},{16,0},... | collective-permute-start | bytes 786440 | tf_op jit(solution)/shard_map/ppermute | solution.py:1152
  178.5 12.7 %collective-permute-start.20 = (bf16[1,64,2048]{2,1,0:T(8,128)(2,1)}, bf16[1,64,2048]{2,1,0:T(8,128)(2,1)S(1)}, u32[]{:S(2)}, u32[]{:S(2)}) collective-permute-start(bf16[1,64,2048]{2,1,0:T(8,128)(2,1)} %get-tuple-element.210), channel_id=1, source_target_pairs={{0,4},{2,6},{4,0},{6,2},{8,12},{10,14},{12,8},{14,10},{16,20},{18,... | collective-permute-start | bytes 786440 | tf_op jit(solution)/shard_map/ppermute | solution.py:1152
  183.3 23.0 %collective-permute-start.16 = (bf16[1,64,2176]{2,1,0:T(8,128)(2,1)S(1)}, bf16[1,64,2176]{2,1,0:T(8,128)(2,1)S(1)}, u32[]{:S(2)}, u32[]{:S(2)}) collective-permute-start(bf16[1,64,2176]{2,1,0:T(8,128)(2,1)S(1)} %get-tuple-element.204), channel_id=1, source_target_pairs={{0,8},{2,10},{4,12},{6,14},{8,16},{10,18},{12,20},{14,22},{16,24},... | collective-permute-start | bytes 835592 | tf_op jit(solution)/shard_map/ppermute | solution.py:1152
  183.4 28.9 %collective-permute-start.17 = (bf16[1,64,2176]{2,1,0:T(8,128)(2,1)S(1)}, bf16[1,64,2176]{2,1,0:T(8,128)(2,1)S(1)}, u32[]{:S(2)}, u32[]{:S(2)}) collective-permute-start(bf16[1,64,2176]{2,1,0:T(8,128)(2,1)S(1)} %get-tuple-element.205), channel_id=1, source_target_pairs={{0,16},{2,18},{4,20},{6,22},{8,24},{10,26},{12,28},{14,30},{16,0},... | collective-permute-start | bytes 835592 | tf_op jit(solution)/shard_map/ppermute | solution.py:1152
  183.5 31.0 %collective-permute-start.18 = (bf16[1,64,2176]{2,1,0:T(8,128)(2,1)S(1)}, bf16[1,64,2176]{2,1,0:T(8,128)(2,1)S(1)}, u32[]{:S(2)}, u32[]{:S(2)}) collective-permute-start(bf16[1,64,2176]{2,1,0:T(8,128)(2,1)S(1)} %get-tuple-element.206), channel_id=1, source_target_pairs={{0,24},{2,26},{4,28},{6,30},{8,0},{10,2},{12,4},{14,6},{16,8},{18,... | collective-permute-start | bytes 835592 | tf_op jit(solution)/shard_map/ppermute | solution.py:1152
  185.5 5.7 %copy-start.5 = (bf16[1,64,2048]{2,1,0:T(8,128)(2,1)S(1)}, bf16[1,64,2048]{2,1,0:T(8,128)(2,1)}, u32[]{:S(2)}) copy-start(bf16[1,64,2048]{2,1,0:T(8,128)(2,1)} %get-tuple-element.207.refs_0_) | copy-start | bytes 786436
  185.5 5.7 %copy-start.6 = (bf16[1,64,2048]{2,1,0:T(8,128)(2,1)S(1)}, bf16[1,64,2048]{2,1,0:T(8,128)(2,1)}, u32[]{:S(2)}) copy-start(bf16[1,64,2048]{2,1,0:T(8,128)(2,1)} %get-tuple-element.209.refs_2_) | copy-start | bytes 786436
  215.5 3.7 %collective-permute-start.21 = (f32[8,64]{1,0:T(8,128)S(1)}, f32[8,64]{1,0:T(8,128)S(1)}, u32[]{:S(2)}, u32[]{:S(2)}) collective-permute-start(f32[8,64]{1,0:T(8,128)S(1)} %slice.33), channel_id=1, source_target_pairs={{0,1},{1,0},{2,3},{3,2},{4,5},{5,4},{6,7},{7,6},{8,9},{9,8},{10,11... | collective-permute-start | bytes 6152 | tf_op jit(solution)/shard_map/ppermute | solution.py:1113
